TPU v7x, 32 devices: a whole 2x2x4 slice. The times are simulated.
32 devices in a mesh: seq: 4 (over y, core), fsdp: 8 (over z, x).
Axes of the slice: x: 2, y: 2, z: 4, core: 2. Of those that a mesh axis runs over, the one named last changes fastest.
Arguments:
- inputs: bfloat16 [16384, 1024], P(('seq', 'fsdp')), may hold values from -6 to 6
- cotangent: bfloat16 [16384, 1024], P(('seq', 'fsdp')), may hold values from -6 to 6
- lengths: int32 [8, 8], replicated, may hold values from 1 to 1792, 2048 in all within a row
- mixer_weight: float32 [3, 1024, 1024], P(None, 'fsdp'), may hold values from -0.1875 to 0.1875
- strength_weight: float32 [1024, 8], P('fsdp'), may hold values from -0.1875 to 0.1875
- filter_weight: float32 [3, 4, 1024], P(None, None, 'fsdp'), may hold values from -2.5 to 2.5
- norm_gain: float32 [2, 1024], P(None, 'fsdp'), may hold values from 0.5 to 1.5
- head_gain: float32 [128], P('fsdp'), may hold values from 0.5 to 1.5
- output_weight: float32 [1024, 1024], P('fsdp'), may hold values from -0.1875 to 0.1875
- gate_up_weight: float32 [2, 1024, 2816], P(None, 'fsdp'), may hold values from -0.1875 to 0.1875
- down_weight: float32 [2816, 1024], P(None, 'fsdp'), may hold values from -0.109375 to 0.109375
- mixer_moment: float32 [3, 1024, 1024], P(None, 'fsdp'), may hold values from -64 to 64, as said below
- strength_moment: float32 [1024, 8], P('fsdp'), may hold values from -80 to 80
- filter_moment: float32 [3, 4, 1024], P(None, None, 'fsdp'), may hold values from -160 to 160
- gain_moment: float32 [2, 1024], P(None, 'fsdp'), may hold values from -384 to 384
- head_gain_moment: float32 [128], P('fsdp'), may hold values from -768 to 768
- output_moment: float32 [1024, 1024], P('fsdp'), may hold values from -1280 to 1280, as said below
- gate_up_moment: float32 [2, 1024, 2816], P(None, 'fsdp'), may hold values from -384 to 384, as said below
- down_moment: float32 [2816, 1024], P(None, 'fsdp'), may hold values from -640 to 640, as said below
Outputs:
- block_output: float32 [16384, 1024], P(('seq', 'fsdp'))
- input_grad: float32 [16384, 1024], P(('seq', 'fsdp'))
- new_mixer_moment: float32 [3, 1024, 1024], P(None, 'fsdp')
- new_mixer_weight: float32 [3, 1024, 1024], P(None, 'fsdp')
- new_strength_moment: float32 [1024, 8], P('fsdp')
- new_strength_weight: float32 [1024, 8], P('fsdp')
- new_filter_moment: float32 [3, 4, 1024], P(None, None, 'fsdp')
- new_filter_weight: float32 [3, 4, 1024], P(None, None, 'fsdp')
- new_gain_moment: float32 [2, 1024], P(None, 'fsdp')
- new_norm_gain: float32 [2, 1024], P(None, 'fsdp')
- new_head_gain_moment: float32 [128], P('fsdp')
- new_head_gain: float32 [128], P('fsdp')
- new_output_moment: float32 [1024, 1024], P('fsdp')
- new_output_weight: float32 [1024, 1024], P('fsdp')
- new_gate_up_moment: float32 [2, 1024, 2816], P(None, 'fsdp')
- new_gate_up_weight: float32 [2, 1024, 2816], P(None, 'fsdp')
- new_down_moment: float32 [2816, 1024], P(None, 'fsdp')
- new_down_weight: float32 [2816, 1024], P(None, 'fsdp')
Inputs may be any that keep to these rules, and one draw needn't show every extreme that they name: `lengths`: each row lists one stream's documents in order; a row sums to 2048, and its longest document has exactly 1792 positions. `mixer_moment`: momentum entries of the query, key and value projections. `output_moment`: momentum entries of the output projection. `gate_up_moment`: momentum entries of the gate and up projections. `down_moment`: momentum entries of the down projection.
All inputs are finite; a program needn't handle non-finite values.
Results may differ from a plain program's by a relative error of at most 0.02.
The roundings to bfloat16 on the way count: a program that leaves them out, or rounds other values in their place, can miss the bound.
Values may be sent and summed in bfloat16 or wider, within the bound.
A program may use at most 320 MiB of HBM per device.

v0:
```python
from functools import partial

import jax
import jax.numpy as jnp
from jax import lax
from jax.sharding import PartitionSpec as P

HD = 128
CONV = 4
SPAN = 64
NS_STEPS = 3


norm_eps = 1e-06
head_eps = 0.001
momentum_decay = 0.9
matrix_rate = 1.0
filter_rate = 0.01
gain_rate = 0.001
strength_rate = 0.001
coef_linear = 3.4445
coef_cubic = -4.775
coef_quintic = 2.0315


def passed_along(value, axis, by):
    size = lax.axis_size(axis)
    pairs = [(i, i + by) for i in range(size) if 0 <= i + by < size]
    return lax.ppermute(value, axis, pairs)


def rms_scale(values, gain_vector):
    return (
        values
        * lax.rsqrt(jnp.mean(values * values, axis=-1, keepdims=True) + norm_eps)
        * gain_vector
    )


def head_rms(values, gain_vector):
    return (
        values
        * lax.rsqrt(jnp.mean(values * values, axis=-1, keepdims=True) + head_eps)
        * gain_vector
    )


def unit_rows(values):
    return values * lax.rsqrt(jnp.sum(values * values, axis=-1, keepdims=True) + norm_eps)


def swish_product(gate_value, up_value):
    return jax.nn.silu(gate_value) * up_value


def token_piece(extended, filters, logits, valid_mask):
    row_count = logits.shape[0]
    filter_len = filters.shape[1]
    summed = jnp.zeros((row_count,) + extended.shape[1:], jnp.float32)
    for lag_index in range(filter_len):
        offset = filter_len - 1 - lag_index
        summed = (
            summed
            + valid_mask[lag_index][:, None, None]
            * extended[offset : offset + row_count]
            * filters[:, lag_index, :][None]
        )
    activated = jax.nn.silu(summed)
    heads_view = activated.reshape(row_count, 3, -1, HD)
    query_rows = unit_rows(heads_view[:, 0]) * HD ** (-0.5)
    key_rows = unit_rows(heads_view[:, 1])
    mixed = jnp.stack([query_rows, key_rows, heads_view[:, 2]], axis=1).reshape(row_count, 3, -1)
    return (mixed, jax.nn.sigmoid(logits))


def delta_blocks(query_rows, key_rows, value_rows, strength_rows, segment):
    total_rows, heads_here, head_width = query_rows.shape
    block_count = total_rows // SPAN
    highest = lax.Precision.HIGHEST

    def blocked(values):
        return values.reshape(block_count, SPAN, heads_here, head_width).transpose(0, 2, 1, 3)

    query_blk = blocked(query_rows)
    key_blk = blocked(key_rows)
    value_blk = blocked(value_rows)
    strength_blk = strength_rows.reshape(block_count, SPAN, heads_here).transpose(0, 2, 1)
    segment_blk = segment.reshape(block_count, SPAN)
    before = jnp.concatenate([jnp.full((1,), -1, jnp.int32), segment_blk[:-1, -1]])
    carry_in = (segment_blk == before[:, None]).astype(jnp.float32)
    tail_same = (segment_blk == segment_blk[:, -1:]).astype(jnp.float32)
    same_doc = (segment_blk[:, :, None] == segment_blk[:, None, :]).astype(jnp.float32)
    order_ids = jnp.arange(SPAN, dtype=jnp.int32)
    strict = (order_ids[:, None] > order_ids[None, :]).astype(jnp.float32)
    inclusive = (order_ids[:, None] >= order_ids[None, :]).astype(jnp.float32)
    key_key = jnp.einsum("nhtk,nhik->nhti", key_blk, key_blk, precision=highest)
    system = (
        jnp.eye(SPAN, dtype=jnp.float32)
        + strength_blk[..., :, None] * key_key * (strict * same_doc)[:, None]
    )
    right_side = jnp.concatenate(
        [
            strength_blk[..., None] * value_blk,
            (strength_blk * carry_in[:, None, :])[..., None] * key_blk,
        ],
        axis=-1,
    )
    solved = jax.scipy.linalg.solve_triangular(system, right_side, lower=True, unit_diagonal=True)
    base_update = solved[..., :head_width]
    key_weight = solved[..., head_width:]
    scores = (
        jnp.einsum("nhtk,nhik->nhti", query_blk, key_blk, precision=highest)
        * (inclusive * same_doc)[:, None]
    )

    def block_step(state_in, block_items):
        base_part, weight_part, score_part, query_part, key_part, carry_part, tail_part = (
            block_items
        )
        update = base_part - jnp.einsum("htk,hvk->htv", weight_part, state_in, precision=highest)
        output = carry_part[None, :, None] * jnp.einsum(
            "htk,hvk->htv", query_part, state_in, precision=highest
        ) + jnp.einsum("hti,hiv->htv", score_part, update, precision=highest)
        state_out = carry_part[-1] * state_in + jnp.einsum(
            "htv,htk->hvk", update * tail_part[None, :, None], key_part, precision=highest
        )
        return (state_out, output)

    initial = jnp.zeros((heads_here, head_width, head_width), jnp.float32)
    ignored, outputs = lax.scan(
        block_step,
        initial,
        (base_update, key_weight, scores, query_blk, key_blk, carry_in, tail_same),
    )
    return outputs.transpose(0, 2, 1, 3).reshape(total_rows, heads_here, head_width)


def head_piece(mixed_heads, strength_heads, gain_vector, segment):
    total_rows = mixed_heads.shape[0]
    split_view = mixed_heads.reshape(total_rows, 3, -1, HD)
    delta_out = delta_blocks(
        split_view[:, 0], split_view[:, 1], split_view[:, 2], strength_heads, segment
    )
    return head_rms(delta_out, gain_vector).reshape(total_rows, -1)


def orthogonalize(matrix):
    highest = lax.Precision.HIGHEST
    current = matrix / (jnp.sqrt(jnp.sum(matrix * matrix)) + 1e-07)
    for sweep_index in range(NS_STEPS):
        square = jnp.dot(current, current.T, precision=highest)
        mapped = coef_cubic * square + coef_quintic * jnp.dot(square, square, precision=highest)
        current = coef_linear * current + jnp.dot(mapped, current, precision=highest)
    return current


def on_device(
    inputs,
    cotangent,
    lengths,
    mixer_weight,
    strength_weight,
    filter_weight,
    norm_gain,
    head_gain,
    output_weight,
    gate_up_weight,
    down_weight,
    mixer_moment,
    strength_moment,
    filter_moment,
    gain_moment,
    head_gain_moment,
    output_moment,
    gate_up_moment,
    down_moment,
):
    low_type = jnp.bfloat16
    full_type = jnp.float32
    highest = lax.Precision.HIGHEST
    seq_count = lax.axis_size("seq")
    seq_index = lax.axis_index("seq")
    fsdp_count = lax.axis_size("fsdp")
    fsdp_index = lax.axis_index("fsdp")
    row_count = inputs.shape[0]
    group_rows = row_count * seq_count
    mixer_full, strength_full, filter_full, gain_full, head_gain_full = (
        lax.all_gather(mixer_weight.astype(low_type), "fsdp", axis=1, tiled=True),
        lax.all_gather(strength_weight.astype(low_type), "fsdp", axis=0, tiled=True),
        lax.all_gather(filter_weight.astype(low_type), "fsdp", axis=2, tiled=True),
        lax.all_gather(norm_gain.astype(low_type), "fsdp", axis=1, tiled=True),
        lax.all_gather(head_gain.astype(low_type), "fsdp", axis=0, tiled=True),
    )
    output_full, gate_up_full, down_full = (
        lax.all_gather(output_weight.astype(low_type), "fsdp", axis=0, tiled=True),
        lax.all_gather(gate_up_weight.astype(low_type), "fsdp", axis=1, tiled=True),
        lax.all_gather(down_weight.astype(low_type), "fsdp", axis=1, tiled=True),
    )
    gains_wide = gain_full.astype(full_type)
    filters_wide = filter_full.astype(full_type)
    my_lengths = lax.dynamic_slice_in_dim(lengths, fsdp_index, 1, 0)[0]
    doc_ends = jnp.cumsum(my_lengths)
    positions = jnp.arange(group_rows, dtype=jnp.int32)
    passed = (positions[:, None] >= doc_ends[None, :]).astype(jnp.int32)
    segment = jnp.sum(passed, axis=1)
    doc_first = jnp.sum(passed * my_lengths[None, :], axis=1)
    own_start = seq_index * row_count
    own_positions = lax.dynamic_slice_in_dim(positions, own_start, row_count)
    own_first = lax.dynamic_slice_in_dim(doc_first, own_start, row_count)
    valid_mask = jnp.stack(
        [(own_positions - lag_index >= own_first).astype(full_type) for lag_index in range(CONV)]
    )
    residual_in = inputs.astype(full_type)
    normed, norm_one_back = jax.vjp(rms_scale, residual_in, gains_wide[0])
    normed_low = normed.astype(low_type)
    projected_low = jnp.einsum(
        "td,jde->tje", normed_low, mixer_full, preferred_element_type=full_type
    ).astype(low_type)
    logits = jnp.dot(normed_low, strength_full, preferred_element_type=full_type)
    rim_rows = passed_along(projected_low[row_count - (CONV - 1) :], "seq", 1)
    extended = jnp.concatenate([rim_rows, projected_low], axis=0).astype(full_type)
    (mixed, strength), token_back = jax.vjp(
        partial(token_piece, valid_mask=valid_mask), extended, filters_wide, logits
    )
    mixed_heads, strength_heads = (
        lax.all_to_all(mixed.astype(low_type), "seq", split_axis=2, concat_axis=0, tiled=True),
        lax.all_to_all(
            strength.astype(low_type)[:, None, :], "seq", split_axis=2, concat_axis=0, tiled=True
        ),
    )
    head_out, head_back = jax.vjp(
        partial(head_piece, segment=segment),
        mixed_heads.astype(full_type),
        strength_heads[:, 0, :].astype(full_type),
        head_gain_full.astype(full_type),
    )
    head_normed = lax.all_to_all(
        head_out.astype(low_type), "seq", split_axis=0, concat_axis=1, tiled=True
    )
    attention = jnp.dot(head_normed, output_full, preferred_element_type=full_type)
    residual = residual_in + attention
    normed_two, norm_two_back = jax.vjp(rms_scale, residual, gains_wide[1])
    normed_two_low = normed_two.astype(low_type)
    gate_up_value = jnp.einsum(
        "td,jdf->jtf", normed_two_low, gate_up_full, preferred_element_type=full_type
    )
    hidden, swish_back = jax.vjp(swish_product, gate_up_value[0], gate_up_value[1])
    hidden_low = hidden.astype(low_type)
    block_output = residual + jnp.dot(hidden_low, down_full, preferred_element_type=full_type)
    output_back, gate_up_back, down_back = (
        lax.all_gather(output_weight.astype(low_type), "fsdp", axis=0, tiled=True),
        lax.all_gather(gate_up_weight.astype(low_type), "fsdp", axis=1, tiled=True),
        lax.all_gather(down_weight.astype(low_type), "fsdp", axis=1, tiled=True),
    )
    upstream = cotangent.astype(full_type)
    grad_down = jnp.einsum("tf,td->fd", hidden_low, cotangent, preferred_element_type=full_type)
    grad_hidden = jnp.einsum("td,fd->tf", cotangent, down_back, preferred_element_type=full_type)
    grad_gate, grad_up = swish_back(grad_hidden)
    grad_gate_up_low = jnp.stack([grad_gate, grad_up]).astype(low_type)
    grad_gate_up = jnp.einsum(
        "td,jtf->jdf", normed_two_low, grad_gate_up_low, preferred_element_type=full_type
    )
    grad_normed_two = jnp.einsum(
        "jtf,jdf->td", grad_gate_up_low, gate_up_back, preferred_element_type=full_type
    )
    grad_residual, grad_gain_two = norm_two_back(grad_normed_two)
    grad_residual = grad_residual + upstream
    grad_attention = grad_residual.astype(low_type)
    grad_output = jnp.einsum(
        "te,td->ed", head_normed, grad_attention, preferred_element_type=full_type
    )
    grad_head_normed = jnp.einsum(
        "td,ed->te", grad_attention, output_back, preferred_element_type=full_type
    ).astype(low_type)
    grad_heads = lax.all_to_all(grad_head_normed, "seq", split_axis=1, concat_axis=0, tiled=True)
    grad_mixed_heads, grad_strength_heads, grad_head_gain = head_back(grad_heads.astype(full_type))
    grad_mixed, grad_strength = (
        lax.all_to_all(
            grad_mixed_heads.astype(low_type), "seq", split_axis=0, concat_axis=2, tiled=True
        ),
        lax.all_to_all(
            grad_strength_heads.astype(low_type)[:, None, :],
            "seq",
            split_axis=0,
            concat_axis=2,
            tiled=True,
        ),
    )
    grad_extended, grad_filter, grad_logits = token_back(
        (grad_mixed.astype(full_type), grad_strength[:, 0, :].astype(full_type))
    )
    incoming = passed_along(grad_extended[: CONV - 1].astype(jnp.bfloat16), "seq", -1).astype(
        jnp.float32
    )
    grad_projected = grad_extended[CONV - 1 :].at[row_count - (CONV - 1) :].add(incoming)
    grad_projected_low = grad_projected.astype(low_type)
    grad_logits_low = grad_logits.astype(low_type)
    mixer_back, strength_back = (
        lax.all_gather(mixer_weight.astype(low_type), "fsdp", axis=1, tiled=True),
        lax.all_gather(strength_weight.astype(low_type), "fsdp", axis=0, tiled=True),
    )
    grad_mixer = jnp.einsum(
        "td,tje->jde", normed_low, grad_projected_low, preferred_element_type=full_type
    )
    grad_strength_weight = jnp.einsum(
        "td,th->dh", normed_low, grad_logits_low, preferred_element_type=full_type
    )
    grad_normed = jnp.einsum(
        "tje,jde->td", grad_projected_low, mixer_back, preferred_element_type=full_type
    ) + jnp.einsum("th,dh->td", grad_logits_low, strength_back, preferred_element_type=full_type)
    grad_input_norm, grad_gain_one = norm_one_back(grad_normed)
    input_grad = grad_residual + grad_input_norm
    partial_terms = (
        grad_mixer,
        grad_strength_weight,
        grad_filter,
        jnp.stack([grad_gain_one, grad_gain_two]),
        grad_head_gain,
        grad_output,
        grad_gate_up,
        grad_down,
    )
    shard_terms = (
        lax.psum_scatter(
            partial_terms[0].astype(jnp.bfloat16), "fsdp", scatter_dimension=1, tiled=True
        ).astype(jnp.float32),
        lax.psum_scatter(
            partial_terms[1].astype(jnp.bfloat16), "fsdp", scatter_dimension=0, tiled=True
        ).astype(jnp.float32),
        lax.psum_scatter(
            partial_terms[2].astype(jnp.bfloat16), "fsdp", scatter_dimension=2, tiled=True
        ).astype(jnp.float32),
        lax.psum_scatter(
            partial_terms[3].astype(jnp.bfloat16), "fsdp", scatter_dimension=1, tiled=True
        ).astype(jnp.float32),
        lax.psum_scatter(
            partial_terms[4].astype(jnp.bfloat16), "fsdp", scatter_dimension=0, tiled=True
        ).astype(jnp.float32),
        lax.psum_scatter(
            partial_terms[5].astype(jnp.bfloat16), "fsdp", scatter_dimension=0, tiled=True
        ).astype(jnp.float32),
        lax.psum_scatter(
            partial_terms[6].astype(jnp.bfloat16), "fsdp", scatter_dimension=1, tiled=True
        ).astype(jnp.float32),
        lax.psum_scatter(
            partial_terms[7].astype(jnp.bfloat16), "fsdp", scatter_dimension=1, tiled=True
        ).astype(jnp.float32),
    )
    total_terms = (
        lax.psum(shard_terms[0].astype(jnp.bfloat16), "seq").astype(jnp.float32),
        lax.psum(shard_terms[1].astype(jnp.bfloat16), "seq").astype(jnp.float32),
        lax.psum(shard_terms[2].astype(jnp.bfloat16), "seq").astype(jnp.float32),
        lax.psum(shard_terms[3].astype(jnp.bfloat16), "seq").astype(jnp.float32),
        lax.psum(shard_terms[4].astype(jnp.bfloat16), "seq").astype(jnp.float32),
        lax.psum(shard_terms[5].astype(jnp.bfloat16), "seq").astype(jnp.float32),
        lax.psum(shard_terms[6].astype(jnp.bfloat16), "seq").astype(jnp.float32),
        lax.psum(shard_terms[7].astype(jnp.bfloat16), "seq").astype(jnp.float32),
    )
    moments = (
        mixer_moment,
        strength_moment,
        filter_moment,
        gain_moment,
        head_gain_moment,
        output_moment,
        gate_up_moment,
        down_moment,
    )
    fresh = tuple(
        (momentum_decay * prior + gradient for prior, gradient in zip(moments, total_terms))
    )
    square_stack = jnp.concatenate([fresh[0], fresh[5][None]], axis=0)
    wide_stack = jnp.concatenate([fresh[6], fresh[7].T[None]], axis=0)
    slot_ids = jnp.arange(fsdp_count, dtype=jnp.int32)
    square_slot = jnp.arange(4, dtype=jnp.int32) * fsdp_count // 7
    wide_slot = (jnp.arange(3, dtype=jnp.int32) + 4) * fsdp_count // 7
    square_pick = (slot_ids[:, None] == square_slot[None, :]).astype(full_type)
    wide_pick = (slot_ids[:, None] == wide_slot[None, :]).astype(full_type)
    square_send = jnp.einsum("sm,mrc->src", square_pick, square_stack, precision=highest)
    wide_send = jnp.einsum("sm,mrc->src", wide_pick, wide_stack, precision=highest)
    square_whole, wide_whole = (
        lax.all_to_all(
            square_send.astype(jnp.bfloat16), "fsdp", split_axis=0, concat_axis=1, tiled=True
        ).astype(square_send.dtype),
        lax.all_to_all(
            wide_send.astype(jnp.bfloat16), "fsdp", split_axis=0, concat_axis=1, tiled=True
        ).astype(wide_send.dtype),
    )
    square_orth = lax.cond(
        jnp.any(square_slot == fsdp_index), orthogonalize, jnp.zeros_like, square_whole[0]
    )
    wide_orth = lax.cond(
        jnp.any(wide_slot == fsdp_index), orthogonalize, jnp.zeros_like, wide_whole[0]
    )
    square_parts, wide_parts = (
        lax.all_to_all(
            square_orth[None].astype(jnp.bfloat16), "fsdp", split_axis=1, concat_axis=0, tiled=True
        ).astype(jnp.float32),
        lax.all_to_all(
            wide_orth[None].astype(jnp.bfloat16), "fsdp", split_axis=1, concat_axis=0, tiled=True
        ).astype(jnp.float32),
    )
    square_update = jnp.einsum("sm,src->mrc", square_pick, square_parts, precision=highest)
    wide_update = jnp.einsum("sm,src->mrc", wide_pick, wide_parts, precision=highest)
    new_mixer = mixer_weight - matrix_rate * square_update[:3]
    new_output = output_weight - matrix_rate * square_update[3]
    new_gate_up = gate_up_weight - matrix_rate * wide_update[:2]
    new_down = down_weight - matrix_rate * wide_update[2].T
    new_strength = strength_weight - strength_rate * fresh[1]
    new_filter = filter_weight - filter_rate * fresh[2]
    new_gain = norm_gain - gain_rate * fresh[3]
    new_head = head_gain - gain_rate * fresh[4]
    return (
        block_output,
        input_grad,
        fresh[0],
        new_mixer,
        fresh[1],
        new_strength,
        fresh[2],
        new_filter,
        fresh[3],
        new_gain,
        fresh[4],
        new_head,
        fresh[5],
        new_output,
        fresh[6],
        new_gate_up,
        fresh[7],
        new_down,
    )


def solution(mesh):
    return jax.shard_map(
        on_device,
        mesh=mesh,
        in_specs=(
            P(("seq", "fsdp"), None),
            P(("seq", "fsdp"), None),
            P(),
            P(None, "fsdp", None),
            P("fsdp", None),
            P(None, None, "fsdp"),
            P(None, "fsdp"),
            P("fsdp"),
            P("fsdp", None),
            P(None, "fsdp", None),
            P(None, "fsdp"),
            P(None, "fsdp", None),
            P("fsdp", None),
            P(None, None, "fsdp"),
            P(None, "fsdp"),
            P("fsdp"),
            P("fsdp", None),
            P(None, "fsdp", None),
            P(None, "fsdp"),
        ),
        out_specs=(
            P(("seq", "fsdp"), None),
            P(("seq", "fsdp"), None),
            P(None, "fsdp", None),
            P(None, "fsdp", None),
            P("fsdp", None),
            P("fsdp", None),
            P(None, None, "fsdp"),
            P(None, None, "fsdp"),
            P(None, "fsdp"),
            P(None, "fsdp"),
            P("fsdp"),
            P("fsdp"),
            P("fsdp", None),
            P("fsdp", None),
            P(None, "fsdp", None),
            P(None, "fsdp", None),
            P(None, "fsdp"),
            P(None, "fsdp"),
        ),
        check_vma=False,
    )
```

profile of v0, /device:TPU:31, one launch (start us, length us, event | category | flops | bytes accessed | tf_op | source)
XLA Modules:
  0.0 3123.6 jit_solution(15709582426172029086)
XLA Ops:
  24.7 22.9 all_gather.30
  81.6 27.2 all-gather.5.cloned.1.call-done
  173.8 24.2 all-to-all-done.1
  226.7 134.0 %custom-call.10 = f32[32,2,1,64,64]{0,3,4,2,1:T(8,128)} custom-call(f32[32,2,1,64,64]{0,4,3,2,1:T(8,128)} %add_bitcast_fusion), custom_call_target="InvertDiagBlocksLowerTriangular" | custom-call | tf_op jit(solution)/shard_map/jvp(jit(_solve_triangular))/vmap(vmap())/triangular_solve | solution.py:108
  386.0 297.3 %while.51 = (s32[]{:T(128)}, f32[2,128,128]{2,1,0:T(8,128)S(1)}, f32[32,2,64,128]{3,1,2,0:T(2,128)}, f32[32,2,128,128]{3,2,1,0:T(8,128)}, f32[32,1,64,1]{2,3,1,0...) while((s32[]{:T(128)}, f32[2,128,128]{2,1,0:T(8,128)S(1)}, ...), condition=%wide.region_7.8_spmd.clone, body=%wide.region_6.7_spmd.clone.sunk | while | flops 88358912 | bytes 1774949 | solution.py:130
  707.8 17.8 all_to_all.115
  827.7 488.9 %while.52 = (s32[]{:T(128)}, f32[2,128,128]{2,1,0:T(8,128)S(1)}, f32[32,2,64,128]{3,2,1,0:T(8,128)}, f32[32,2,64,128]{3,2,1,0:T(8,128)}, f32[32,2,64,64]{3,2,1,0...) while((s32[]{:T(128)}, f32[2,128,128]{2,1,0:T(8,128)S(1)}, ...), condition=%wide.region_13.14_spmd.clone, body=%wide.region_12.13_spmd.clone.sunk | while | flops 176455680 | bytes 2498556 | solution.py:130
  1377.7 51.9 %all_to_all.116 = bf16[2048,3,256]{2,1,0:T(4,128)(2,1)S(1)} all-to-all(bf16[2048,3,256]{2,1,0:T(4,128)(2,1)} %copy.513), channel_id=1, replica_groups=mesh['seq'=4,'fsdp'=8] {'seq'}, dimensions={0} | all-to-all | bytes 6291456 | tf_op jit(solution)/shard_map/all_to_all | solution.py:278
  1458.5 16.1 multiply_reduce_fusion.3
  1539.5 29.0 copy.576
  1600.8 42.8 %reduce-scatter.22.cloned.1.call-done = bf16[128,3072]{1,0:T(8,128)(2,1)} async-done(((bf16[1024,3072]{1,0:T(8,128)(2,1)}), bf16[128,3072]{1,0:T(8,128)(2,1)}) %reduce-scatter.22.cloned.1.call-update) | async-done | bytes 786448
  1647.2 191.6 %reduce-scatter.32.cloned.1.call-done = bf16[128,5632]{1,0:T(8,128)(2,1)} async-done(((bf16[1024,5632]{1,0:T(8,128)(2,1)}), bf16[128,5632]{1,0:T(8,128)(2,1)}) %reduce-scatter.32.cloned.1.call-update) | async-done | bytes 1441808
  1843.1 65.1 %reduce-scatter.24.cloned.1.call-done = bf16[128,1024]{1,0:T(8,128)(2,1)} async-done(((bf16[1024,1024]{1,0:T(8,128)(2,1)}), bf16[128,1024]{1,0:T(8,128)(2,1)}) %reduce-scatter.24.cloned.1.call-update) | async-done | bytes 262160 | tf_op jit(solution)/shard_map/reduce_scatter | solution.py:339
  1908.3 114.8 %reduce-scatter.34.cloned.1.call-done = bf16[128,2816]{1,0:T(8,128)(2,1)} async-done(((bf16[1024,2816]{1,0:T(8,128)(2,1)}), bf16[128,2816]{1,0:T(8,128)(2,1)}) %reduce-scatter.34.cloned.1.call-update) | async-done | bytes 720912
  2029.8 70.8 %all-reduce.22.cloned.1.call-done = (bf16[3,128,1024]{2,0,1:T(4,128)(2,1)}, bf16[128,1024]{1,0:T(8,128)(2,1)}, bf16[2,128,2816]{2,0,1:T(2,128)(2,1)}, bf16[2816,128]{0,1:T(8,128)(2,1)}) async-done(((bf16[3,128,1024]{2,0,1:T(4,128)(2,1)}, bf16[128,1024]{1,0:T(8,128)(2,1)}, bf16[2,128,2816]{2,0,1:T(2,128)(2,1)}, bf16[2816,128]{0,1:T(8,128)(2,1)}), (bf16[3,128,1024]{2,0,1:T(4,128)(2,1)}, ...) | async-done | bytes 3211280 | tf_op jit(solution)/shard_map/psum | solution.py:350
  2141.2 24.4 all-to-all-done.6
  2201.3 95.1 %all-to-all-done.8 = bf16[8,128,2816]{2,1,0:T(8,128)(2,1)} async-done(((bf16[8,128,2816]{2,1,0:T(8,128)(2,1)}), bf16[8,128,2816]{2,1,0:T(8,128)(2,1)}, u32[]{:S(2)}, u32[]{:S(2)}) %all-to-all-start.8) | async-done | bytes 5767200 | tf_op jit(solution)/shard_map/all_to_all | solution.py:385
  2296.4 34.1 %all-to-all-start.7 = ((bf16[8,2,65536]{2,1,0:T(2,128)(2,1)}), bf16[8,2,65536]{2,1,0:T(2,128)(2,1)}, u32[]{:S(2)}, u32[]{:S(2)}) async-start(bf16[8,2,65536]{2,1,0:T(2,128)(2,1)} %reshape.514), calls=%async_computation.7 | async-start | bytes 4194304 | tf_op jit(solution)/shard_map/all_to_all | solution.py:396
  2354.6 59.3 %reduce.18 = bf16[1024,2816]{1,0:T(8,128)(2,1)} reduce(bf16[1024,1,2816]{2,1,0:T(2,128)(2,1)} %bitcast.458, bf16[]{:T(256)} %broadcast.684), dimensions={1}, to_apply=%bitcast.383.reduce_sub_computation | reduce | bytes 11534338
  2421.8 299.6 %all-to-all-start.9 = ((bf16[8,2,180224]{2,1,0:T(2,128)(2,1)}), bf16[8,2,180224]{2,1,0:T(2,128)(2,1)}, u32[]{:S(2)}, u32[]{:S(2)}) async-start(bf16[8,2,180224]{2,1,0:T(2,128)(2,1)} %reshape.516), calls=%async_computation.9 | async-start | bytes 11534336 | tf_op jit(solution)/shard_map/all_to_all | solution.py:399
  2731.8 120.4 %all-reduce.17 = bf16[128]{0:T(256)(128)(2,1)S(1)} all-reduce(bf16[128]{0:T(256)(128)(2,1)S(1)} %copy-done.114), channel_id=7, replica_groups=mesh['seq'=4,'fsdp'=8] {'fsdp'}, use_global_device_ids=true, to_apply=%region_41.42.clone | all-reduce | flops 128 | bytes 512
  2856.1 61.1 %reduce-scatter.26.cloned.1.call-done = bf16[128,8]{1,0:T(8,128)(2,1)} async-done(((bf16[1024,8]{1,0:T(8,128)(2,1)}), bf16[128,8]{1,0:T(8,128)(2,1)}) %reduce-scatter.26.cloned.1.call-update) | async-done | bytes 2064
  2935.8 52.5 %reduce-scatter.30.cloned.1.call-done = bf16[128,2]{1,0:T(8,128)(2,1)} async-done(((bf16[1024,2]{1,0:T(8,128)(2,1)}), bf16[128,2]{1,0:T(8,128)(2,1)}) %reduce-scatter.30.cloned.1.call-update) | async-done | bytes 528
  2989.1 63.6 %reduce-scatter.28.cloned.1.call-done = bf16[128,12]{1,0:T(8,128)(2,1)} async-done(((bf16[1024,12]{1,0:T(8,128)(2,1)}), bf16[128,12]{1,0:T(8,128)(2,1)}) %reduce-scatter.28.cloned.1.call-update) | async-done | bytes 3088
  (1192 shorter events, 1486.8 us)
Async XLA Ops:
  7.2 101.7 %all-gather.5.cloned.1.call-start = ((), (), s32[]{:S(2)}) async-start(), calls=%async_computation.17 | async-start | bytes 7077888 | tf_op jit(solution)/shard_map/all_gather | solution.py:188
  9.8 718.0 %all-gather.7.cloned.1.call-start = ((), (), s32[]{:S(2)}) async-start(), calls=%async_computation.18 | async-start | bytes 2359296 | tf_op jit(solution)/shard_map/all_gather | solution.py:195
  10.7 722.0 %all-gather.9.cloned.1.call-start = ((), (), s32[]{:S(2)}) async-start(), calls=%async_computation.19 | async-start | bytes 12976128 | tf_op jit(solution)/shard_map/all_gather | solution.py:196
  53.3 92.0 %all-to-all-start = ((bf16[4,2,512]{2,1,0:T(2,128)(2,1)}), bf16[4,2,512]{2,1,0:T(2,128)(2,1)S(1)}, u32[]{:S(2)}, u32[]{:S(2)}) async-start(bf16[4,2,512]{2,1,0:T(2,128)(2,1)} %reshape.510), calls=%async_computation | async-start | bytes 16384 | tf_op jit(solution)/shard_map/all_to_all | solution.py:227
  115.5 3.1 collective-permute-start
  145.3 52.6 %all-to-all-start.1 = ((bf16[512,3,1024]{0,1,2:T(4,128)(2,1)}), bf16[512,3,1024]{0,1,2:T(4,128)(2,1)}, u32[]{:S(2)}, u32[]{:S(2)}) async-start(bf16[512,3,1024]{0,1,2:T(4,128)(2,1)} %copy.472), calls=%async_computation.1 | async-start | bytes 8388608 | tf_op jit(solution)/shard_map/all_to_all | solution.py:226
  151.2 593.7 %all-gather.11.cloned.1.call-start = ((), (), s32[]{:S(2)}) async-start(), calls=%async_computation.20 | async-start | bytes 6488064 | tf_op jit(solution)/shard_map/all_gather | solution.py:197
  775.6 19.2 all-to-all-start.3
  782.2 861.4 %reduce-scatter.22.cloned.1.call-start = ((), (), s32[]{:S(2)}) async-start(), calls=%async_computation.21 | async-start | bytes 7077888
  1486.8 5.7 collective-permute-start.1
  1526.0 312.8 %reduce-scatter.32.cloned.1.call-start = ((), (), s32[]{:S(2)}) async-start(), calls=%async_computation.26 | async-start | bytes 12976128
  1580.0 328.3 %reduce-scatter.24.cloned.1.call-start = ((), (), s32[]{:S(2)}) async-start(), calls=%async_computation.22 | async-start | bytes 2359296 | tf_op jit(solution)/shard_map/reduce_scatter | solution.py:339
  1584.5 438.6 %reduce-scatter.34.cloned.1.call-start = ((), (), s32[]{:S(2)}) async-start(), calls=%async_computation.27 | async-start | bytes 6488064
  1600.7 499.9 %all-reduce.22.cloned.1.call-start = ((), (), s32[]{:S(2)}) async-start(), calls=%async_computation.28 | async-start | bytes 6946816 | tf_op jit(solution)/shard_map/psum | solution.py:350
  1647.2 376.1 %copy-start.55 = (f32[32,64]{1,0:T(8,128)S(1)}, f32[32,64]{1,0:T(8,128)}, u32[]{:S(2)}) copy-start(f32[32,64]{1,0:T(8,128)} %copy-done.54) | copy-start | bytes 24580
  2025.7 86.8 %all-to-all-start.5 = ((bf16[4,2,512]{2,1,0:T(2,128)(2,1)}), bf16[4,2,512]{2,1,0:T(2,128)(2,1)S(1)}, u32[]{:S(2)}, u32[]{:S(2)}) async-start(bf16[4,2,512]{2,1,0:T(2,128)(2,1)} %reshape.512), calls=%async_computation.5 | async-start | bytes 16384 | tf_op jit(solution)/shard_map/all_to_all | solution.py:281
  2113.2 52.5 %all-to-all-start.6 = ((bf16[8,128,1024]{2,1,0:T(8,128)(2,1)}), bf16[8,128,1024]{2,1,0:T(8,128)(2,1)S(1)}, u32[]{:S(2)}, u32[]{:S(2)}) async-start(bf16[8,128,1024]{2,1,0:T(8,128)(2,1)} %copy.528), calls=%async_computation.6 | async-start | bytes 4194304 | tf_op jit(solution)/shard_map/all_to_all | solution.py:382
  2165.6 130.8 %all-to-all-start.8 = ((bf16[8,128,2816]{2,1,0:T(8,128)(2,1)}), bf16[8,128,2816]{2,1,0:T(8,128)(2,1)}, u32[]{:S(2)}, u32[]{:S(2)}) async-start(bf16[8,128,2816]{2,1,0:T(8,128)(2,1)} %copy.539), calls=%async_computation.8 | async-start | bytes 11534336 | tf_op jit(solution)/shard_map/all_to_all | solution.py:385
  2296.4 125.4 %all-to-all-start.7 = ((bf16[8,2,65536]{2,1,0:T(2,128)(2,1)}), bf16[8,2,65536]{2,1,0:T(2,128)(2,1)}, u32[]{:S(2)}, u32[]{:S(2)}) async-start(bf16[8,2,65536]{2,1,0:T(2,128)(2,1)} %reshape.514), calls=%async_computation.7 | async-start | bytes 4194304 | tf_op jit(solution)/shard_map/all_to_all | solution.py:396
  2421.8 301.8 %copy-start.18 = (f32[512,1024]{1,0:T(8,128)S(1)}, f32[512,1024]{1,0:T(8,128)}, u32[]{:S(2)}) copy-start(f32[512,1024]{1,0:T(8,128)} %get-tuple-element.1110) | copy-start | bytes 6291460
  2421.8 666.7 %all-to-all-start.9 = ((bf16[8,2,180224]{2,1,0:T(2,128)(2,1)}), bf16[8,2,180224]{2,1,0:T(2,128)(2,1)}, u32[]{:S(2)}, u32[]{:S(2)}) async-start(bf16[8,2,180224]{2,1,0:T(2,128)(2,1)} %reshape.516), calls=%async_computation.9 | async-start | bytes 11534336 | tf_op jit(solution)/shard_map/all_to_all | solution.py:399
  2721.5 195.7 %reduce-scatter.26.cloned.1.call-start = ((), (), s32[]{:S(2)}) async-start(), calls=%async_computation.23 | async-start | bytes 294912
  2855.6 132.7 %reduce-scatter.30.cloned.1.call-start = ((), (), s32[]{:S(2)}) async-start(), calls=%async_computation.25 | async-start | bytes 294912
  2927.9 124.9 %reduce-scatter.28.cloned.1.call-start = ((), (), s32[]{:S(2)}) async-start(), calls=%async_computation.24 | async-start | bytes 294912
  (115 other events, 3843.8 us)
Sparse Core Ops, SparseCore 0:
  10.8 98.0 all-gather.4
  111.6 47.6 all-gather.6
  162.1 162.0 all-gather.8
  326.0 91.7 all-gather.10
  1526.1 117.3 reduce-scatter.21
  1647.0 191.7 reduce-scatter.31
  1842.9 65.3 reduce-scatter.23
  1911.9 111.1 reduce-scatter.33
  2026.3 74.2 all-reduce.21
  2855.7 61.4 reduce-scatter.25
  2928.0 60.2 reduce-scatter.29
  2992.4 60.2 reduce-scatter.27
where the time goes:
time: 3150 us; the launch traced here: 3120 us
  waiting for transfers between devices  844 us (27%)
  matrix products  767 us (24%)
  local copies, waits for them, and re-layouts  473 us (15%)
  starting transfers between devices  378 us (12%)
  other arithmetic  361 us (11%)
  blocking collectives  264 us (8%)
    unnamed x18, waiting for transfers between devices  527 us
    all_to_all x1, starting transfers between devices, on_device(): lax.all_to_all(wide_orth[None].astype(jnp.bfloat16), 'fsdp', split_axis=1...  300 us
    unnamed x278, local copies, waits for them, and re-layouts  170 us
    dot_general x96, matrix products, block_step(): jnp.einsum('htk,hvk->htv', query_part, state_in, precision=highest)  159 us
    dot_general x96, matrix products, block_step(): jnp.einsum('htk,hvk->htv', weight_part, state_in, precision=highest)  157 us
    dot_general x96, matrix products, block_step(): jnp.einsum('htv,htk->hvk', update * tail_part[None, :, None], key_part, p...  155 us
    dot_general x96, matrix products, block_step(): jnp.einsum('hti,hiv->htv', score_part, update, precision=highest)  144 us
    another operation x5, other arithmetic, delta_blocks(): jax.scipy.linalg.solve_triangular(system, right_side, lower=True, unit_di...  140 us
  transfers between devices with their start and end apart: 22, of which 14 were waited for; matrix products, arithmetic and copies ran while one was open for 27% of the time, Pallas kernels for 0%

commit v1 on v0

v1 whole, which is shorter than its diff:
```python
from functools import partial

import jax
import jax.numpy as jnp
from jax import lax
from jax.experimental import pallas as pl
from jax.experimental.pallas import tpu as pltpu
from jax.sharding import PartitionSpec as P

HD = 128
CONV = 4
BLOCK = 128
GROUP = 8
RIM = 16
NS_STEPS = 3

norm_eps = 1e-06
head_eps = 0.001
momentum_decay = 0.9
matrix_rate = 1.0
filter_rate = 0.01
gain_rate = 0.001
strength_rate = 0.001
coef_linear = 3.4445
coef_cubic = -4.775
coef_quintic = 2.0315

LOW = jnp.bfloat16
FULL = jnp.float32


def halves(values):
    top = values.astype(LOW)
    return (top, (values - top.astype(FULL)).astype(LOW))


def product(left, right, dims=(1, 0)):
    left = left if isinstance(left, tuple) else (left,)
    right = right if isinstance(right, tuple) else (right,)
    total = None
    for i, a in enumerate(left):
        for j, b in enumerate(right):
            if i + j < 2:
                term = lax.dot_general(
                    a, b, (((dims[0],), (dims[1],)), ((), ())), preferred_element_type=FULL
                )
                total = term if total is None else total + term
    return total


def low_product(left, right, dims=(1, 0)):
    return product(left.astype(LOW), right.astype(LOW), dims)


def lanes(values, head):
    return values[:, head * HD : (head + 1) * HD]


def unit_scale(values):
    return lax.rsqrt(jnp.sum(values * values, axis=-1, keepdims=True) + norm_eps)


def block_ids():
    rows = lax.broadcasted_iota(jnp.int32, (BLOCK, BLOCK), 0)
    cols = lax.broadcasted_iota(jnp.int32, (BLOCK, BLOCK), 1)
    return rows, cols


def short_conv(current, previous, taps, meta):
    joined = jnp.concatenate([previous, current], axis=0)
    total = None
    shifted = []
    for lag in range(CONV):
        moved = joined if lag == 0 else pltpu.roll(joined, lag, 0)
        moved = moved[RIM:] * meta[:, lag : lag + 1]
        shifted.append(moved)
        term = moved * taps[lag : lag + 1, :]
        total = term if total is None else total + term
    return total, shifted


def inverse(system, differ):
    rows, cols = block_ids()
    eye = jnp.where(rows == cols, 1.0, 0.0).astype(FULL)
    found = [eye - jnp.where((differ >> 0) == 1, one, 0.0) for one in system]
    level = 1
    while (1 << level) < BLOCK:
        picked = [jnp.where((differ >> level) == 1, one, 0.0).astype(LOW) for one in system]
        low = [one.astype(LOW) for one in found]
        inner = [product(a, b).astype(LOW) for a, b in zip(picked, low)]
        outer = [product(b, a) for a, b in zip(inner, low)]
        found = [a - b for a, b in zip(found, outer)]
        level += 1
    split = [halves(one) for one in found]
    wide = [halves(one) for one in system]
    error = [eye - a - product(b, c) for a, b, c in zip(found, wide, split)]
    return [a + product(b[0], c.astype(LOW)) for a, b, c in zip(found, split, error)]


def forward_kernel(
    proj_ref, prev_ref, rim_ref, taps_ref, strength_ref, strength_row_ref, meta_ref, meta_row_ref,
    mixed_ref, solve_ref, weight_ref, update_ref, drift_ref, out_ref, query_ref, state_ref, end_ref, transfer_ref,
    carry_ref,
):
    step = pl.program_id(1)
    rows, cols = block_ids()
    meta = meta_ref[...]
    carry, tail, segment = meta[:, 4:5], meta[:, 5:6], meta[:, 6:7]
    same = segment == meta_row_ref[0:1, :]
    strict = (rows > cols) & same
    inclusive = (rows >= cols) & same
    differ = rows ^ cols
    carry_last = carry[BLOCK - 1 : BLOCK, :]

    @pl.when(step == 0)
    def _():
        start = jnp.concatenate(
            [jnp.zeros((HD, HD), FULL), jnp.where(rows == cols, 1.0, 0.0).astype(FULL)], axis=1
        )
        for head in range(GROUP):
            carry_ref[head] = start

    first = step == 0
    parts = []
    for j in range(3):
        at = slice(j * GROUP * HD, (j + 1) * GROUP * HD)
        previous = jnp.where(first, rim_ref[:, at].astype(FULL), prev_ref[:, at].astype(FULL))
        conv, _ = short_conv(proj_ref[:, at].astype(FULL), previous, taps_ref[j], meta)
        parts.append(conv * jax.nn.sigmoid(conv))
    queries, keys, values = [], [], []
    for head in range(GROUP):
        query, key = lanes(parts[0], head), lanes(parts[1], head)
        queries.append((query * (unit_scale(query) * HD ** (-0.5))).astype(LOW))
        keys.append((key * unit_scale(key)).astype(LOW))
        values.append(lanes(parts[2], head).astype(LOW))
        mixed_ref[0, :, head * HD : (head + 1) * HD] = queries[head]
        mixed_ref[1, :, head * HD : (head + 1) * HD] = keys[head]
        mixed_ref[2, :, head * HD : (head + 1) * HD] = values[head]
    strength = strength_ref[0]
    strength_row = strength_row_ref[0]
    heads = range(GROUP)
    gram = [product(keys[h], keys[h], (1, 1)) for h in heads]
    system = [jnp.where(strict, strength[:, h : h + 1] * gram[h], 0.0) for h in heads]
    scores = [jnp.where(inclusive, product(queries[h], keys[h], (1, 1)), 0.0) for h in heads]
    solve = inverse(system, differ)
    carry_low, tail_low = carry.astype(LOW), tail.astype(LOW)
    carried_query = [queries[h] * carry_low for h in heads]
    tail_key = [keys[h] * tail_low for h in heads]
    right = [jnp.concatenate([values[h], keys[h] * carry_low], axis=1) for h in heads]
    solved = [product(halves(solve[h] * strength_row[h : h + 1, :]), right[h]) for h in heads]
    state = [carry_ref[h] for h in heads]
    state_parts = [halves(state[h]) for h in heads]
    passed = [product(halves(solved[h][:, HD:]), state_parts[h]) for h in heads]
    zero = jnp.zeros((BLOCK, HD), FULL)
    both = [
        jnp.concatenate([solved[h][:, :HD], zero], axis=1) - passed[h] for h in heads
    ]
    both_parts = [halves(both[h]) for h in heads]
    result = [
        product(carried_query[h], state_parts[h]) + product(halves(scores[h]), both_parts[h])
        for h in heads
    ]
    after = [
        carry_last * state[h] + product(tail_key[h], both_parts[h], (0, 0)) for h in heads
    ]
    for h in heads:
        solve_ref[0, h] = solve[h].astype(LOW)
        at = slice(h * HD, (h + 1) * HD)
        weight_ref[:, at] = solved[h][:, HD:].astype(LOW)
        update_ref[:, at] = both[h][:, :HD]
        drift_ref[:, at] = both[h][:, HD:].astype(LOW)
        out_ref[:, at] = result[h][:, :HD]
        query_ref[:, at] = result[h][:, HD:]
        state_ref[0, h] = state[h]
        carry_ref[h] = after[h]
        end_ref[h] = after[h][:, :HD]
        transfer_ref[h] = after[h][:, HD:]


def forward_blocks(projected, rim, taps, strength, meta, meta_row):
    total = projected.shape[0]
    width = projected.shape[1] // 3
    head_count = width // HD
    groups, steps = head_count // GROUP, total // BLOCK
    span = GROUP * HD
    grouped = strength.reshape(total, groups, GROUP)
    strength_col = grouped.transpose(1, 0, 2)
    strength_row = grouped.transpose(1, 2, 0)
    rows_of = lambda g, n: (n, g)
    shapes = (
        jax.ShapeDtypeStruct((3, total, width), LOW),
        jax.ShapeDtypeStruct((steps, head_count, BLOCK, BLOCK), LOW),
        jax.ShapeDtypeStruct((total, width), LOW),
        jax.ShapeDtypeStruct((total, width), FULL),
        jax.ShapeDtypeStruct((total, width), LOW),
        jax.ShapeDtypeStruct((total, width), FULL),
        jax.ShapeDtypeStruct((total, width), FULL),
        jax.ShapeDtypeStruct((steps, head_count, HD, 2 * HD), FULL),
        jax.ShapeDtypeStruct((head_count, HD, HD), FULL),
        jax.ShapeDtypeStruct((head_count, HD, HD), FULL),
    )
    wide = pl.BlockSpec((BLOCK, span), rows_of)
    ratio = BLOCK // RIM
    return pl.pallas_call(
        forward_kernel,
        grid=(groups, steps),
        in_specs=[
            pl.BlockSpec((BLOCK, 3 * span), rows_of),
            pl.BlockSpec((RIM, 3 * span), lambda g, n: (jnp.maximum(n * ratio - 1, 0), g)),
            pl.BlockSpec((RIM, 3 * span), lambda g, n: (0, g)),
            pl.BlockSpec((3, CONV, span), lambda g, n: (0, 0, g)),
            pl.BlockSpec((1, BLOCK, GROUP), lambda g, n: (g, n, 0)),
            pl.BlockSpec((1, GROUP, BLOCK), lambda g, n: (g, 0, n)),
            pl.BlockSpec((BLOCK, 8), lambda g, n: (n, 0)),
            pl.BlockSpec((8, BLOCK), lambda g, n: (0, n)),
        ],
        out_specs=(
            pl.BlockSpec((3, BLOCK, span), lambda g, n: (0, n, g)),
            pl.BlockSpec((1, GROUP, BLOCK, BLOCK), lambda g, n: (n, g, 0, 0)),
            wide,
            wide,
            wide,
            wide,
            wide,
            pl.BlockSpec((1, GROUP, HD, 2 * HD), lambda g, n: (n, g, 0, 0)),
            pl.BlockSpec((GROUP, HD, HD), lambda g, n: (g, 0, 0)),
            pl.BlockSpec((GROUP, HD, HD), lambda g, n: (g, 0, 0)),
        ),
        out_shape=shapes,
        scratch_shapes=[pltpu.VMEM((GROUP, HD, 2 * HD), FULL)],
        compiler_params=pltpu.CompilerParams(vmem_limit_bytes=48 << 20),
        cost_estimate=pl.CostEstimate(flops=8 << 30, bytes_accessed=24 << 20, transcendentals=0),
    )(projected, projected, rim, taps, strength_col, strength_row, meta, meta_row)


def out_kernel(local_ref, query_ref, state_ref, gain_ref, delta_ref, normed_ref):
    gain = gain_ref[0:1, :]
    for head in range(local_ref.shape[1] // HD):
        at = slice(head * HD, (head + 1) * HD)
        value = local_ref[:, at] + product(halves(query_ref[:, at]), halves(state_ref[head]))
        delta_ref[:, at] = value
        scale = lax.rsqrt(jnp.mean(value * value, axis=-1, keepdims=True) + head_eps)
        normed_ref[:, at] = (value * scale * gain).astype(LOW)


def head_outputs(local_out, effective, state_in, gain):
    total, width = local_out.shape
    rows = pl.BlockSpec((BLOCK, width), lambda n: (n, 0))
    return pl.pallas_call(
        out_kernel,
        grid=(total // BLOCK,),
        in_specs=[
            rows,
            rows,
            pl.BlockSpec(state_in.shape, lambda n: (0, 0, 0)),
            pl.BlockSpec((1, HD), lambda n: (0, 0)),
        ],
        out_specs=(rows, rows),
        out_shape=(
            jax.ShapeDtypeStruct((total, width), FULL),
            jax.ShapeDtypeStruct((total, width), LOW),
        ),
        compiler_params=pltpu.CompilerParams(vmem_limit_bytes=32 << 20),
    )(local_out, effective, state_in, gain)


def head_back_kernel(grad_ref, delta_ref, query_ref, gain_ref, upstream_ref, adjoint_ref, gain_grad_ref):
    step = pl.program_id(0)
    gain = gain_ref[0:1, :]

    @pl.when(step == 0)
    def _():
        adjoint_ref[...] = jnp.zeros_like(adjoint_ref)
        gain_grad_ref[...] = jnp.zeros_like(gain_grad_ref)

    gained = jnp.zeros((1, HD), FULL)
    for head in range(grad_ref.shape[1] // HD):
        at = slice(head * HD, (head + 1) * HD)
        value = delta_ref[:, at]
        grad = grad_ref[:, at].astype(FULL)
        scale = lax.rsqrt(jnp.mean(value * value, axis=-1, keepdims=True) + head_eps)
        unit = value * scale
        gained = gained + jnp.sum(grad * unit, axis=0, keepdims=True)
        grad = grad * gain
        back = scale * (grad - unit * jnp.mean(grad * unit, axis=-1, keepdims=True))
        low = back.astype(LOW)
        upstream_ref[:, at] = low
        adjoint_ref[head] += product(query_ref[:, at].astype(LOW), low, (0, 0))
    gain_grad_ref[...] += gained


def head_back(grad_normed, delta_out, effective, gain):
    total, width = delta_out.shape
    head_count = width // HD
    rows = pl.BlockSpec((BLOCK, width), lambda n: (n, 0))
    return pl.pallas_call(
        head_back_kernel,
        grid=(total // BLOCK,),
        in_specs=[rows, rows, rows, pl.BlockSpec((1, HD), lambda n: (0, 0))],
        out_specs=(
            rows,
            pl.BlockSpec((head_count, HD, HD), lambda n: (0, 0, 0)),
            pl.BlockSpec((1, HD), lambda n: (0, 0)),
        ),
        out_shape=(
            jax.ShapeDtypeStruct((total, width), LOW),
            jax.ShapeDtypeStruct((head_count, HD, HD), FULL),
            jax.ShapeDtypeStruct((1, HD), FULL),
        ),
        compiler_params=pltpu.CompilerParams(vmem_limit_bytes=32 << 20),
    )(grad_normed, delta_out, effective, gain)


def backward_kernel(
    proj_ref, prev_ref, rim_ref, taps_ref, strength_ref, meta_ref, meta_row_ref,
    mixed_ref, solve_ref, weight_ref, update_ref, drift_ref, upstream_ref, state_ref, enter_ref, leave_ref,
    grad_ref, strength_grad_ref, taps_grad_ref, edge_ref, lead_ref,
    adjoint_ref, spill_ref,
):
    turn = pl.program_id(1)
    last_turn = pl.num_programs(1) - 1
    rows, cols = block_ids()
    meta = meta_ref[...]
    carry, tail, segment = meta[:, 4:5], meta[:, 5:6], meta[:, 6:7]
    same = segment == meta_row_ref[0:1, :]
    strict = (rows > cols) & same
    inclusive = (rows >= cols) & same
    carry_last = carry[BLOCK - 1 : BLOCK, :]
    carry_low, tail_low = carry.astype(LOW), tail.astype(LOW)
    heads = range(GROUP)

    @pl.when(turn == 0)
    def _():
        for h in heads:
            adjoint_ref[h] = leave_ref[h]
        spill_ref[...] = jnp.zeros_like(spill_ref)
        taps_grad_ref[...] = jnp.zeros_like(taps_grad_ref)

    strength = strength_ref[0]
    at = [slice(h * HD, (h + 1) * HD) for h in heads]
    query = [mixed_ref[0, :, at[h]] for h in heads]
    key = [mixed_ref[1, :, at[h]] for h in heads]
    value = [mixed_ref[2, :, at[h]] for h in heads]
    upstream = [upstream_ref[:, at[h]] for h in heads]
    enter = [enter_ref[h].astype(LOW) for h in heads]
    state = [
        (state_ref[0, h, :, :HD] + product(state_ref[0, h, :, HD:].astype(LOW), enter[h])).astype(LOW)
        for h in heads
    ]
    update = [
        (update_ref[:, at[h]] + product(drift_ref[:, at[h]], enter[h])).astype(LOW) for h in heads
    ]
    gram = [product(key[h], key[h], (1, 1)) for h in heads]
    scores = [
        jnp.where(inclusive, product(query[h], key[h], (1, 1)), 0.0).astype(LOW) for h in heads
    ]
    tail_key = [key[h] * tail_low for h in heads]
    adjoint = [adjoint_ref[h] for h in heads]
    adjoint_low = [adjoint[h].astype(LOW) for h in heads]
    grad_update = [
        (product(scores[h], upstream[h], (0, 0)) + product(tail_key[h], adjoint_low[h])).astype(LOW)
        for h in heads
    ]
    for h in heads:
        adjoint_ref[h] = (
            carry_last * adjoint[h]
            + product(query[h] * carry_low, upstream[h], (0, 0))
            - product(weight_ref[:, at[h]], grad_update[h], (0, 0))
        )
    grad_right = [product(solve_ref[0, h], grad_update[h], (0, 0)) for h in heads]
    right_low = [grad_right[h].astype(LOW) for h in heads]
    grad_scores = [
        jnp.where(inclusive, product(upstream[h], update[h], (1, 1)), 0.0).astype(LOW) for h in heads
    ]
    grad_query = [
        carry * product(upstream[h], state[h], (1, 1)) + product(grad_scores[h], key[h]) for h in heads
    ]
    right_state = [product(right_low[h], state[h], (1, 1)) for h in heads]
    grad_system = [
        jnp.where(strict, -product(right_low[h], update[h], (1, 1)), 0.0) for h in heads
    ]
    beta = [strength[:, h : h + 1] for h in heads]
    grad_gram = [(beta[h] * grad_system[h]).astype(LOW) for h in heads]
    grad_key = [
        product(grad_scores[h], query[h], (0, 0))
        + tail * product(update[h], adjoint_low[h], (1, 1))
        - (beta[h] * carry) * right_state[h]
        + product(grad_gram[h], key[h])
        + product(grad_gram[h], key[h], (0, 0))
        for h in heads
    ]
    grad_value = [beta[h] * grad_right[h] for h in heads]
    columns = [
        jnp.sum(
            grad_right[h] * value[h].astype(FULL)
            - carry * right_state[h] * key[h].astype(FULL)
            + grad_system[h] * gram[h],
            axis=-1,
            keepdims=True,
        )
        for h in heads
    ]
    strength_grad_ref[0] = jnp.concatenate(columns, axis=1)

    def rounded(values):
        return values.astype(LOW).astype(FULL)

    first = turn == last_turn
    grads = (grad_query, grad_key, grad_value)
    span = GROUP * HD
    for j in range(3):
        at = slice(j * span, (j + 1) * span)
        previous = jnp.where(first, rim_ref[:, at].astype(FULL), prev_ref[:, at].astype(FULL))
        taps = taps_ref[j]
        conv, shifted = short_conv(proj_ref[:, at].astype(FULL), previous, taps, meta)
        gate = jax.nn.sigmoid(conv)
        active = conv * gate
        pieces = []
        for h in heads:
            grad = rounded(grads[j][h])
            if j < 2:
                raw = lanes(active, h)
                scale = unit_scale(raw)
                unit = raw * scale
                if j == 0:
                    grad = grad * HD ** (-0.5)
                grad = scale * (grad - unit * jnp.sum(unit * grad, axis=-1, keepdims=True))
            pieces.append(grad)
        grad_conv = jnp.concatenate(pieces, axis=1) * (gate * (1.0 + conv * (1.0 - gate)))
        total = None
        for lag in range(CONV):
            taps_grad_ref[j, lag : lag + 1, :] += jnp.sum(grad_conv * shifted[lag], axis=0, keepdims=True)
            spread = grad_conv * (meta[:, lag : lag + 1] * taps[lag : lag + 1, :])
            spread = jnp.concatenate([jnp.zeros((8, span), FULL), spread], axis=0)
            if lag:
                spread = pltpu.roll(spread, BLOCK + 8 - lag, 0)
            total = spread if total is None else total + spread
        bottom = total[BLOCK:] + spill_ref[j]
        spill_ref[j] = total[:8]
        grad_ref[:, at] = jnp.concatenate([total[8:BLOCK], bottom], axis=0).astype(LOW)

        @pl.when(turn == 0)
        def _():
            edge_ref[:, at] = bottom

        lead_ref[:, at] = total[:8]


def backward_blocks(
    projected, rim, taps, strength, meta, meta_row, mixed, solve, weight, update, drift, upstream,
    states, enter, leave,
):
    total, width = projected.shape[0], projected.shape[1] // 3
    head_count = width // HD
    groups, steps = head_count // GROUP, total // BLOCK
    span = GROUP * HD
    strength_col = strength.reshape(total, groups, GROUP).transpose(1, 0, 2)
    ratio = BLOCK // RIM
    back = lambda n: steps - 1 - n
    wide = pl.BlockSpec((BLOCK, span), lambda g, n: (back(n), g))
    deep = pl.BlockSpec((3, BLOCK, span), lambda g, n: (0, back(n), g))
    per_group = pl.BlockSpec((GROUP, HD, HD), lambda g, n: (g, 0, 0))
    flat = pl.BlockSpec((BLOCK, 3 * span), lambda g, n: (back(n), g))
    narrow = pl.BlockSpec((8, 3 * span), lambda g, n: (0, g))
    grads, strength_grad, taps_grad, edge, lead = pl.pallas_call(
        backward_kernel,
        grid=(groups, steps),
        in_specs=[
            flat,
            pl.BlockSpec((RIM, 3 * span), lambda g, n: (jnp.maximum(back(n) * ratio - 1, 0), g)),
            pl.BlockSpec((RIM, 3 * span), lambda g, n: (0, g)),
            pl.BlockSpec((3, CONV, span), lambda g, n: (0, 0, g)),
            pl.BlockSpec((1, BLOCK, GROUP), lambda g, n: (g, back(n), 0)),
            pl.BlockSpec((BLOCK, 8), lambda g, n: (back(n), 0)),
            pl.BlockSpec((8, BLOCK), lambda g, n: (0, back(n))),
            deep,
            pl.BlockSpec((1, GROUP, BLOCK, BLOCK), lambda g, n: (back(n), g, 0, 0)),
            wide,
            wide,
            wide,
            wide,
            pl.BlockSpec((1, GROUP, HD, 2 * HD), lambda g, n: (back(n), g, 0, 0)),
            per_group,
            per_group,
        ],
        out_specs=(
            flat,
            pl.BlockSpec((1, BLOCK, GROUP), lambda g, n: (g, back(n), 0)),
            pl.BlockSpec((3, CONV, span), lambda g, n: (0, 0, g)),
            narrow,
            narrow,
        ),
        out_shape=(
            jax.ShapeDtypeStruct((total, 3 * width), LOW),
            jax.ShapeDtypeStruct((groups, total, GROUP), FULL),
            jax.ShapeDtypeStruct((3, CONV, width), FULL),
            jax.ShapeDtypeStruct((8, 3 * width), FULL),
            jax.ShapeDtypeStruct((8, 3 * width), FULL),
        ),
        scratch_shapes=[pltpu.VMEM((GROUP, HD, HD), FULL), pltpu.VMEM((3, 8, span), FULL)],
        compiler_params=pltpu.CompilerParams(vmem_limit_bytes=48 << 20),
        cost_estimate=pl.CostEstimate(flops=4 << 30, bytes_accessed=24 << 20, transcendentals=0),
    )(
        projected, projected, rim, taps, strength_col, meta, meta_row, mixed, solve, weight, update,
        drift, upstream, states, enter, leave,
    )
    return grads, strength_grad.transpose(1, 0, 2).reshape(total, head_count), taps_grad, edge, lead


def fsdp_split(count):
    along = 4 if count % 4 == 0 else 1
    return along, count // along


def gather_kernel(along, across, seq_count, shard_ref, small_ref, full_ref, small_full_ref, local_sem, small_send,
                  small_recv, z_send, z_recv, x_send, x_recv, core_send, core_recv):
    count = along * across
    seq, mine = lax.axis_index("seq"), lax.axis_index("fsdp")
    core, z, x = lax.rem(seq, 2), lax.div(mine, across), lax.rem(mine, across)
    partner = seq + 1 - 2 * core
    rows = shard_ref.shape[0]
    half = rows // 2
    mesh_id = pl.DeviceIdType.MESH

    barrier = pltpu.get_barrier_semaphore()
    for d in range(1, count):
        pl.semaphore_signal(barrier, inc=1, device_id=(seq, lax.rem(mine + d, count)), device_id_type=mesh_id)
    pl.semaphore_signal(barrier, inc=1, device_id=(partner, mine), device_id_type=mesh_id)
    pl.semaphore_wait(barrier, count)

    def place(k, j):
        owner = lax.rem(z - k + along, along) * across + lax.rem(x - j + across, across)
        start = pl.multiple_of(owner * rows + core * half, 16)
        return full_ref.at[pl.ds(start, half), :]

    own_half = shard_ref.at[pl.ds(pl.multiple_of(core * half, 16), half), :]
    keep = pltpu.make_async_copy(
        shard_ref, full_ref.at[pl.ds(pl.multiple_of(mine * rows, 16), rows), :], local_sem.at[0]
    )
    keep.start()
    small_place = small_full_ref.at[:, pl.ds(pl.multiple_of(mine * 128, 128), 128)]
    keep_small = pltpu.make_async_copy(small_ref, small_place, local_sem.at[1])
    keep_small.start()

    def sent(source, target, send, recv, device):
        copy = pltpu.make_async_remote_copy(
            src_ref=source, dst_ref=target, send_sem=send, recv_sem=recv, device_id=device, device_id_type=mesh_id
        )
        copy.start()
        return copy

    def along_z(k):
        source = own_half if k == 1 else place(k - 1, 0)
        device = (seq, lax.rem(z + 1, along) * across + x)
        return sent(source, place(k - 1, 0), z_send.at[k - 1], z_recv.at[k - 1], device)

    def along_x(k, j):
        source = own_half if k == 0 else place(k, 0)
        at = k * (across - 1) + j - 1
        device = (seq, z * across + lax.rem(x + j, across))
        return sent(source, place(k, 0), x_send.at[at], x_recv.at[at], device)

    def to_core(k, j):
        at = k * across + j
        return sent(place(k, j), place(k, j), core_send.at[at], core_recv.at[at], (partner, mine))

    copies = []
    z_copies = {1: along_z(1)} if along > 1 else {}
    x_copies = {}
    for j in range(1, across):
        x_copies[0, j] = along_x(0, j)
    for d in range(1, count):
        copies.append(
            sent(small_ref, small_place, small_send.at[d - 1], small_recv.at[d - 1],
                 (seq, lax.rem(mine + d, count)))
        )
    core_copies = []
    for k in range(1, along):
        z_copies[k].wait_recv()
        if k + 1 < along:
            z_copies[k + 1] = along_z(k + 1)
        for j in range(1, across):
            x_copies[k, j] = along_x(k, j)
        core_copies.append(to_core(k, 0))
        for j in range(1, across):
            x_copies[k - 1, j].wait_recv()
            core_copies.append(to_core(k - 1, j))
    for j in range(1, across):
        x_copies[along - 1, j].wait_recv()
        core_copies.append(to_core(along - 1, j))
    keep.wait()
    keep_small.wait()
    for copy in list(z_copies.values()) + list(x_copies.values()):
        copy.wait_send()
    for copy in copies + core_copies:
        copy.wait()


def gathered_mixer(shard, small, seq_count, fsdp_count):
    along, across = fsdp_split(fsdp_count)
    rows, width = shard.shape
    dma = pltpu.SemaphoreType.DMA
    hold = pl.BlockSpec(memory_space=pl.ANY)
    links = max(along * (across - 1), 1)
    return pl.pallas_call(
        partial(gather_kernel, along, across, seq_count),
        in_specs=[hold, hold],
        out_specs=(hold, hold),
        out_shape=(
            jax.ShapeDtypeStruct((rows * fsdp_count, width), shard.dtype),
            jax.ShapeDtypeStruct((small.shape[0], fsdp_count * 128), small.dtype),
        ),
        scratch_shapes=[
            dma((2,)),
            dma((fsdp_count - 1,)),
            dma((fsdp_count - 1,)),
            dma((along,)),
            dma((along,)),
            dma((links,)),
            dma((links,)),
            dma((along * across,)),
            dma((along * across,)),
        ],
        compiler_params=pltpu.CompilerParams(collective_id=0, has_side_effects=True),
    )(shard, small)


def core_swapped(value):
    count = lax.axis_size("seq")
    return lax.ppermute(value, "seq", [(i, i + 1 - 2 * (i % 2)) for i in range(count)])


def chip_shifted(value, by):
    count = lax.axis_size("seq")
    return lax.ppermute(value, "seq", [(i, (i + 2 * by) % count) for i in range(count)])


def seq_blocks(value):
    chips = lax.axis_size("seq") // 2
    far = [chip_shifted(value, k) for k in range(1, chips)]
    found = []
    for one in [value] + far:
        found += [one, core_swapped(one)]
    return found


def seq_stacked(value):
    count, index = lax.axis_size("seq"), lax.axis_index("seq")
    core = index % 2
    result = jnp.zeros((count,) + value.shape, value.dtype)
    for place, one in enumerate(seq_blocks(value)):
        chip = (index // 2 - place // 2) % (count // 2)
        at = chip * 2 + (core if place % 2 == 0 else 1 - core)
        result = lax.dynamic_update_slice_in_dim(result, one[None], at, 0)
    return result


def low_dot(left, right, dims):
    return lax.dot_general(left, right, (((dims[0],), (dims[1],)), ((), ())), preferred_element_type=FULL)


def exchange_kernel(backward, seq_count, local_ref, transfer_ref, result_ref, other_local, other_transfer, chip_ref, sent_ref,
                    swap_send, swap_recv, chip_send, chip_recv, half_send, half_recv):
    seq, mine = lax.axis_index("seq"), lax.axis_index("fsdp")
    core, chip = lax.rem(seq, 2), lax.div(seq, 2)
    partner = seq + 1 - 2 * core
    chips = seq_count // 2
    heads = local_ref.shape[0]
    mesh_id = pl.DeviceIdType.MESH
    lead = core == (1 if backward else 0)
    dims = (0, 0) if backward else (1, 0)
    step = -1 if backward else 1

    for head in range(heads):
        chip_ref[head] = jnp.zeros((HD, HD), FULL)
    barrier = pltpu.get_barrier_semaphore()
    pl.semaphore_signal(barrier, inc=1, device_id=(partner, mine), device_id_type=mesh_id)
    for k in range(1, chips):
        other = lax.rem(seq + 2 * k, seq_count)
        pl.semaphore_signal(barrier, inc=1, device_id=(other, mine), device_id_type=mesh_id)
    pl.semaphore_wait(barrier, chips)

    swaps = [
        pltpu.make_async_remote_copy(
            src_ref=source, dst_ref=target, send_sem=swap_send.at[i], recv_sem=swap_recv.at[i],
            device_id=(partner, mine), device_id_type=mesh_id,
        )
        for i, (source, target) in enumerate(((local_ref, other_local), (transfer_ref, other_transfer)))
    ]
    for swap in swaps:
        swap.start()
    for swap in swaps:
        swap.wait()
    share = pl.ds(pl.multiple_of(core * (heads // 2), heads // 2), heads // 2)

    def applied(matrix, value):
        return product(halves(matrix), halves(value), dims)

    for i in range(chips - 1):
        source = chips - 1 - i if backward else i

        @pl.when(chip == source)
        def _():
            for head in range(heads):
                lead_local = jnp.where(lead, local_ref[head], other_local[head])
                trail_local = jnp.where(lead, other_local[head], local_ref[head])
                lead_transfer = jnp.where(lead, transfer_ref[head], other_transfer[head])
                trail_transfer = jnp.where(lead, other_transfer[head], transfer_ref[head])
                inner = lead_local if i == 0 else lead_local + applied(lead_transfer, chip_ref[head])
                sent_ref[head] = trail_local + applied(trail_transfer, inner)

        onward = pltpu.make_async_remote_copy(
            src_ref=sent_ref.at[share], dst_ref=chip_ref.at[share], send_sem=chip_send.at[i], recv_sem=chip_recv.at[i],
            device_id=(lax.rem(seq + 2 * step + seq_count, seq_count), mine), device_id_type=mesh_id,
        )
        half = pltpu.make_async_remote_copy(
            src_ref=chip_ref.at[share], dst_ref=chip_ref.at[share], send_sem=half_send.at[i], recv_sem=half_recv.at[i],
            device_id=(partner, mine), device_id_type=mesh_id,
        )

        @pl.when(chip == source)
        def _():
            onward.start()
            onward.wait_send()

        @pl.when(chip == source + step)
        def _():
            onward.wait_recv()
            half.start()
            half.wait()

    for head in range(heads):
        lead_local = jnp.where(lead, local_ref[head], other_local[head])
        lead_transfer = jnp.where(lead, transfer_ref[head], other_transfer[head])
        state = chip_ref[head]
        result_ref[head] = jnp.where(lead, state, lead_local + applied(lead_transfer, state))


def exchanged(local, transfer, backward, call_id):
    seq_count = lax.axis_size("seq")
    dma = pltpu.SemaphoreType.DMA
    vmem = pl.BlockSpec(memory_space=pltpu.VMEM)
    hops = max(seq_count // 2 - 1, 1)
    return pl.pallas_call(
        partial(exchange_kernel, backward, seq_count),
        in_specs=[vmem, vmem],
        out_specs=vmem,
        out_shape=jax.ShapeDtypeStruct(local.shape, FULL),
        scratch_shapes=[pltpu.VMEM(local.shape, FULL)] * 4 + [dma((2,))] * 2 + [dma((hops,))] * 4,
        compiler_params=pltpu.CompilerParams(collective_id=call_id, has_side_effects=True, vmem_limit_bytes=24 << 20),
    )(local, transfer)


def norm_back(unit, scale, gain, grad):
    gained = jnp.sum(grad * unit, axis=0)
    grad = grad * gain
    return scale * (grad - unit * jnp.mean(grad * unit, axis=-1, keepdims=True)), gained


def matrix_owners(fsdp_count):
    along, across = fsdp_split(fsdp_count)
    if along == 4 and across > 1:
        first, second = across, 2 * across + 1
        return [(0, first), (0, second), (1, first), (1, second), (1, first + 1), (0, first + 1), (1, second - 1)]
    return [(m % 2, m * fsdp_count // 7) for m in range(7)]


def remote(source, target, send, recv, device):
    return pltpu.make_async_remote_copy(
        src_ref=source, dst_ref=target, send_sem=send, recv_sem=recv, device_id=device,
        device_id_type=pl.DeviceIdType.MESH,
    )


class Place:
    def __init__(self, seq_count, count):
        self.seq_count, self.count, self.chips = seq_count, count, seq_count // 2
        self.seq, self.mine = lax.axis_index("seq"), lax.axis_index("fsdp")
        self.core, self.chip = lax.rem(self.seq, 2), lax.div(self.seq, 2)
        self.partner = (self.seq + 1 - 2 * self.core, self.mine)

    def fsdp(self, d):
        return lax.rem(self.mine + d, self.count)

    def next_seq(self, k):
        return (lax.rem(self.seq + k, self.seq_count), self.mine)

    def next_chip(self, k):
        return (lax.rem(self.seq + 2 * k, self.seq_count), self.mine)

    def greet(self, chips_too):
        barrier = pltpu.get_barrier_semaphore()
        others = [(self.seq, self.fsdp(d)) for d in range(1, self.count)]
        others += [self.next_seq(k) for k in range(1, self.seq_count)] if chips_too else [self.partner]
        for other in others:
            pl.semaphore_signal(barrier, inc=1, device_id=other, device_id_type=pl.DeviceIdType.MESH)
        pl.semaphore_wait(barrier, len(others))


def collect(here, owners, pieces, whole, send, recv, local_sem, core_send, core_recv):
    def piece(n, target, source):
        return remote(pieces.at[n], whole.at[source, here.core], send.at[n], recv.at[source], (here.seq, target))

    for n, (row, owner) in enumerate(owners):
        @pl.when((here.chip == row) & (here.mine != owner))
        def _():
            piece(n, owner, here.mine).start()

    def finish():
        for n, (row, owner) in enumerate(owners):
            @pl.when((here.chip == row) & (here.mine == owner))
            def _():
                keep = pltpu.make_async_copy(pieces.at[n], whole.at[here.mine, here.core], local_sem)
                keep.start()
                for d in range(1, here.count):
                    piece(n, here.fsdp(d), here.fsdp(d)).wait_recv()
                keep.wait()
                half = whole.at[:, here.core]
                swap = remote(half, half, core_send, core_recv, here.partner)
                swap.start()
                swap.wait()

        for n, (row, owner) in enumerate(owners):
            @pl.when((here.chip == row) & (here.mine != owner))
            def _():
                piece(n, owner, here.mine).wait_send()

    return finish


def hand_back(here, owners, rows, parts, local_sem, send, recv, chip_send, chip_recv, core_send, core_recv):
    def part(m):
        return parts.at[m, here.core]

    def piece(m, d):
        return remote(rows.at[here.fsdp(d)], part(m), send.at[d], recv.at[m], (here.seq, here.fsdp(d)))

    def onward(m, k):
        return remote(part(m), part(m), chip_send.at[m, k - 1], chip_recv.at[m], here.next_chip(k))

    def swap(m):
        return remote(part(m), part(m), core_send.at[m], core_recv.at[m], here.partner)

    for m, (row, owner) in enumerate(owners):
        @pl.when((here.chip == row) & (here.mine == owner))
        def _():
            for d in range(1, here.count):
                piece(m, d).start()
            keep = pltpu.make_async_copy(rows.at[here.mine], part(m), local_sem)
            keep.start()
            keep.wait()

    def finish():
        for m, (row, owner) in enumerate(owners):
            @pl.when((here.chip == row) & (here.mine != owner))
            def _():
                piece(m, 0).wait_recv()

            @pl.when(here.chip == row)
            def _():
                for k in range(1, here.chips):
                    onward(m, k).start()
                swap(m).start()

        for m, (row, owner) in enumerate(owners):
            @pl.when(here.chip != row)
            def _():
                onward(m, 1).wait_recv()
                swap(m).start()

        for m, (row, owner) in enumerate(owners):
            swap(m).wait()

            @pl.when(here.chip == row)
            def _():
                for k in range(1, here.chips):
                    onward(m, k).wait_send()

            @pl.when((here.chip == row) & (here.mine == owner))
            def _():
                for d in range(1, here.count):
                    piece(m, d).wait_send()

    return finish


def collect_sems(kinds, count):
    dma = pltpu.SemaphoreType.DMA
    return [dma((kinds,)), dma((count,)), dma, dma, dma]


def hand_back_sems(kinds, count, chips):
    dma = pltpu.SemaphoreType.DMA
    return [dma, dma((count,)), dma((kinds,)), dma((kinds, chips)), dma((kinds,)), dma((kinds,)), dma((kinds,))]


def middle_kernel(owners, seq_count, count, part_ref, prior_ref, small_ref, wide_ref, sum_ref, small_out, square_whole,
                  wide_whole, chip_ref, total_ref, piece_ref, place_ref, seq_ref, chip_send, chip_recv, half_sem,
                  place_send, place_recv, seq_send, seq_recv, *sems):
    here = Place(seq_count, count)
    width = piece_ref.shape[2]
    chip_ref[here.chip] = part_ref[...]
    place_ref[here.mine] = small_ref[here.mine]
    here.greet(True)
    small_copies = []
    for d in range(1, count):
        copy = remote(
            small_ref.at[here.fsdp(d)], place_ref.at[here.mine], place_send.at[d - 1], place_recv.at[here.mine],
            (here.seq, here.fsdp(d)),
        )
        copy.start()
        small_copies.append(copy)
    own = chip_ref.at[here.chip]
    onward = [
        remote(own, own, chip_send.at[k - 1], chip_recv.at[here.chip], here.next_chip(k)) for k in range(1, here.chips)
    ]
    for copy in onward:
        copy.start()
    finish_wide = collect(here, owners[:3], wide_ref, wide_whole, *sems[:5])
    for k in range(1, here.chips):
        source = lax.rem(here.chip + k, here.chips)
        other = chip_ref.at[source]
        remote(other, other, chip_send.at[k - 1], chip_recv.at[source], here.next_chip(k)).wait_recv()
    total = chip_ref[0].astype(FULL)
    for i in range(1, here.chips):
        total = total + chip_ref[i].astype(FULL)
    total_ref[...] = total
    fresh = (momentum_decay * prior_ref[...] + total).astype(LOW)
    span = GROUP * HD
    for g in range(width // span):
        for j in range(3):
            at = (3 * g + j) * span
            piece_ref[j, :, g * span : (g + 1) * span] = fresh[:, at : at + span]
    piece_ref[3] = fresh[:, 3 * width :]
    finish_square = collect(here, owners[3:], piece_ref, square_whole, *sems[5:])
    half_copy = remote(total_ref, sum_ref.at[here.core], half_sem.at[0], half_sem.at[1], here.partner)
    half_copy.start()
    keep = pltpu.make_async_copy(total_ref, sum_ref.at[here.core], half_sem.at[2])
    keep.start()
    for d in range(1, count):
        source = here.fsdp(d)
        other = place_ref.at[source]
        remote(other, other, place_send.at[d - 1], place_recv.at[source], (here.seq, source)).wait_recv()
    small = place_ref[0]
    for i in range(1, count):
        small = small + place_ref[i]
    seq_ref[here.seq] = small
    own = seq_ref.at[here.seq]
    for k in range(1, seq_count):
        copy = remote(own, own, seq_send.at[k - 1], seq_recv.at[here.seq], here.next_seq(k))
        copy.start()
        small_copies.append(copy)
    for k in range(1, seq_count):
        source = lax.rem(here.seq + k, seq_count)
        other = seq_ref.at[source]
        remote(other, other, seq_send.at[k - 1], seq_recv.at[source], here.next_seq(k)).wait_recv()
    small = seq_ref[0]
    for i in range(1, seq_count):
        small = small + seq_ref[i]
    small_out[...] = small
    finish_square()
    finish_wide()
    keep.wait()
    half_copy.wait()
    for copy in onward + small_copies:
        copy.wait_send()


def middle(part, prior, small, wide, owners, call_id, seq_count, count):
    half, columns = part.shape
    width = columns // 4
    chips = seq_count // 2
    dma = pltpu.SemaphoreType.DMA
    hold, vmem = pl.BlockSpec(memory_space=pl.ANY), pl.BlockSpec(memory_space=pltpu.VMEM)
    return pl.pallas_call(
        partial(middle_kernel, owners, seq_count, count),
        in_specs=[vmem, vmem, vmem, hold],
        out_specs=(hold, vmem, hold, hold),
        out_shape=(
            jax.ShapeDtypeStruct((2, half, columns), FULL),
            jax.ShapeDtypeStruct(small.shape[1:], FULL),
            jax.ShapeDtypeStruct((count, 2, half, width), LOW),
            jax.ShapeDtypeStruct((count, 2) + wide.shape[1:], LOW),
        ),
        scratch_shapes=[
            pltpu.VMEM((chips, half, columns), LOW),
            pltpu.VMEM((half, columns), FULL),
            pltpu.VMEM((4, half, width), LOW),
            pltpu.VMEM(small.shape, FULL),
            pltpu.VMEM((seq_count,) + small.shape[1:], FULL),
            dma((max(chips - 1, 1),)),
            dma((chips,)),
            dma((3,)),
            dma((count,)),
            dma((count,)),
            dma((seq_count,)),
            dma((seq_count,)),
        ]
        + collect_sems(3, count)
        + collect_sems(4, count),
        compiler_params=pltpu.CompilerParams(collective_id=call_id, has_side_effects=True, vmem_limit_bytes=24 << 20),
    )(part, prior, small, wide)


def hand_back_kernel(owners, seq_count, count, wide_ref, square_ref, wide_parts, square_parts, *sems):
    here = Place(seq_count, count)
    here.greet(True)
    finish_square = hand_back(here, owners[3:], square_ref, square_parts, *sems[7:])
    finish_wide = hand_back(here, owners[:3], wide_ref, wide_parts, *sems[:7])
    finish_square()
    finish_wide()


def handed_back(wide_rows, square_rows, owners, call_id, seq_count, count):
    hold = pl.BlockSpec(memory_space=pl.ANY)
    chips = seq_count // 2
    return pl.pallas_call(
        partial(hand_back_kernel, owners, seq_count, count),
        in_specs=[hold, hold],
        out_specs=(hold, hold),
        out_shape=(
            jax.ShapeDtypeStruct((3, 2) + wide_rows.shape[1:], LOW),
            jax.ShapeDtypeStruct((4, 2) + square_rows.shape[1:], LOW),
        ),
        scratch_shapes=hand_back_sems(3, count, chips) + hand_back_sems(4, count, chips),
        compiler_params=pltpu.CompilerParams(collective_id=call_id, has_side_effects=True),
    )(wide_rows, square_rows)


def tile_count(width, seq_count):
    return -(-(width // HD) // seq_count)


def prepare_kernel(seq_count, mixer_ref, output_ref, gate_up_ref, down_ref, strength_ref, filter_ref, gain_ref, head_ref,
                   square_ref, ff_ref, small_ref):
    shard, width = output_ref.shape
    span = GROUP * HD
    tiles = gate_up_ref.shape[2] // HD
    per = tile_count(gate_up_ref.shape[2], seq_count)
    seq = lax.axis_index("seq")
    for g in range(width // span):
        for j in range(3):
            at = (3 * g + j) * span
            square_ref[:, at : at + span] = mixer_ref[j, :, g * span : (g + 1) * span].astype(LOW)
    square_ref[:, 3 * width :] = output_ref[...].astype(LOW)
    for i in range(per):
        tile = i * seq_count + seq
        at = pl.ds(pl.multiple_of(jnp.minimum(tile, tiles - 1) * HD, HD), HD)
        kept = jnp.where(tile < tiles, 1.0, 0.0).astype(FULL)
        for j in range(2):
            to = (j * per + i) * HD
            ff_ref[:, to : to + HD] = (gate_up_ref[j, :, at] * kept).astype(LOW)
        to = (2 * per + i) * HD
        ff_ref[:, to : to + HD] = (down_ref[at, :] * kept).T.astype(LOW)
    small_ref[...] = jnp.zeros_like(small_ref)
    heads = strength_ref.shape[1]
    rows = [strength_ref[...].T] + [filter_ref[j] for j in range(3)] + [gain_ref[...]]
    at = 0
    for one in rows:
        small_ref[at : at + one.shape[0], :shard] = one.astype(LOW)
        at += one.shape[0]
    small_ref[at : at + 1, : head_ref.shape[1]] = head_ref[...].astype(LOW)


def prepared(mixer, output, gate_up, down, strength, filters, gain, head, seq_count):
    shard, width = output.shape
    columns = 3 * tile_count(gate_up.shape[2], seq_count) * HD
    vmem = pl.BlockSpec(memory_space=pltpu.VMEM)
    return pl.pallas_call(
        partial(prepare_kernel, seq_count),
        in_specs=[vmem] * 8,
        out_specs=(vmem,) * 3,
        out_shape=(
            jax.ShapeDtypeStruct((shard, 4 * width), LOW),
            jax.ShapeDtypeStruct((shard, columns), LOW),
            jax.ShapeDtypeStruct((32, 128), LOW),
        ),
        compiler_params=pltpu.CompilerParams(vmem_limit_bytes=40 << 20),
    )(mixer, output, gate_up, down, strength, filters, gain, head[None])


def wide_moment_kernel(seq_count, gate_up_ref, down_ref, stack_ref, gate_up_out, down_out, sent_ref, hold_ref):
    half = sent_ref.shape[1]
    tiles = gate_up_ref.shape[2] // HD
    per = stack_ref.shape[2] // (3 * HD)
    core = lax.rem(lax.axis_index("seq"), 2)
    mine = pl.ds(pl.multiple_of(core * half, half), half)
    for t in range(tiles):
        source, i = t % seq_count, t // seq_count
        at = slice(t * HD, (t + 1) * HD)
        for j in range(2):
            grad = stack_ref[source, :, (j * per + i) * HD : (j * per + i + 1) * HD].astype(FULL)
            gate_up_out[j, :, at] = momentum_decay * gate_up_ref[j, :, at] + grad
            sent_ref[j, :, at] = gate_up_out[j, mine, at].astype(LOW)
        grad = stack_ref[source, :, (2 * per + i) * HD : (2 * per + i + 1) * HD].astype(FULL)
        fresh = momentum_decay * down_ref[at, :] + grad.T
        down_out[at, :] = fresh
        hold_ref[...] = fresh.T
        sent_ref[2, :, at] = hold_ref[mine, :].astype(LOW)


def wide_moments(gate_up, down, stack, seq_count):
    shard, width = gate_up.shape[1:]
    vmem = pl.BlockSpec(memory_space=pltpu.VMEM)
    return pl.pallas_call(
        partial(wide_moment_kernel, seq_count),
        in_specs=[vmem] * 3,
        out_specs=(vmem,) * 3,
        out_shape=(
            jax.ShapeDtypeStruct(gate_up.shape, FULL),
            jax.ShapeDtypeStruct(down.shape, FULL),
            jax.ShapeDtypeStruct((3, shard // 2, width), LOW),
        ),
        scratch_shapes=[pltpu.VMEM((shard, HD), FULL)],
        compiler_params=pltpu.CompilerParams(vmem_limit_bytes=40 << 20),
    )(gate_up, down, stack)


def finish_kernel(
    wide_ref, square_ref, sum_ref, small_ref, mixer_w, output_w, gate_up_w, down_w, strength_w, filter_w, gain_w, head_w,
    mixer_m, output_m, strength_m, filter_m, gain_m, head_m,
    new_mixer_m, new_mixer_w, new_strength_m, new_strength_w, new_filter_m, new_filter_w, new_gain_m, new_gain_w,
    new_head_m, new_head_w, new_output_m, new_output_w, new_gate_up_w, new_down_w,
):
    shard, width = output_w.shape
    span = GROUP * HD
    for g in range(width // span):
        for j in range(3):
            at, to = (3 * g + j) * span, slice(g * span, (g + 1) * span)
            new_mixer_m[j, :, to] = momentum_decay * mixer_m[j, :, to] + sum_ref[:, at : at + span]
    for j in range(3):
        new_mixer_w[j] = mixer_w[j] - matrix_rate * square_ref[j].astype(FULL)
    new_output_m[...] = momentum_decay * output_m[...] + sum_ref[:, 3 * width :]
    new_output_w[...] = output_w[...] - matrix_rate * square_ref[3].astype(FULL)
    for j in range(2):
        new_gate_up_w[j] = gate_up_w[j] - matrix_rate * wide_ref[j].astype(FULL)
    for t in range(down_w.shape[0] // HD):
        at = slice(t * HD, (t + 1) * HD)
        new_down_w[at, :] = down_w[at, :] - matrix_rate * wide_ref[2, :, at].astype(FULL).T
    heads = strength_w.shape[1]
    fresh = momentum_decay * strength_m[...] + small_ref[:heads, :].T
    new_strength_m[...] = fresh
    new_strength_w[...] = strength_w[...] - strength_rate * fresh
    for j in range(3):
        fresh = momentum_decay * filter_m[j] + small_ref[heads + CONV * j : heads + CONV * (j + 1), :]
        new_filter_m[j] = fresh
        new_filter_w[j] = filter_w[j] - filter_rate * fresh
    at = heads + 3 * CONV
    fresh = momentum_decay * gain_m[...] + small_ref[at : at + 2, :]
    new_gain_m[...] = fresh
    new_gain_w[...] = gain_w[...] - gain_rate * fresh
    fresh = momentum_decay * head_m[...] + small_ref[at + 2 : at + 3, : head_m.shape[1]]
    new_head_m[...] = fresh
    new_head_w[...] = head_w[...] - gain_rate * fresh


def finished(wide, square, total, small, weights, moments):
    mixer_w, output_w, gate_up_w, down_w, strength_w, filter_w, gain_w, head_w = weights
    mixer_m, output_m, strength_m, filter_m, gain_m, head_m = moments
    pairs = [mixer_w, strength_w, filter_w, gain_w, head_w[None], output_w]
    shapes = [jax.ShapeDtypeStruct(one.shape, FULL) for pair in zip(pairs, pairs) for one in pair]
    shapes += [jax.ShapeDtypeStruct(one.shape, FULL) for one in (gate_up_w, down_w)]
    vmem = pl.BlockSpec(memory_space=pltpu.VMEM)
    return pl.pallas_call(
        finish_kernel,
        in_specs=[vmem] * 18,
        out_specs=(vmem,) * len(shapes),
        out_shape=tuple(shapes),
        compiler_params=pltpu.CompilerParams(vmem_limit_bytes=56 << 20),
    )(
        wide, square, total, small, mixer_w, output_w, gate_up_w, down_w, strength_w, filter_w, gain_w, head_w[None],
        mixer_m, output_m, strength_m, filter_m, gain_m, head_m[None],
    )


TILE = 256


def row_loop(rows, body):
    @pl.loop(0, rows // TILE)
    def _(i):
        body(pl.ds(pl.multiple_of(i * TILE, TILE), TILE))


def trace_of(square_ref):
    total = jnp.zeros((1, 1), FULL)
    for i in range(square_ref.shape[0] // TILE):
        tile = square_ref[i * TILE : (i + 1) * TILE, i * TILE : (i + 1) * TILE]
        rows = lax.broadcasted_iota(jnp.int32, (TILE, TILE), 0)
        cols = lax.broadcasted_iota(jnp.int32, (TILE, TILE), 1)
        total = total + jnp.sum(jnp.where(rows == cols, tile, 0.0), keepdims=True)
    return total


def pick_rows(count, half, source_ref, target_ref):
    core = lax.rem(lax.axis_index("seq"), 2)
    for f in range(count):
        at = pl.multiple_of(f * 2 * half + core * half, 16)
        target_ref[f * half : (f + 1) * half, :] = source_ref[pl.ds(at, half), :]


def orth_wide_kernel(
    count, half, whole_ref, out_ref, square_ref, middle_ref, mapped_ref, gathered_ref,
    square_low, mapped_low, first_low, second_low, rows_low, rows_own,
):
    size = whole_ref.shape[0]

    def start(at):
        square_ref[at, :] = product(whole_ref[at, :], whole_ref[...], (1, 1))

    row_loop(size, start)
    scale = 1.0 / (jnp.sqrt(trace_of(square_ref)) + 1e-07)

    def scaled(at):
        value = square_ref[at, :] * (scale * scale)
        square_ref[at, :] = value
        square_low[at, :] = value.astype(LOW)

    row_loop(size, scaled)
    level = 1.0
    gathered_low, spare_low = first_low, second_low
    for sweep in range(NS_STEPS):
        keep_ref = gathered_ref if sweep == 0 else mapped_ref

        def mapping(at):
            value = coef_cubic * square_ref[at, :] + coef_quintic * product(square_low[at, :], square_low[...])
            keep_ref[at, :] = value
            mapped_low[at, :] = value.astype(LOW)

        row_loop(size, mapping)
        if sweep == 0:
            def copy_low(at):
                gathered_low[at, :] = mapped_low[at, :]

            row_loop(size, copy_low)
        else:
            def gather(at):
                value = (
                    coef_linear * gathered_ref[at, :]
                    + level * mapped_ref[at, :]
                    + product(mapped_low[at, :], gathered_low[...])
                )
                gathered_ref[at, :] = value
                spare_low[at, :] = value.astype(LOW)

            row_loop(size, gather)
            gathered_low, spare_low = spare_low, gathered_low
        level = level * coef_linear
        if sweep < NS_STEPS - 1:
            def middle(at):
                value = coef_linear * square_ref[at, :] + product(mapped_low[at, :], square_low[...])
                middle_ref[at, :] = value
                spare_low[at, :] = value.astype(LOW)

            row_loop(size, middle)

            def squared(at):
                value = coef_linear * middle_ref[at, :] + product(spare_low[at, :], mapped_low[...])
                square_ref[at, :] = value
                square_low[at, :] = value.astype(LOW)

            row_loop(size, squared)
    pick_rows(count, half, gathered_low, rows_low)
    pick_rows(count, half, whole_ref, rows_own)

    @pl.loop(0, whole_ref.shape[1] // TILE)
    def _(i):
        at = pl.ds(pl.multiple_of(i * TILE, TILE), TILE)
        value = level * rows_own[:, at].astype(FULL) + product(rows_low[...], whole_ref[:, at])
        out_ref[:, at] = (value * scale).astype(LOW)


def orth_square_kernel(
    count, half, whole_ref, out_ref, square_ref, current_ref, square_low, mapped_low, first_low, second_low,
    rows_low, rows_own,
):
    size = whole_ref.shape[0]

    def start(at):
        square_ref[at, :] = product(whole_ref[at, :], whole_ref[...], (1, 1))

    row_loop(size, start)
    scale = 1.0 / (jnp.sqrt(trace_of(square_ref)) + 1e-07)

    def scaled(at):
        value = whole_ref[at, :].astype(FULL) * scale
        current_ref[at, :] = value
        first_low[at, :] = value.astype(LOW)
        value = square_ref[at, :] * (scale * scale)
        square_ref[at, :] = value
        square_low[at, :] = value.astype(LOW)

    row_loop(size, scaled)
    now, later = first_low, second_low
    for sweep in range(NS_STEPS):
        if sweep:
            def squared(at):
                value = product(now[at, :], now[...], (1, 1))
                square_ref[at, :] = value
                square_low[at, :] = value.astype(LOW)

            row_loop(size, squared)

        def mapping(at):
            value = coef_cubic * square_ref[at, :] + coef_quintic * product(square_low[at, :], square_low[...])
            mapped_low[at, :] = value.astype(LOW)

        row_loop(size, mapping)
        if sweep < NS_STEPS - 1:
            def step(at):
                value = coef_linear * current_ref[at, :] + product(mapped_low[at, :], now[...])
                current_ref[at, :] = value
                later[at, :] = value.astype(LOW)

            row_loop(size, step)
            now, later = later, now
    pick_rows(count, half, mapped_low, rows_low)
    pick_rows(count, half, current_ref, rows_own)

    @pl.loop(0, size // TILE)
    def _(i):
        at = pl.ds(pl.multiple_of(i * TILE, TILE), TILE)
        value = coef_linear * rows_own[:, at] + product(rows_low[...], now[:, at])
        out_ref[:, at] = value.astype(LOW)


def orth_call(kernel, scratch, count, whole):
    half, width = whole.shape[2:]
    size = count * 2 * half
    flat = whole.reshape(size, width)
    vmem = pl.BlockSpec(memory_space=pltpu.VMEM)
    result = pl.pallas_call(
        partial(kernel, count, half),
        in_specs=[vmem],
        out_specs=vmem,
        out_shape=jax.ShapeDtypeStruct((size // 2, width), LOW),
        scratch_shapes=scratch(size, width),
        compiler_params=pltpu.CompilerParams(vmem_limit_bytes=56 << 20),
    )(flat)
    return result.reshape(count, half, width)


def orth_wide(count, whole):
    def scratch(size, width):
        return (
            [pltpu.VMEM((size, size), FULL)] * 4
            + [pltpu.VMEM((size, size), LOW)] * 4
            + [pltpu.VMEM((size // 2, size), LOW), pltpu.VMEM((size // 2, width), LOW)]
        )

    return orth_call(orth_wide_kernel, scratch, count, whole)


def orth_square(count, whole):
    def scratch(size, width):
        return (
            [pltpu.VMEM((size, size), FULL)] * 2
            + [pltpu.VMEM((size, size), LOW)] * 4
            + [pltpu.VMEM((size // 2, size), LOW), pltpu.VMEM((size // 2, width), FULL)]
        )

    return orth_call(orth_square_kernel, scratch, count, whole)


def chosen_place(owners, mine, chip):
    chosen = (mine == owners[0][1]) & (chip == owners[0][0])
    for row, place in owners[1:]:
        chosen = chosen | ((mine == place) & (chip == row))
    return chosen


def orthogonal(whole, owners, method, mine, chip, count):
    half, width = whole.shape[2:]
    return lax.cond(
        chosen_place(owners, mine, chip),
        partial(method, count),
        lambda one: jnp.zeros((count, half, width), LOW),
        whole,
    )


def on_device(
    inputs,
    cotangent,
    lengths,
    mixer_weight,
    strength_weight,
    filter_weight,
    norm_gain,
    head_gain,
    output_weight,
    gate_up_weight,
    down_weight,
    mixer_moment,
    strength_moment,
    filter_moment,
    gain_moment,
    head_gain_moment,
    output_moment,
    gate_up_moment,
    down_moment,
):
    seq_count = lax.axis_size("seq")
    seq_index = lax.axis_index("seq")
    fsdp_count = lax.axis_size("fsdp")
    fsdp_index = lax.axis_index("fsdp")
    row_count, width = inputs.shape
    shard = width // fsdp_count
    heads_all = strength_weight.shape[1]

    wide_ff = tile_count(gate_up_weight.shape[2], seq_count) * HD
    core = seq_index % 2
    half = shard // 2
    groups = heads_all // GROUP
    span = GROUP * HD
    small_count = heads_all + 3 * CONV + 3
    top_near = core_swapped(cotangent)
    top_far = [chip_shifted(cotangent, k) for k in range(1, seq_count // 2)]
    square_own, ff_own, small_own = prepared(
        mixer_weight, output_weight, gate_up_weight, down_weight, strength_weight, filter_weight, norm_gain, head_gain,
        seq_count,
    )
    square_full, small_full = gathered_mixer(square_own, small_own, seq_count, fsdp_count)
    by_place = small_full.reshape(-1, fsdp_count, 128)
    small_wide = small_full if shard == 128 else by_place[:, :, :shard].reshape(-1, width)
    strength_full = small_wide[:heads_all]
    filters_wide = small_wide[heads_all : heads_all + 3 * CONV].reshape(3, CONV, width).astype(FULL)
    gains_wide = small_wide[heads_all + 3 * CONV : heads_all + 3 * CONV + 2].astype(FULL)
    head_part = head_gain.shape[0]
    head_gain_full = by_place[small_count - 1, :, :head_part].reshape(1, HD).astype(FULL)

    square_full, ff_own, top_near, top_far = lax.optimization_barrier((square_full, ff_own, top_near, top_far))
    top_parts = [cotangent, top_near] + [part for one in top_far for part in (one, core_swapped(one))]
    ff_full = lax.all_gather(ff_own, "fsdp", axis=0, tiled=True)
    mixer_full, output_full = square_full[:, : 3 * width], square_full[:, 3 * width :]
    ff_parts = [ff_full[:, j * wide_ff : (j + 1) * wide_ff] for j in range(3)]

    my_lengths = lax.dynamic_slice_in_dim(lengths, fsdp_index, 1, 0)[0]
    doc_ends = jnp.cumsum(my_lengths)

    def passed_docs(at):
        return (at[:, None] >= doc_ends[None, :]).astype(jnp.int32)

    own = seq_index * row_count + jnp.arange(row_count, dtype=jnp.int32)
    passed = passed_docs(own)
    segment = jnp.sum(passed, axis=1)
    doc_first = jnp.sum(passed * my_lengths[None, :], axis=1)
    block_start = own.reshape(-1, BLOCK)[:, 0]
    before = jnp.where(block_start == 0, -1, jnp.sum(passed_docs(block_start - 1), axis=1))
    blocked = segment.reshape(-1, BLOCK)
    carried = (blocked == before[:, None]).reshape(-1)
    trailing = (blocked == blocked[:, -1:]).reshape(-1)
    columns = [own - lag >= doc_first for lag in range(CONV)] + [carried, trailing, segment]
    meta = jnp.stack([one.astype(FULL) for one in columns] + [jnp.zeros((row_count,), FULL)], axis=1)
    meta_row = jnp.broadcast_to(segment.astype(FULL)[None, :], (8, row_count))

    residual_in = inputs.astype(FULL)
    scale_one = lax.rsqrt(jnp.mean(residual_in * residual_in, axis=-1, keepdims=True) + norm_eps)
    unit_one = residual_in * scale_one
    normed_low = (unit_one * gains_wide[0]).astype(LOW)
    projected = low_dot(normed_low, mixer_full, (1, 0)).astype(LOW)
    logits = low_dot(normed_low, strength_full, (1, 1))
    strength = jax.nn.sigmoid(logits).astype(LOW).astype(FULL)
    forth = [(i, i + 1) for i in range(seq_count - 1)]
    rim = lax.ppermute(projected[row_count - RIM :], "seq", forth)
    mixed, solve, weight, update, drift, local_out, effective, states, end, transfer = forward_blocks(
        projected, rim, filters_wide, strength, meta, meta_row
    )
    enter = exchanged(end, transfer, False, 4)
    delta_out, head_normed = head_outputs(local_out, effective, enter, head_gain_full)
    residual = residual_in + low_dot(head_normed, output_full, (1, 0))
    scale_two = lax.rsqrt(jnp.mean(residual * residual, axis=-1, keepdims=True) + norm_eps)
    unit_two = residual * scale_two
    normed_two = (unit_two * gains_wide[1]).astype(LOW)
    gate_full, up_full, down_full = ff_parts
    chips = seq_count // 2
    near_norm = jnp.concatenate([normed_two, core_swapped(normed_two)])
    far_straight = [chip_shifted(normed_two, k) for k in range(1, chips)]

    def spread_out(normed_part, top_part):
        gate = low_dot(normed_part, gate_full, (1, 0))
        up = low_dot(normed_part, up_full, (1, 0))
        gate_sigmoid = jax.nn.sigmoid(gate)
        gate_silu = gate * gate_sigmoid
        hidden = (gate_silu * up).astype(LOW)
        grad_hidden = low_dot(top_part, down_full, (1, 0))
        grad_gate = (grad_hidden * up * (gate_sigmoid * (1.0 + gate * (1.0 - gate_sigmoid)))).astype(LOW)
        grad_up = (grad_hidden * gate_silu).astype(LOW)
        return hidden, grad_gate, grad_up

    def grad_in(values):
        return low_dot(values[1], gate_full, (1, 1)) + low_dot(values[2], up_full, (1, 1))

    def weight_grad(values, normed_part, top_part, which):
        left, right = ((normed_part, values[1]), (normed_part, values[2]), (top_part, values[0]))[which]
        return low_dot(left, right, (0, 0))

    near_top, far_top = jnp.concatenate(top_parts[:2]), jnp.concatenate(top_parts[2:])
    near = spread_out(near_norm, near_top)
    near_grad = grad_in(near)
    far_straight, near, near_grad = lax.optimization_barrier((far_straight, near, near_grad))
    far_parts = [part for one in far_straight for part in (one, core_swapped(one))]
    near_back = core_swapped(near_grad[row_count:].astype(LOW))
    near_out = low_dot(near[0], down_full, (1, 1))
    near_weights = [weight_grad(near, near_norm, near_top, 0)]
    near_weights, near_out, far_parts = lax.optimization_barrier((near_weights, near_out, far_parts))
    far_norm = jnp.concatenate(far_parts)
    far = spread_out(far_norm, far_top)

    def picked(values, side):
        size = 2 * row_count
        return [
            tuple(one[i * size + side * row_count : i * size + (side + 1) * row_count] for one in values)
            for i in range(chips - 1)
        ]

    crossed = [core_swapped(grad_in(one).astype(LOW)) for one in picked(far, 1)]
    joint = [(grad_in(one) + other.astype(FULL)).astype(LOW) for one, other in zip(picked(far, 0), crossed)]
    far, near, joint = lax.optimization_barrier((far, near, joint))
    grad_parts = [chip_shifted(one, -(k + 1)) for k, one in enumerate(joint)]
    near_weights = list(near_weights) + [weight_grad(near, near_norm, near_top, j) for j in (1, 2)]
    far_weights = [weight_grad(far, far_norm, far_top, j) for j in range(3)]
    ff_grads = jnp.concatenate([(a + b).astype(LOW) for a, b in zip(near_weights, far_weights)], axis=1)
    ff_part = lax.psum_scatter(ff_grads, "fsdp", scatter_dimension=0, tiled=True)
    far_out = low_dot(far[0], down_full, (1, 1))
    out_crossed = [core_swapped(one[0].astype(LOW)) for one in picked((far_out,), 1)]
    out_joint = [(one[0] + other.astype(FULL)).astype(LOW) for one, other in zip(picked((far_out,), 0), out_crossed)]
    out_near = near_out[:row_count] + core_swapped(near_out[row_count:].astype(LOW)).astype(FULL)
    done_grads, out_joint, out_near, grad_parts = lax.optimization_barrier((ff_grads, out_joint, out_near, grad_parts))
    grad_normed_two = near_grad[:row_count] + sum(one.astype(FULL) for one in [near_back] + list(grad_parts))
    back_two, grad_gain_two = norm_back(unit_two, scale_two, gains_wide[1], grad_normed_two)
    grad_residual = back_two + cotangent.astype(FULL)
    grad_attention = grad_residual.astype(LOW)
    grad_head_normed = low_dot(grad_attention, output_full, (1, 1)).astype(LOW)

    upstream, adjoint_local, grad_head_gain = head_back(
        grad_head_normed, delta_out, effective, head_gain_full
    )
    leave = exchanged(adjoint_local, transfer, True, 5)
    leave, out_joint = lax.optimization_barrier((leave, out_joint))
    out_parts = [chip_shifted(one, -(k + 1)) for k, one in enumerate(out_joint)]
    grad_projected, grad_strength, grad_filter, edge, lead = backward_blocks(
        projected, rim, filters_wide, strength, meta, meta_row, mixed, solve, weight, update, drift,
        upstream, states, enter, leave,
    )
    lead, out_parts = lax.optimization_barrier((lead, out_parts))
    back = [(i + 1, i) for i in range(seq_count - 1)]
    incoming = lax.ppermute(lead.astype(LOW), "seq", back).astype(FULL)
    grad_projected = lax.dynamic_update_slice(
        grad_projected, (edge + incoming).astype(LOW), (row_count - 8, 0)
    )
    grad_strength = grad_strength.astype(LOW).astype(FULL)
    grad_logits = (grad_strength * strength * (1.0 - strength)).astype(LOW)
    def core_rows(values):
        by_core = values.reshape(row_count, fsdp_count, 2, half)
        return [
            lax.dynamic_slice_in_dim(by_core, at, 1, 2).reshape(row_count, width // 2) for at in (core, 1 - core)
        ]

    grad_mixer = [low_dot(one, grad_projected, (0, 0)) for one in core_rows(normed_low)]
    grad_output = [low_dot(one, grad_attention, (0, 0)) for one in core_rows(head_normed)]
    square_grads = jnp.concatenate(
        [
            (mine + core_swapped(other.astype(LOW)).astype(FULL)).astype(LOW)
            for mine, other in (grad_mixer, grad_output)
        ],
        axis=1,
    )
    square_grads, ff_part, grad_projected, grad_logits = lax.optimization_barrier(
        (square_grads, ff_part, grad_projected, grad_logits)
    )
    square_part = lax.psum_scatter(square_grads, "fsdp", scatter_dimension=0, tiled=True)
    grad_strength_weight = low_dot(grad_logits, normed_low, (0, 0))
    grad_normed = low_dot(grad_logits, strength_full, (1, 0)) + low_dot(grad_projected, mixer_full, (1, 1))
    ff_stack = seq_stacked(ff_part)
    back_one, grad_gain_one = norm_back(unit_one, scale_one, gains_wide[0], grad_normed)
    input_grad = grad_residual + back_one

    head_row = jnp.pad(
        grad_head_gain.reshape(fsdp_count, head_part), ((0, 0), (0, shard - head_part))
    ).reshape(1, width)
    small_grads = jnp.concatenate(
        [
            grad_strength_weight,
            grad_filter.reshape(3 * CONV, width),
            grad_gain_one[None],
            grad_gain_two[None],
            head_row,
            jnp.zeros((-small_count % 8, width), FULL),
        ],
        axis=0,
    )
    small_pieces = small_grads.reshape(-1, fsdp_count, shard).transpose(1, 0, 2)

    ff_stack, input_grad, small_pieces = lax.optimization_barrier((ff_stack, input_grad, small_pieces))
    new_gate_up_moment, new_down_moment, wide_sent = wide_moments(gate_up_moment, down_moment, ff_stack, seq_count)
    owners = tuple(matrix_owners(fsdp_count))
    chip = seq_index // 2
    mixer_prior = lax.dynamic_slice_in_dim(mixer_moment, core * half, half, 1)
    output_prior = lax.dynamic_slice_in_dim(output_moment, core * half, half, 0)
    square_prior = jnp.concatenate(
        [mixer_prior[j, :, g * span : (g + 1) * span] for g in range(groups) for j in range(3)] + [output_prior], axis=1
    )
    block_output = residual + (out_near + sum(one.astype(FULL) for one in out_parts))
    wide_sent, square_prior, block_output = lax.optimization_barrier((wide_sent, square_prior, block_output))
    square_sum, small_own, square_all, wide_all = middle(
        square_part, square_prior, small_pieces, wide_sent, owners, 2, seq_count, fsdp_count
    )
    square_rows = orthogonal(square_all, owners[3:], orth_square, fsdp_index, chip, fsdp_count)
    wide_rows = orthogonal(wide_all, owners[:3], orth_wide, fsdp_index, chip, fsdp_count)
    wide_parts, square_parts = handed_back(wide_rows, square_rows, owners, 3, seq_count, fsdp_count)
    weights = (
        mixer_weight, output_weight, gate_up_weight, down_weight, strength_weight, filter_weight, norm_gain, head_gain
    )
    moments = (mixer_moment, output_moment, strength_moment, filter_moment, gain_moment, head_gain_moment)
    done = finished(
        wide_parts.reshape(3, shard, -1),
        square_parts.reshape(4, shard, width),
        square_sum.reshape(shard, -1),
        small_own,
        weights,
        moments,
    )
    head_pair = [one[0] for one in done[8:10]]
    return (
        (block_output, input_grad)
        + tuple(done[:8])
        + tuple(head_pair)
        + tuple(done[10:12])
        + (new_gate_up_moment, done[12], new_down_moment, done[13])
    )


def solution(mesh):
    return jax.shard_map(
        on_device,
        mesh=mesh,
        in_specs=(
            P(("seq", "fsdp"), None),
            P(("seq", "fsdp"), None),
            P(),
            P(None, "fsdp", None),
            P("fsdp", None),
            P(None, None, "fsdp"),
            P(None, "fsdp"),
            P("fsdp"),
            P("fsdp", None),
            P(None, "fsdp", None),
            P(None, "fsdp"),
            P(None, "fsdp", None),
            P("fsdp", None),
            P(None, None, "fsdp"),
            P(None, "fsdp"),
            P("fsdp"),
            P("fsdp", None),
            P(None, "fsdp", None),
            P(None, "fsdp"),
        ),
        out_specs=(
            P(("seq", "fsdp"), None),
            P(("seq", "fsdp"), None),
            P(None, "fsdp", None),
            P(None, "fsdp", None),
            P("fsdp", None),
            P("fsdp", None),
            P(None, None, "fsdp"),
            P(None, None, "fsdp"),
            P(None, "fsdp"),
            P(None, "fsdp"),
            P("fsdp"),
            P("fsdp"),
            P("fsdp", None),
            P("fsdp", None),
            P(None, "fsdp", None),
            P(None, "fsdp", None),
            P(None, "fsdp"),
            P(None, "fsdp"),
        ),
        check_vma=False,
    )
```

time: 3150 us -> 578 us (0.18)
  waiting for transfers between devices: 844 us -> 84.3 us
  matrix products: 767 us -> 83 us
  local copies, waits for them, and re-layouts: 473 us -> 54.5 us
  starting transfers between devices: 378 us -> 15.5 us
  other arithmetic: 361 us -> 26.9 us
  Pallas kernels: 0 us -> 290 us
  blocking collectives: 264 us -> 0 us
    dot_general x410 -> x31, matrix products: 756 us -> 83 us  [low_dot(): lax.dot_general(left, right, (((dims[0],), (dims[1],)), ((), ())), prefer...]
    unnamed x18 -> x3, waiting for transfers between devices: 527 us -> 0.05 us
    all_to_all x8 -> x0, starting transfers between devices: 373 us -> none  [the longest x1 300 us: on_device(): lax.all_to_all(wide_orth[None].astype(jnp.bfloat16), 'fsdp', split_axis=1...]
    pallas_call x0 -> x12, Pallas kernels: none -> 290 us  [the longest x1 114 us: handed_back(): pl.pallas_call(partial(hand_back_kernel, owners, seq_count, count), in_sp...]
    all_to_all x8 -> x0, waiting for transfers between devices: 152 us -> none  [the longest x1 95.1 us: on_device(): lax.all_to_all(wide_send.astype(jnp.bfloat16), 'fsdp', split_axis=0, conc...]
    another operation x12 -> x1, other arithmetic: 141 us -> 0.18 us  [the longest x5 140 us: delta_blocks(): jax.scipy.linalg.solve_triangular(system, right_side, lower=True, unit_di...]
    unnamed x2 -> x0, blocking collectives: 135 us -> none
    unnamed x278 -> x158, local copies, waits for them, and re-layouts: 170 us -> 34.8 us
  transfers between devices with their start and end apart: 22 -> 22, of which waited for: 14 -> 7; matrix products, arithmetic and copies ran while one was open for 27% -> 22% of each run, Pallas kernels for 0% -> 25%
where the time goes in v1:
time: 578 us; the launch traced here: 570 us
  Pallas kernels  290 us (50%)
  waiting for transfers between devices  84.3 us (15%)
  matrix products  83 us (14%)
  local copies, waits for them, and re-layouts  54.5 us (9%)
  other arithmetic  26.9 us (5%)
  starting transfers between devices  15.5 us (3%)
  between operations  15.3 us (3%)
    pallas_call x1, Pallas kernels, handed_back(): pl.pallas_call(partial(hand_back_kernel, owners, seq_count, count), in_sp...  114 us
    dot_general x31, matrix products, low_dot(): lax.dot_general(left, right, (((dims[0],), (dims[1],)), ((), ())), prefer...  83 us
    reduce_scatter x1, waiting for transfers between devices, on_device(): lax.psum_scatter(square_grads, 'fsdp', scatter_dimension=0, tiled=True)  56.6 us
    pallas_call x1, Pallas kernels, gathered_mixer(): pl.pallas_call(partial(gather_kernel, along, across, seq_count), in_specs...  54 us
    unnamed x158, local copies, waits for them, and re-layouts  34.8 us
    pallas_call x1, Pallas kernels, backward_blocks(): pl.pallas_call(backward_kernel, grid=(groups, steps), in_specs=[flat, pl....  28.9 us
    pallas_call x2, Pallas kernels, exchanged(): pl.pallas_call(partial(exchange_kernel, backward, seq_count), in_specs=[v...  26.5 us
    pallas_call x1, Pallas kernels, forward_blocks(): pl.pallas_call(forward_kernel, grid=(groups, steps), in_specs=[pl.BlockSp...  24.8 us
  transfers between devices with their start and end apart: 22, of which 7 were waited for; matrix products, arithmetic and copies ran while one was open for 22% of the time, Pallas kernels for 25%

profile of v1, /device:TPU:31, one launch (start us, length us, event | category | flops | bytes accessed | tf_op | source)
XLA Modules:
  0.0 569.9 jit_solution(7416148863288757791)
XLA Ops:
  19.3 54.0 %shard_map.323 = (bf16[1024,4096]{1,0:T(8,128)(2,1)}, bf16[32,1024]{1,0:T(8,128)(2,1)}) custom-call(bf16[128,4096]{1,0:T(8,128)(2,1)} %copy-done.14, bf16[32,128]{1,0:T(8,128)(2,1)} %copy-done.30), custom_call_target="tpu_custom_call" | custom-call | tf_op jit(solution)/shard_map/pallas_call | solution.py:605
  79.7 6.6 %fusion.4.proj_ref.prev_ref = bf16[512,3072]{1,0:T(8,128)(2,1)S(1)} fusion(bf16[512,1024]{1,0:T(8,128)(2,1)S(1)} %fusion.13, bf16[1024,4096]{1,0:T(8,128)(2,1)} %get-tuple-element.115), kind=kOutput, calls=%fused_computation.6 | convolution fusion | flops 3222798336 | bytes 10485760 | tf_op jit(solution)/shard_map/dot_general | solution.py:659
  91.2 24.8 %shard_map.324 = (bf16[3,512,1024]{2,1,0:T(8,128)(2,1)}, bf16[4,8,128,128]{3,2,1,0:T(8,128)(2,1)S(1)}, bf16[512,1024]{1,0:T(8,128)(2,1)S(1)}, f32[512,1024]{1,0:...) custom-call(bf16[512,3072]{1,0:T(8,128)(2,1)} %copy-done.43, ...), custom_call_target="tpu_custom_call" | custom-call | flops 8589934592 | bytes 25165824 | tf_op jit(solution)/shard_map/pallas_call | solution.py:204
  116.1 16.2 %shard_map.325.state_ref.enter_ref = f32[8,128,128]{2,1,0:T(8,128)S(1)} custom-call(f32[8,128,128]{2,1,0:T(8,128)S(1)} %get-tuple-element.123.local_ref, f32[8,128,128]{2,1,0:T(8,128)S(1)} %get-tuple-element.124.transfer_ref), custom_call_target="tpu_custom_call" | custom-call | tf_op jit(solution)/shard_map/pallas_call | solution.py:744
  145.2 6.0 %all-gather.2.cloned.1.call-done = bf16[1024,2304]{1,0:T(8,128)(2,1)} async-done(((bf16[128,2304]{1,0:T(8,128)(2,1)}), bf16[1024,2304]{1,0:T(8,128)(2,1)}) %all-gather.2.cloned.1.call-update) | async-done | bytes 4718608 | tf_op jit(solution)/shard_map/all_gather | solution.py:1434
  151.2 4.0 fusion.51
  158.8 4.1 multiply_convert_fusion.3
  164.7 3.8 convolution_add_fusion
  184.6 3.7 multiply_convert_fusion
  215.6 3.8 convert_add_fusion.2
  222.2 15.5 %collective-permute-done.11 = bf16[512,1024]{1,0:T(8,128)(2,1)S(1)} collective-permute-done((bf16[512,1024]{1,0:T(8,128)(2,1)}, bf16[512,1024]{1,0:T(8,128)(2,1)S(1)}, u32[]{:S(2)}, u32[]{:S(2)}) %collective-permute-start.11) | collective-permute-done | bytes 1048608 | tf_op jit(solution)/shard_map/ppermute | solution.py:635
  239.9 3.7 fusion.30.grad_ref
  246.7 10.3 %shard_map.328.leave_ref = f32[8,128,128]{2,1,0:T(8,128)S(1)} custom-call(f32[8,128,128]{2,1,0:T(8,128)S(1)} %get-tuple-element.148.local_ref, f32[8,128,128]{2,1,0:T(8,128)S(1)} %get-tuple-element.124.transfer_ref), custom_call_target="tpu_custom_call" | custom-call | tf_op jit(solution)/shard_map/pallas_call | solution.py:744
  257.0 4.0 collective-permute-start.12
  266.8 28.9 %shard_map.329 = (bf16[512,3072]{1,0:T(8,128)(2,1)}, f32[1,512,8]{2,1,0:T(8,128)S(1)}, f32[3,4,1024]{2,1,0:T(4,128)S(1)}, f32[8,3072]{1,0:T(8,128)S(1)}, f32[8,3072]{1,0:T(8,128)S(1)}) custom-call(bf16[512,3072]{1,0:T(8,128)(2,1)} %copy-done.43, bf16[512,3072]{1,0:T(8,128)(2,1)} %copy-done.43, bf16[16,3072]{1,0:T(8,128)(2,1)S(1)} %collective-permute-done.2.rim_ref, ...), custom_call_target="tpu_custom_call" | custom-call | flops 4294967296 | bytes 25165824 | tf_op jit(solution)/shard_map/pallas_call | solution.py:465
  299.6 5.4 convolution_convert_fusion
  314.8 3.7 add_convert_fusion
  325.0 3.9 add_add_fusion
  332.7 8.0 %fusion.18 = (f32[1024]{0:T(1024)S(1)}, f32[512]{0:T(512)S(1)}, f32[512,1024]{1,0:T(8,128)}) fusion(bf16[512,1024]{1,0:T(8,128)(2,1)S(1)} %copy-done.48, f32[512]{0:T(512)S(1)} %copy-done.69, f32[1024]{0:T(1024)S(1)} %bitcast.123, f32[512,1024]{1,0:T(8,128)S(1)} %fusion.72, bf16[512,3072]{1,0:T(8,128)(2,1)S(1)} %copy-done.74, ...), kind=kOutput, calls=%fused_computation.34 | convolution fusion | flops 3225418240 | bytes 14692352 | tf_op jit(solution)/shard_map/dot_general | solution.py:659
  340.8 3.8 fusion.17
  352.7 56.6 %reduce-scatter.5.cloned.1.call-done.part_ref = bf16[64,4096]{1,0:T(8,128)(2,1)} async-done(((bf16[512,4096]{1,0:T(8,128)(2,1)}), bf16[64,4096]{1,0:T(8,128)(2,1)}) %reduce-scatter.5.cloned.1.call-update) | async-done | bytes 524304 | tf_op jit(solution)/shard_map/reduce_scatter | solution.py:1572
  410.3 23.2 %shard_map.331 = (f32[2,64,4096]{2,1,0:T(8,128)S(1)}, f32[24,128]{1,0:T(8,128)S(1)}, bf16[8,2,64,1024]{3,2,1,0:T(8,128)(2,1)}, bf16[8,2,64,2816]{3,2,1,0:T(8,128)(2,1)}) custom-call(bf16[64,4096]{1,0:T(8,128)(2,1)S(1)} %copy-done.23, f32[64,4096]{1,0:T(8,128)S(1)} %pad_maximum_fusion.3.prior_ref, f32[8,24,128]{2,1,0:T(8,128)S(1)} %bitcast.99, ...), custom_call_target="tpu_custom_call" | custom-call | tf_op jit(solution)/shard_map/pallas_call | solution.py:975
  437.1 114.0 %shard_map.332 = (bf16[3,2,64,2816]{3,2,1,0:T(8,128)(2,1)}, bf16[4,2,64,1024]{3,2,1,0:T(8,128)(2,1)}) custom-call(bf16[8,64,2816]{2,1,0:T(8,128)(2,1)S(1)} %get-tuple-element.320.wide_ref, bf16[8,64,1024]{2,1,0:T(8,128)(2,1)} %get-tuple-element.321.square_ref), custom_call_target="tpu_custom_call" | custom-call | tf_op jit(solution)/shard_map/pallas_call | solution.py:1017
  551.1 9.0 %shard_map.333 = (f32[3,128,1024]{2,1,0:T(8,128)}, f32[3,128,1024]{2,1,0:T(8,128)}, f32[128,8]{1,0:T(8,128)}, f32[128,8]{1,0:T(8,128)}, f32[3,4,128]{2,1,0:T(4,1...) custom-call(bf16[3,128,2816]{2,1,0:T(8,128)(2,1)} %bitcast.107, ...), custom_call_target="tpu_custom_call" | custom-call | tf_op jit(solution)/shard_map/pallas_call | solution.py:1164
  (298 shorter events, 138.6 us)
Async XLA Ops:
  7.2 144.1 %all-gather.2.cloned.1.call-start = ((), (), s32[]{:S(2)}) async-start(), calls=%async_computation.2 | async-start | bytes 5308416 | tf_op jit(solution)/shard_map/all_gather | solution.py:1434
  7.2 66.0 %collective-permute-start = (bf16[512,1024]{1,0:T(8,128)(2,1)}, bf16[512,1024]{1,0:T(8,128)(2,1)S(1)}, u32[]{:S(2)}, u32[]{:S(2)}) collective-permute-start(bf16[512,1024]{1,0:T(8,128)(2,1)} %param.24), channel_id=1, source_target_pairs={{0,8},{8,0},{16,24},{24,16},{1,9},{9,1},{17,25},{25,17},{2,10},{10... | collective-permute-start | bytes 3145736 | tf_op jit(solution)/shard_map/ppermute | solution.py:630
  8.0 65.3 %collective-permute-start.1 = (bf16[512,1024]{1,0:T(8,128)(2,1)}, bf16[512,1024]{1,0:T(8,128)(2,1)}, u32[]{:S(2)}, u32[]{:S(2)}) collective-permute-start(bf16[512,1024]{1,0:T(8,128)(2,1)} %param.24), channel_id=1, source_target_pairs={{0,16},{8,24},{16,0},{24,8},{1,17},{9,25},{17,1},{25,9},{2,18},{10... | collective-permute-start | bytes 3145736 | tf_op jit(solution)/shard_map/ppermute | solution.py:635
  19.3 56.3 %copy-start.46 = (bf16[512,1024]{1,0:T(8,128)(2,1)S(1)}, bf16[512,1024]{1,0:T(8,128)(2,1)}, u32[]{:S(2)}) copy-start(bf16[512,1024]{1,0:T(8,128)(2,1)} %param.23) | copy-start | bytes 3145732
  73.3 247.5 %reduce-scatter.3.cloned.1.call-start = ((), (), s32[]{:S(2)}) async-start(), calls=%async_computation.3 | async-start | bytes 5308416 | tf_op jit(solution)/shard_map/reduce_scatter | solution.py:1524
  88.0 3.2 collective-permute-start.2
  91.2 41.1 %copy-start.31 = (f32[1,128]{1,0:T(1,128)S(1)}, f32[1,128]{1,0:T(1,128)}, u32[]{:S(2)}) copy-start(f32[1,128]{1,0:T(1,128)} %reshape.296.gain_ref) | copy-start | bytes 1540
  142.2 3.0 collective-permute-start.4
  143.0 29.1 %collective-permute-start.7 = (bf16[512,1024]{1,0:T(8,128)(2,1)}, bf16[512,1024]{1,0:T(8,128)(2,1)}, u32[]{:S(2)}, u32[]{:S(2)}) collective-permute-start(bf16[512,1024]{1,0:T(8,128)(2,1)} %collective-permute-done.1), channel_id=1, source_target_pairs={{0,8},{8,0},{16,24},{24,16},{1,9},{9,1},{17,25},{25,17},{2,10},{10... | collective-permute-start | bytes 3145736 | tf_op jit(solution)/shard_map/ppermute | solution.py:630
  145.0 24.9 %collective-permute-start.3 = (bf16[512,1024]{1,0:T(8,128)(2,1)}, bf16[512,1024]{1,0:T(8,128)(2,1)}, u32[]{:S(2)}, u32[]{:S(2)}) collective-permute-start(bf16[512,1024]{1,0:T(8,128)(2,1)} %multiply_convert_fusion.6), channel_id=1, source_target_pairs={{0,16},{8,24},{16,0},{24,8},{1,17},{9,25},{17,1},{25,9},{2,18},{10... | collective-permute-start | bytes 3145736 | tf_op jit(solution)/shard_map/ppermute | solution.py:635
  169.9 8.9 %collective-permute-start.6 = (bf16[512,1024]{1,0:T(8,128)(2,1)}, bf16[512,1024]{1,0:T(8,128)(2,1)S(1)}, u32[]{:S(2)}, u32[]{:S(2)}) collective-permute-start(bf16[512,1024]{1,0:T(8,128)(2,1)} %collective-permute-done.3), channel_id=1, source_target_pairs={{0,8},{8,0},{16,24},{24,16},{1,9},{9,1},{17,25},{25,17},{2,10},{10... | collective-permute-start | bytes 3145736 | tf_op jit(solution)/shard_map/ppermute | solution.py:630
  190.4 2.7 collective-permute-start.8
  191.6 24.0 %collective-permute-start.10 = (bf16[512,1024]{1,0:T(8,128)(2,1)}, bf16[512,1024]{1,0:T(8,128)(2,1)}, u32[]{:S(2)}, u32[]{:S(2)}) collective-permute-start(bf16[512,1024]{1,0:T(8,128)(2,1)} %slice.202), channel_id=1, source_target_pairs={{0,8},{8,0},{16,24},{24,16},{1,9},{9,1},{17,25},{25,17},{2,10},{10... | collective-permute-start | bytes 3145736 | tf_op jit(solution)/shard_map/ppermute | solution.py:630
  200.2 19.2 %collective-permute-start.9 = (bf16[512,1024]{1,0:T(8,128)(2,1)}, bf16[512,1024]{1,0:T(8,128)(2,1)}, u32[]{:S(2)}, u32[]{:S(2)}) collective-permute-start(bf16[512,1024]{1,0:T(8,128)(2,1)} %slice.203), channel_id=1, source_target_pairs={{0,8},{8,0},{16,24},{24,16},{1,9},{9,1},{17,25},{25,17},{2,10},{10... | collective-permute-start | bytes 3145736 | tf_op jit(solution)/shard_map/ppermute | solution.py:630
  212.8 196.5 %reduce-scatter.5.cloned.1.call-start = ((), (), s32[]{:S(2)}) async-start(), calls=%async_computation.4 | async-start | bytes 4718592 | tf_op jit(solution)/shard_map/reduce_scatter | solution.py:1572
  212.9 24.8 %collective-permute-start.11 = (bf16[512,1024]{1,0:T(8,128)(2,1)}, bf16[512,1024]{1,0:T(8,128)(2,1)S(1)}, u32[]{:S(2)}, u32[]{:S(2)}) collective-permute-start(bf16[512,1024]{1,0:T(8,128)(2,1)} %add_convert_fusion.5), channel_id=1, source_target_pairs={{0,16},{8,24},{16,0},{24,8},{1,17},{9,25},{17,1},{25,9},{2,18},{10... | collective-permute-start | bytes 3145736 | tf_op jit(solution)/shard_map/ppermute | solution.py:635
  214.9 22.8 %collective-permute-start.5 = (bf16[512,1024]{1,0:T(8,128)(2,1)S(1)}, bf16[512,1024]{1,0:T(8,128)(2,1)S(1)}, u32[]{:S(2)}, u32[]{:S(2)}) collective-permute-start(bf16[512,1024]{1,0:T(8,128)(2,1)S(1)} %slice.204), channel_id=1, source_target_pairs={{0,8},{8,0},{16,24},{24,16},{1,9},{9,1},{17,25},{25,17},{2,10},{10... | collective-permute-start | bytes 3145736 | tf_op jit(solution)/shard_map/ppermute | solution.py:630
  257.0 38.8 %collective-permute-start.12 = (bf16[512,1024]{1,0:T(8,128)(2,1)}, bf16[512,1024]{1,0:T(8,128)(2,1)}, u32[]{:S(2)}, u32[]{:S(2)}) collective-permute-start(bf16[512,1024]{1,0:T(8,128)(2,1)} %fusion.20), channel_id=1, source_target_pairs={{0,16},{8,24},{16,0},{24,8},{1,17},{9,25},{17,1},{25,9},{2,18},{10... | collective-permute-start | bytes 3145736 | tf_op jit(solution)/shard_map/ppermute | solution.py:635
  295.8 3.2 collective-permute-start.13
  305.1 8.4 %collective-permute-start.14 = (bf16[512,3072]{1,0:T(8,128)(2,1)}, bf16[512,3072]{1,0:T(8,128)(2,1)}, u32[]{:S(2)}, u32[]{:S(2)}) collective-permute-start(bf16[512,3072]{1,0:T(8,128)(2,1)} %convolution_convert_fusion), channel_id=1, source_target_pairs={{0,8},{8,0},{16,24},{24,16},{1,9},{9,1},{17,25},{25,17},{2,10},{10... | collective-permute-start | bytes 9437192 | tf_op jit(solution)/shard_map/ppermute | solution.py:630
  309.0 3.8 collective-permute-start.15
  328.9 17.9 %collective-permute-start.16 = (bf16[128,2304]{1,0:T(8,128)(2,1)}, bf16[128,2304]{1,0:T(8,128)(2,1)}, u32[]{:S(2)}, u32[]{:S(2)}) collective-permute-start(bf16[128,2304]{1,0:T(8,128)(2,1)} %reduce-scatter.3.cloned.1.call-done), channel_id=1, source_target_pairs={{0,8},{8,0},{16,24},{24,16},{1,9},{9,1},{17,25},{25,17},{2,10},{10... | collective-permute-start | bytes 1769480 | tf_op jit(solution)/shard_map/ppermute | solution.py:630
  329.3 16.7 %collective-permute-start.17 = (bf16[128,2304]{1,0:T(8,128)(2,1)}, bf16[128,2304]{1,0:T(8,128)(2,1)}, u32[]{:S(2)}, u32[]{:S(2)}) collective-permute-start(bf16[128,2304]{1,0:T(8,128)(2,1)} %reduce-scatter.3.cloned.1.call-done), channel_id=1, source_target_pairs={{0,16},{8,24},{16,0},{24,8},{1,17},{9,25},{17,1},{25,9},{2,18},{10... | collective-permute-start | bytes 1769480 | tf_op jit(solution)/shard_map/ppermute | solution.py:635
  346.1 3.0 collective-permute-start.18
  (73 other events, 480.1 us)
Sparse Core Ops, SparseCore 0:
  73.5 77.7 all-gather.1
  213.0 94.9 reduce-scatter.2
  321.0 88.3 reduce-scatter.4

commit v2 on v1

--- a/solution.py
+++ b/solution.py
@@ -659,7 +659,8 @@
     return lax.dot_general(left, right, (((dims[0],), (dims[1],)), ((), ())), preferred_element_type=FULL)
 
 
-def exchange_kernel(backward, seq_count, local_ref, transfer_ref, result_ref, other_local, other_transfer, chip_ref, sent_ref,
+def exchange_kernel(backward, seq_count, local_ref, transfer_ref, result_ref, local_low, transfer_low, other_local,
+                    other_transfer, chip_ref, sent_ref,
                     swap_send, swap_recv, chip_send, chip_recv, half_send, half_recv):
     seq, mine = lax.axis_index("seq"), lax.axis_index("fsdp")
     core, chip = lax.rem(seq, 2), lax.div(seq, 2)
@@ -672,7 +673,9 @@
     step = -1 if backward else 1
 
     for head in range(heads):
-        chip_ref[head] = jnp.zeros((HD, HD), FULL)
+        chip_ref[head] = jnp.zeros((HD, HD), LOW)
+        local_low[head] = local_ref[head].astype(LOW)
+        transfer_low[head] = transfer_ref[head].astype(LOW)
     barrier = pltpu.get_barrier_semaphore()
     pl.semaphore_signal(barrier, inc=1, device_id=(partner, mine), device_id_type=mesh_id)
     for k in range(1, chips):
@@ -685,7 +688,7 @@
             src_ref=source, dst_ref=target, send_sem=swap_send.at[i], recv_sem=swap_recv.at[i],
             device_id=(partner, mine), device_id_type=mesh_id,
         )
-        for i, (source, target) in enumerate(((local_ref, other_local), (transfer_ref, other_transfer)))
+        for i, (source, target) in enumerate(((local_low, other_local), (transfer_low, other_transfer)))
     ]
     for swap in swaps:
         swap.start()
@@ -694,7 +697,17 @@
     share = pl.ds(pl.multiple_of(core * (heads // 2), heads // 2), heads // 2)
 
     def applied(matrix, value):
-        return product(halves(matrix), halves(value), dims)
+        return product(matrix, value.astype(LOW), dims)
+
+    def by_role(head):
+        own_local, own_transfer = local_ref[head], transfer_low[head]
+        far_local, far_transfer = other_local[head].astype(FULL), other_transfer[head]
+        return (
+            jnp.where(lead, own_local, far_local),
+            jnp.where(lead, own_transfer, far_transfer),
+            jnp.where(lead, far_local, own_local),
+            jnp.where(lead, far_transfer, own_transfer),
+        )
 
     for i in range(chips - 1):
         source = chips - 1 - i if backward else i
@@ -702,12 +715,9 @@
         @pl.when(chip == source)
         def _():
             for head in range(heads):
-                lead_local = jnp.where(lead, local_ref[head], other_local[head])
-                trail_local = jnp.where(lead, other_local[head], local_ref[head])
-                lead_transfer = jnp.where(lead, transfer_ref[head], other_transfer[head])
-                trail_transfer = jnp.where(lead, other_transfer[head], transfer_ref[head])
+                lead_local, lead_transfer, trail_local, trail_transfer = by_role(head)
                 inner = lead_local if i == 0 else lead_local + applied(lead_transfer, chip_ref[head])
-                sent_ref[head] = trail_local + applied(trail_transfer, inner)
+                sent_ref[head] = (trail_local + applied(trail_transfer, inner)).astype(LOW)
 
         onward = pltpu.make_async_remote_copy(
             src_ref=sent_ref.at[share], dst_ref=chip_ref.at[share], send_sem=chip_send.at[i], recv_sem=chip_recv.at[i],
@@ -730,10 +740,9 @@
             half.wait()
 
     for head in range(heads):
-        lead_local = jnp.where(lead, local_ref[head], other_local[head])
-        lead_transfer = jnp.where(lead, transfer_ref[head], other_transfer[head])
+        lead_local, lead_transfer, _, _ = by_role(head)
         state = chip_ref[head]
-        result_ref[head] = jnp.where(lead, state, lead_local + applied(lead_transfer, state))
+        result_ref[head] = jnp.where(lead, state.astype(FULL), lead_local + applied(lead_transfer, state))
 
 
 def exchanged(local, transfer, backward, call_id):
@@ -746,7 +755,7 @@
         in_specs=[vmem, vmem],
         out_specs=vmem,
         out_shape=jax.ShapeDtypeStruct(local.shape, FULL),
-        scratch_shapes=[pltpu.VMEM(local.shape, FULL)] * 4 + [dma((2,))] * 2 + [dma((hops,))] * 4,
+        scratch_shapes=[pltpu.VMEM(local.shape, LOW)] * 6 + [dma((2,))] * 2 + [dma((hops,))] * 4,
         compiler_params=pltpu.CompilerParams(collective_id=call_id, has_side_effects=True, vmem_limit_bytes=24 << 20),
     )(local, transfer)
 
@@ -1219,7 +1228,7 @@
     row_loop(size, scaled)
     level = 1.0
     gathered_low, spare_low = first_low, second_low
-    for sweep in range(NS_STEPS):
+    for sweep in range(NS_STEPS - 1):
         keep_ref = gathered_ref if sweep == 0 else mapped_ref
 
         def mapping(at):
@@ -1246,22 +1255,33 @@
             row_loop(size, gather)
             gathered_low, spare_low = spare_low, gathered_low
         level = level * coef_linear
-        if sweep < NS_STEPS - 1:
-            def middle(at):
-                value = coef_linear * square_ref[at, :] + product(mapped_low[at, :], square_low[...])
-                middle_ref[at, :] = value
-                spare_low[at, :] = value.astype(LOW)
-
-            row_loop(size, middle)
-
-            def squared(at):
-                value = coef_linear * middle_ref[at, :] + product(spare_low[at, :], mapped_low[...])
-                square_ref[at, :] = value
-                square_low[at, :] = value.astype(LOW)
-
-            row_loop(size, squared)
-    pick_rows(count, half, gathered_low, rows_low)
+
+        def middle(at):
+            value = coef_linear * square_ref[at, :] + product(mapped_low[at, :], square_low[...])
+            middle_ref[at, :] = value
+            spare_low[at, :] = value.astype(LOW)
+
+        row_loop(size, middle)
+
+        def squared(at):
+            value = coef_linear * middle_ref[at, :] + product(spare_low[at, :], mapped_low[...])
+            square_ref[at, :] = value
+            square_low[at, :] = value.astype(LOW)
+
+        row_loop(size, squared)
+
+    pick_rows(count, half, square_low, rows_low)
+    pick_rows(count, half, square_ref, mapped_ref)
+    pick_rows(count, half, gathered_ref, middle_ref)
     pick_rows(count, half, whole_ref, rows_own)
+
+    def last(at):
+        mapped = coef_cubic * mapped_ref[at, :] + coef_quintic * product(rows_low[at, :], square_low[...])
+        value = coef_linear * middle_ref[at, :] + level * mapped + product(mapped.astype(LOW), gathered_low[...])
+        rows_low[at, :] = value.astype(LOW)
+
+    row_loop(size // 2, last)
+    level = level * coef_linear
 
     @pl.loop(0, whole_ref.shape[1] // TILE)
     def _(i):
@@ -1497,13 +1517,11 @@
 
     near_top, far_top = jnp.concatenate(top_parts[:2]), jnp.concatenate(top_parts[2:])
     near = spread_out(near_norm, near_top)
+    far_straight, near = lax.optimization_barrier((far_straight, near))
+    far_parts = [part for one in far_straight for part in (one, core_swapped(one))]
     near_grad = grad_in(near)
-    far_straight, near, near_grad = lax.optimization_barrier((far_straight, near, near_grad))
-    far_parts = [part for one in far_straight for part in (one, core_swapped(one))]
     near_back = core_swapped(near_grad[row_count:].astype(LOW))
-    near_out = low_dot(near[0], down_full, (1, 1))
-    near_weights = [weight_grad(near, near_norm, near_top, 0)]
-    near_weights, near_out, far_parts = lax.optimization_barrier((near_weights, near_out, far_parts))
+    near_grad, far_parts = lax.optimization_barrier((near_grad, far_parts))
     far_norm = jnp.concatenate(far_parts)
     far = spread_out(far_norm, far_top)
 
@@ -1518,15 +1536,11 @@
     joint = [(grad_in(one) + other.astype(FULL)).astype(LOW) for one, other in zip(picked(far, 0), crossed)]
     far, near, joint = lax.optimization_barrier((far, near, joint))
     grad_parts = [chip_shifted(one, -(k + 1)) for k, one in enumerate(joint)]
-    near_weights = list(near_weights) + [weight_grad(near, near_norm, near_top, j) for j in (1, 2)]
+    near_weights = [weight_grad(near, near_norm, near_top, j) for j in range(3)]
     far_weights = [weight_grad(far, far_norm, far_top, j) for j in range(3)]
     ff_grads = jnp.concatenate([(a + b).astype(LOW) for a, b in zip(near_weights, far_weights)], axis=1)
     ff_part = lax.psum_scatter(ff_grads, "fsdp", scatter_dimension=0, tiled=True)
-    far_out = low_dot(far[0], down_full, (1, 1))
-    out_crossed = [core_swapped(one[0].astype(LOW)) for one in picked((far_out,), 1)]
-    out_joint = [(one[0] + other.astype(FULL)).astype(LOW) for one, other in zip(picked((far_out,), 0), out_crossed)]
-    out_near = near_out[:row_count] + core_swapped(near_out[row_count:].astype(LOW)).astype(FULL)
-    done_grads, out_joint, out_near, grad_parts = lax.optimization_barrier((ff_grads, out_joint, out_near, grad_parts))
+    done_grads, grad_parts = lax.optimization_barrier((ff_grads, grad_parts))
     grad_normed_two = near_grad[:row_count] + sum(one.astype(FULL) for one in [near_back] + list(grad_parts))
     back_two, grad_gain_two = norm_back(unit_two, scale_two, gains_wide[1], grad_normed_two)
     grad_residual = back_two + cotangent.astype(FULL)
@@ -1537,13 +1551,10 @@
         grad_head_normed, delta_out, effective, head_gain_full
     )
     leave = exchanged(adjoint_local, transfer, True, 5)
-    leave, out_joint = lax.optimization_barrier((leave, out_joint))
-    out_parts = [chip_shifted(one, -(k + 1)) for k, one in enumerate(out_joint)]
     grad_projected, grad_strength, grad_filter, edge, lead = backward_blocks(
         projected, rim, filters_wide, strength, meta, meta_row, mixed, solve, weight, update, drift,
         upstream, states, enter, leave,
     )
-    lead, out_parts = lax.optimization_barrier((lead, out_parts))
     back = [(i + 1, i) for i in range(seq_count - 1)]
     incoming = lax.ppermute(lead.astype(LOW), "seq", back).astype(FULL)
     grad_projected = lax.dynamic_update_slice(
@@ -1566,9 +1577,15 @@
         ],
         axis=1,
     )
-    square_grads, ff_part, grad_projected, grad_logits = lax.optimization_barrier(
-        (square_grads, ff_part, grad_projected, grad_logits)
-    )
+    near_hidden, far_hidden = near[0], far[0]
+    square_grads, ff_part, grad_projected, grad_logits, near_hidden, far_hidden = lax.optimization_barrier(
+        (square_grads, ff_part, grad_projected, grad_logits, near_hidden, far_hidden)
+    )
+    far_out, near_out = low_dot(far_hidden, down_full, (1, 1)), low_dot(near_hidden, down_full, (1, 1))
+    out_crossed = [core_swapped(one[0].astype(LOW)) for one in picked((far_out,), 1)]
+    out_joint = [(one[0] + other.astype(FULL)).astype(LOW) for one, other in zip(picked((far_out,), 0), out_crossed)]
+    out_parts = [chip_shifted(one, -(k + 1)) for k, one in enumerate(out_joint)]
+    out_near = near_out[:row_count] + core_swapped(near_out[row_count:].astype(LOW)).astype(FULL)
     square_part = lax.psum_scatter(square_grads, "fsdp", scatter_dimension=0, tiled=True)
     grad_strength_weight = low_dot(grad_logits, normed_low, (0, 0))
     grad_normed = low_dot(grad_logits, strength_full, (1, 0)) + low_dot(grad_projected, mixer_full, (1, 1))

time: 578 us -> 568 us (0.983)
  Pallas kernels: 290 us -> 279 us
    reduce_scatter x1, waiting for transfers between devices: 56.6 us -> 25.1 us  [on_device(): lax.psum_scatter(square_grads, 'fsdp', scatter_dimension=0, tiled=True)]
    ppermute x5, waiting for transfers between devices: 16.9 us -> 45.1 us  [chip_shifted(): lax.ppermute(value, 'seq', [(i, (i + 2 * by) % count) for i in range(coun...]
    pallas_call x2, Pallas kernels: 26.5 us -> 18.2 us  [exchanged(): pl.pallas_call(partial(exchange_kernel, backward, seq_count), in_specs=[v...]
    unnamed x158 -> x164, local copies, waits for them, and re-layouts: 34.8 us -> 35.7 us
  transfers between devices with their start and end apart: 22 -> 22, of which waited for: 7 -> 9; matrix products, arithmetic and copies ran while one was open for 22% -> 19% of each run, Pallas kernels for 25% -> 24%
where the time goes in v2:
time: 568 us; the launch traced here: 559 us
  Pallas kernels  279 us (49%)
  matrix products  85.1 us (15%)
  waiting for transfers between devices  84.6 us (15%)
  local copies, waits for them, and re-layouts  54.1 us (10%)
  other arithmetic  25.8 us (5%)
  starting transfers between devices  15.9 us (3%)
  between operations  15.3 us (3%)
    pallas_call x1, Pallas kernels, handed_back(): pl.pallas_call(partial(hand_back_kernel, owners, seq_count, count), in_sp...  111 us
    dot_general x31, matrix products, low_dot(): lax.dot_general(left, right, (((dims[0],), (dims[1],)), ((), ())), prefer...  85.1 us
    pallas_call x1, Pallas kernels, gathered_mixer(): pl.pallas_call(partial(gather_kernel, along, across, seq_count), in_specs...  54 us
    ppermute x5, waiting for transfers between devices, chip_shifted(): lax.ppermute(value, 'seq', [(i, (i + 2 * by) % count) for i in range(coun...  45.1 us
    unnamed x164, local copies, waits for them, and re-layouts  35.7 us
    pallas_call x1, Pallas kernels, backward_blocks(): pl.pallas_call(backward_kernel, grid=(groups, steps), in_specs=[flat, pl....  28.9 us
    reduce_scatter x1, waiting for transfers between devices, on_device(): lax.psum_scatter(square_grads, 'fsdp', scatter_dimension=0, tiled=True)  25.1 us
    pallas_call x1, Pallas kernels, forward_blocks(): pl.pallas_call(forward_kernel, grid=(groups, steps), in_specs=[pl.BlockSp...  24.7 us
  transfers between devices with their start and end apart: 22, of which 9 were waited for; matrix products, arithmetic and copies ran while one was open for 19% of the time, Pallas kernels for 24%

profile of v2, /device:TPU:31, one launch (start us, length us, event | category | flops | bytes accessed | tf_op | source)
XLA Modules:
  0.0 559.4 jit_solution(226743058896515007)
XLA Ops:
  19.3 54.0 %shard_map.323 = (bf16[1024,4096]{1,0:T(8,128)(2,1)}, bf16[32,1024]{1,0:T(8,128)(2,1)}) custom-call(bf16[128,4096]{1,0:T(8,128)(2,1)} %copy-done.14, bf16[32,128]{1,0:T(8,128)(2,1)} %copy-done.28), custom_call_target="tpu_custom_call" | custom-call | tf_op jit(solution)/shard_map/pallas_call | solution.py:605
  79.7 6.6 %fusion.4.proj_ref.prev_ref = bf16[512,3072]{1,0:T(8,128)(2,1)S(1)} fusion(bf16[512,1024]{1,0:T(8,128)(2,1)S(1)} %fusion.13, bf16[1024,4096]{1,0:T(8,128)(2,1)} %get-tuple-element.110), kind=kOutput, calls=%fused_computation.6 | convolution fusion | flops 3222798336 | bytes 10485760 | tf_op jit(solution)/shard_map/dot_general | solution.py:659
  91.4 24.7 %shard_map.324 = (bf16[3,512,1024]{2,1,0:T(8,128)(2,1)}, bf16[4,8,128,128]{3,2,1,0:T(8,128)(2,1)S(1)}, bf16[512,1024]{1,0:T(8,128)(2,1)S(1)}, f32[512,1024]{1,0:...) custom-call(bf16[512,3072]{1,0:T(8,128)(2,1)} %copy-done.40, ...), custom_call_target="tpu_custom_call" | custom-call | flops 8589934592 | bytes 25165824 | tf_op jit(solution)/shard_map/pallas_call | solution.py:204
  116.1 11.9 %shard_map.325.state_ref.enter_ref = f32[8,128,128]{2,1,0:T(8,128)S(1)} custom-call(f32[8,128,128]{2,1,0:T(8,128)S(1)} %get-tuple-element.118.local_ref, f32[8,128,128]{2,1,0:T(8,128)S(1)} %get-tuple-element.119.transfer_ref), custom_call_target="tpu_custom_call" | custom-call | tf_op jit(solution)/shard_map/pallas_call | solution.py:753
  143.6 7.7 %all-gather.2.cloned.1.call-done = bf16[1024,2304]{1,0:T(8,128)(2,1)} async-done(((bf16[128,2304]{1,0:T(8,128)(2,1)}), bf16[1024,2304]{1,0:T(8,128)(2,1)}) %all-gather.2.cloned.1.call-update) | async-done | bytes 4718608 | tf_op jit(solution)/shard_map/all_gather | solution.py:1454
  151.2 4.0 fusion.54
  162.4 6.1 %collective-permute-done.3 = bf16[512,1024]{1,0:T(8,128)(2,1)} collective-permute-done((bf16[512,1024]{1,0:T(8,128)(2,1)}, bf16[512,1024]{1,0:T(8,128)(2,1)}, u32[]{:S(2)}, u32[]{:S(2)}) %collective-permute-start.3) | collective-permute-done | bytes 1048608 | tf_op jit(solution)/shard_map/ppermute | solution.py:635
  172.6 3.9 convolution_add_fusion
  181.5 4.0 multiply_convert_fusion
  215.1 19.5 %collective-permute-done.9 = bf16[512,1024]{1,0:T(8,128)(2,1)} collective-permute-done((bf16[512,1024]{1,0:T(8,128)(2,1)}, bf16[512,1024]{1,0:T(8,128)(2,1)}, u32[]{:S(2)}, u32[]{:S(2)}) %collective-permute-start.9) | collective-permute-done | bytes 1048608 | tf_op jit(solution)/shard_map/ppermute | solution.py:635
  234.6 4.4 multiply_reduce_fusion
  249.5 6.3 %shard_map.328.leave_ref = f32[8,128,128]{2,1,0:T(8,128)S(1)} custom-call(f32[8,128,128]{2,1,0:T(8,128)S(1)} %get-tuple-element.142.local_ref, f32[8,128,128]{2,1,0:T(8,128)S(1)} %get-tuple-element.119.transfer_ref), custom_call_target="tpu_custom_call" | custom-call | tf_op jit(solution)/shard_map/pallas_call | solution.py:753
  255.9 28.9 %shard_map.329 = (bf16[512,3072]{1,0:T(8,128)(2,1)}, f32[1,512,8]{2,1,0:T(8,128)S(1)}, f32[3,4,1024]{2,1,0:T(4,128)S(1)}, f32[8,3072]{1,0:T(8,128)S(1)}, f32[8,3072]{1,0:T(8,128)S(1)}) custom-call(bf16[512,3072]{1,0:T(8,128)(2,1)} %copy-done.40, bf16[512,3072]{1,0:T(8,128)(2,1)} %copy-done.40, bf16[16,3072]{1,0:T(8,128)(2,1)S(1)} %collective-permute-done.2.rim_ref, ...), custom_call_target="tpu_custom_call" | custom-call | flops 4294967296 | bytes 25165824 | tf_op jit(solution)/shard_map/pallas_call | solution.py:465
  289.0 5.5 convolution_convert_fusion
  294.5 4.3 collective-permute-start.11
  319.9 3.9 fusion.40
  326.3 4.1 fusion.42
  334.8 5.0 fusion.18
  350.5 3.8 shard_map.330
  354.3 19.4 %collective-permute-done.18 = bf16[512,1024]{1,0:T(8,128)(2,1)S(1)} collective-permute-done((bf16[512,1024]{1,0:T(8,128)(2,1)S(1)}, bf16[512,1024]{1,0:T(8,128)(2,1)S(1)}, u32[]{:S(2)}, u32[]{:S(2)}) %collective-permute-start.18) | collective-permute-done | bytes 1048608 | tf_op jit(solution)/shard_map/ppermute | solution.py:635
  377.1 25.1 %reduce-scatter.5.cloned.1.call-done.part_ref = bf16[64,4096]{1,0:T(8,128)(2,1)} async-done(((bf16[512,4096]{1,0:T(8,128)(2,1)}), bf16[64,4096]{1,0:T(8,128)(2,1)}) %reduce-scatter.5.cloned.1.call-update) | async-done | bytes 524304 | tf_op jit(solution)/shard_map/reduce_scatter | solution.py:1589
  403.2 23.2 %shard_map.331 = (f32[2,64,4096]{2,1,0:T(8,128)S(1)}, f32[24,128]{1,0:T(8,128)S(1)}, bf16[8,2,64,1024]{3,2,1,0:T(8,128)(2,1)}, bf16[8,2,64,2816]{3,2,1,0:T(8,128)(2,1)}) custom-call(bf16[64,4096]{1,0:T(8,128)(2,1)S(1)} %copy-done.23, f32[64,4096]{1,0:T(8,128)S(1)} %pad_maximum_fusion.3.prior_ref, f32[8,24,128]{2,1,0:T(8,128)S(1)} %bitcast.99, ...), custom_call_target="tpu_custom_call" | custom-call | tf_op jit(solution)/shard_map/pallas_call | solution.py:984
  429.8 110.9 %shard_map.332 = (bf16[3,2,64,2816]{3,2,1,0:T(8,128)(2,1)}, bf16[4,2,64,1024]{3,2,1,0:T(8,128)(2,1)}) custom-call(bf16[8,64,2816]{2,1,0:T(8,128)(2,1)S(1)} %get-tuple-element.310.wide_ref, bf16[8,64,1024]{2,1,0:T(8,128)(2,1)} %get-tuple-element.311.square_ref), custom_call_target="tpu_custom_call" | custom-call | tf_op jit(solution)/shard_map/pallas_call | solution.py:1026
  540.7 9.0 %shard_map.333 = (f32[3,128,1024]{2,1,0:T(8,128)}, f32[3,128,1024]{2,1,0:T(8,128)}, f32[128,8]{1,0:T(8,128)}, f32[128,8]{1,0:T(8,128)}, f32[3,4,128]{2,1,0:T(4,1...) custom-call(bf16[3,128,2816]{2,1,0:T(8,128)(2,1)} %bitcast.107, ...), custom_call_target="tpu_custom_call" | custom-call | tf_op jit(solution)/shard_map/pallas_call | solution.py:1173
  (303 shorter events, 149.3 us)
Async XLA Ops:
  7.2 144.1 %all-gather.2.cloned.1.call-start = ((), (), s32[]{:S(2)}) async-start(), calls=%async_computation.2 | async-start | bytes 5308416 | tf_op jit(solution)/shard_map/all_gather | solution.py:1454
  7.2 66.0 %collective-permute-start = (bf16[512,1024]{1,0:T(8,128)(2,1)}, bf16[512,1024]{1,0:T(8,128)(2,1)S(1)}, u32[]{:S(2)}, u32[]{:S(2)}) collective-permute-start(bf16[512,1024]{1,0:T(8,128)(2,1)} %param.24), channel_id=1, source_target_pairs={{0,8},{8,0},{16,24},{24,16},{1,9},{9,1},{17,25},{25,17},{2,10},{10... | collective-permute-start | bytes 3145736 | tf_op jit(solution)/shard_map/ppermute | solution.py:630
  8.0 65.3 %collective-permute-start.1 = (bf16[512,1024]{1,0:T(8,128)(2,1)}, bf16[512,1024]{1,0:T(8,128)(2,1)}, u32[]{:S(2)}, u32[]{:S(2)}) collective-permute-start(bf16[512,1024]{1,0:T(8,128)(2,1)} %param.24), channel_id=1, source_target_pairs={{0,16},{8,24},{16,0},{24,8},{1,17},{9,25},{17,1},{25,9},{2,18},{10... | collective-permute-start | bytes 3145736 | tf_op jit(solution)/shard_map/ppermute | solution.py:635
  19.3 56.3 %copy-start.43 = (bf16[512,1024]{1,0:T(8,128)(2,1)S(1)}, bf16[512,1024]{1,0:T(8,128)(2,1)}, u32[]{:S(2)}) copy-start(bf16[512,1024]{1,0:T(8,128)(2,1)} %param.23) | copy-start | bytes 3145732
  73.3 240.2 %reduce-scatter.3.cloned.1.call-start = ((), (), s32[]{:S(2)}) async-start(), calls=%async_computation.3 | async-start | bytes 5308416 | tf_op jit(solution)/shard_map/reduce_scatter | solution.py:1542
  88.2 3.2 collective-permute-start.2
  91.4 36.6 %copy-start.29 = (f32[1,128]{1,0:T(1,128)S(1)}, f32[1,128]{1,0:T(1,128)}, u32[]{:S(2)}) copy-start(f32[1,128]{1,0:T(1,128)} %reshape.296.gain_ref) | copy-start | bytes 1540
  139.3 4.3 collective-permute-start.4
  139.5 30.0 %collective-permute-start.7 = (bf16[512,1024]{1,0:T(8,128)(2,1)}, bf16[512,1024]{1,0:T(8,128)(2,1)}, u32[]{:S(2)}, u32[]{:S(2)}) collective-permute-start(bf16[512,1024]{1,0:T(8,128)(2,1)} %collective-permute-done.1), channel_id=1, source_target_pairs={{0,8},{8,0},{16,24},{24,16},{1,9},{9,1},{17,25},{25,17},{2,10},{10... | collective-permute-start | bytes 3145736 | tf_op jit(solution)/shard_map/ppermute | solution.py:630
  143.6 24.9 %collective-permute-start.3 = (bf16[512,1024]{1,0:T(8,128)(2,1)}, bf16[512,1024]{1,0:T(8,128)(2,1)}, u32[]{:S(2)}, u32[]{:S(2)}) collective-permute-start(bf16[512,1024]{1,0:T(8,128)(2,1)} %multiply_convert_fusion.6), channel_id=1, source_target_pairs={{0,16},{8,24},{16,0},{24,8},{1,17},{9,25},{17,1},{25,9},{2,18},{10... | collective-permute-start | bytes 3145736 | tf_op jit(solution)/shard_map/ppermute | solution.py:635
  168.5 8.0 %collective-permute-start.5 = (bf16[512,1024]{1,0:T(8,128)(2,1)}, bf16[512,1024]{1,0:T(8,128)(2,1)S(1)}, u32[]{:S(2)}, u32[]{:S(2)}) collective-permute-start(bf16[512,1024]{1,0:T(8,128)(2,1)} %collective-permute-done.3), channel_id=1, source_target_pairs={{0,8},{8,0},{16,24},{24,16},{1,9},{9,1},{17,25},{25,17},{2,10},{10... | collective-permute-start | bytes 3145736 | tf_op jit(solution)/shard_map/ppermute | solution.py:630
  187.5 2.7 collective-permute-start.8
  209.6 192.6 %reduce-scatter.5.cloned.1.call-start = ((), (), s32[]{:S(2)}) async-start(), calls=%async_computation.4 | async-start | bytes 4718592 | tf_op jit(solution)/shard_map/reduce_scatter | solution.py:1589
  209.6 25.0 %collective-permute-start.9 = (bf16[512,1024]{1,0:T(8,128)(2,1)}, bf16[512,1024]{1,0:T(8,128)(2,1)}, u32[]{:S(2)}, u32[]{:S(2)}) collective-permute-start(bf16[512,1024]{1,0:T(8,128)(2,1)} %add_convert_fusion.5), channel_id=1, source_target_pairs={{0,16},{8,24},{16,0},{24,8},{1,17},{9,25},{17,1},{25,9},{2,18},{10... | collective-permute-start | bytes 3145736 | tf_op jit(solution)/shard_map/ppermute | solution.py:635
  212.4 22.2 %collective-permute-start.6 = (bf16[512,1024]{1,0:T(8,128)(2,1)}, bf16[512,1024]{1,0:T(8,128)(2,1)}, u32[]{:S(2)}, u32[]{:S(2)}) collective-permute-start(bf16[512,1024]{1,0:T(8,128)(2,1)} %slice.209), channel_id=1, source_target_pairs={{0,8},{8,0},{16,24},{24,16},{1,9},{9,1},{17,25},{25,17},{2,10},{10... | collective-permute-start | bytes 3145736 | tf_op jit(solution)/shard_map/ppermute | solution.py:630
  284.8 3.6 collective-permute-start.10
  294.5 11.8 %collective-permute-start.11 = (bf16[512,3072]{1,0:T(8,128)(2,1)}, bf16[512,3072]{1,0:T(8,128)(2,1)}, u32[]{:S(2)}, u32[]{:S(2)}) collective-permute-start(bf16[512,3072]{1,0:T(8,128)(2,1)} %convolution_convert_fusion), channel_id=1, source_target_pairs={{0,8},{8,0},{16,24},{24,16},{1,9},{9,1},{17,25},{25,17},{2,10},{10... | collective-permute-start | bytes 9437192 | tf_op jit(solution)/shard_map/ppermute | solution.py:630
  302.1 3.5 collective-permute-start.12
  317.6 28.4 %collective-permute-start.13 = (bf16[128,2304]{1,0:T(8,128)(2,1)}, bf16[128,2304]{1,0:T(8,128)(2,1)}, u32[]{:S(2)}, u32[]{:S(2)}) collective-permute-start(bf16[128,2304]{1,0:T(8,128)(2,1)} %reduce-scatter.3.cloned.1.call-done), channel_id=1, source_target_pairs={{0,8},{8,0},{16,24},{24,16},{1,9},{9,1},{17,25},{25,17},{2,10},{10... | collective-permute-start | bytes 1769480 | tf_op jit(solution)/shard_map/ppermute | solution.py:630
  318.0 27.4 %collective-permute-start.14 = (bf16[128,2304]{1,0:T(8,128)(2,1)}, bf16[128,2304]{1,0:T(8,128)(2,1)}, u32[]{:S(2)}, u32[]{:S(2)}) collective-permute-start(bf16[128,2304]{1,0:T(8,128)(2,1)} %reduce-scatter.3.cloned.1.call-done), channel_id=1, source_target_pairs={{0,16},{8,24},{16,0},{24,8},{1,17},{9,25},{17,1},{25,9},{2,18},{10... | collective-permute-start | bytes 1769480 | tf_op jit(solution)/shard_map/ppermute | solution.py:635
  324.9 22.2 %collective-permute-start.17 = (bf16[512,1024]{1,0:T(8,128)(2,1)}, bf16[512,1024]{1,0:T(8,128)(2,1)}, u32[]{:S(2)}, u32[]{:S(2)}) collective-permute-start(bf16[512,1024]{1,0:T(8,128)(2,1)} %slice.207), channel_id=1, source_target_pairs={{0,8},{8,0},{16,24},{24,16},{1,9},{9,1},{17,25},{25,17},{2,10},{10... | collective-permute-start | bytes 3145736 | tf_op jit(solution)/shard_map/ppermute | solution.py:630
  330.6 23.7 %collective-permute-start.16 = (bf16[512,1024]{1,0:T(8,128)(2,1)S(1)}, bf16[512,1024]{1,0:T(8,128)(2,1)}, u32[]{:S(2)}, u32[]{:S(2)}) collective-permute-start(bf16[512,1024]{1,0:T(8,128)(2,1)S(1)} %slice.208), channel_id=1, source_target_pairs={{0,8},{8,0},{16,24},{24,16},{1,9},{9,1},{17,25},{25,17},{2,10},{10... | collective-permute-start | bytes 3145736 | tf_op jit(solution)/shard_map/ppermute | solution.py:630
  345.4 4.8 collective-permute-start.15
  348.9 24.9 %collective-permute-start.18 = (bf16[512,1024]{1,0:T(8,128)(2,1)S(1)}, bf16[512,1024]{1,0:T(8,128)(2,1)S(1)}, u32[]{:S(2)}, u32[]{:S(2)}) collective-permute-start(bf16[512,1024]{1,0:T(8,128)(2,1)S(1)} %fusion.20), channel_id=1, source_target_pairs={{0,16},{8,24},{16,0},{24,8},{1,17},{9,25},{17,1},{25,9},{2,18},{10... | collective-permute-start | bytes 3145736 | tf_op jit(solution)/shard_map/ppermute | solution.py:635
  (76 other events, 590.4 us)
Sparse Core Ops, SparseCore 0:
  73.5 77.7 all-gather.1
  209.7 94.8 reduce-scatter.2
  313.7 88.4 reduce-scatter.4

commit v3 on v2

--- a/solution.py
+++ b/solution.py
@@ -901,6 +901,68 @@
 def hand_back_sems(kinds, count, chips):
     dma = pltpu.SemaphoreType.DMA
     return [dma, dma((count,)), dma((kinds,)), dma((kinds, chips)), dma((kinds,)), dma((kinds,)), dma((kinds,))]
+
+
+def weight_grad_kernel(seq_count, joint_ref, near_norm, near_top, far_norm, far_top, near_hidden, near_gate, near_up,
+                       far_hidden, far_gate, far_up, grads_ref, back_ref, send_sem, recv_sem):
+    here = Place(seq_count, 1)
+    turn = pl.program_id(0)
+
+    def onward(k):
+        device = here.next_chip(here.chips - k)
+        return remote(joint_ref.at[k - 1], back_ref.at[k - 1], send_sem.at[k - 1], recv_sem.at[k - 1], device)
+
+    @pl.when(turn == 0)
+    def _():
+        barrier = pltpu.get_barrier_semaphore()
+        for k in range(1, here.chips):
+            pl.semaphore_signal(barrier, inc=1, device_id=here.next_chip(k), device_id_type=pl.DeviceIdType.MESH)
+        pl.semaphore_wait(barrier, here.chips - 1)
+        for k in range(1, here.chips):
+            onward(k).start()
+
+    size = near_gate.shape[1]
+    rows = (
+        (near_norm, near_gate, far_norm, far_gate),
+        (near_norm, near_up, far_norm, far_up),
+        (near_top, near_hidden, far_top, far_hidden),
+    )
+    for j, (near_left, near_right, far_left, far_right) in enumerate(rows):
+        value = product(near_left[...], near_right[...], (0, 0)) + product(far_left[...], far_right[...], (0, 0))
+        grads_ref[:, j * size : (j + 1) * size] = value.astype(LOW)
+
+    @pl.when(turn == pl.num_programs(0) - 1)
+    def _():
+        for k in range(1, here.chips):
+            onward(k).wait()
+
+
+def weight_grads(joint, near_norm, near_top, far_norm, far_top, near, far, seq_count, call_id):
+    width, size = near_norm.shape[1], near[0].shape[1]
+    dma = pltpu.SemaphoreType.DMA
+    hold = pl.BlockSpec(memory_space=pl.ANY)
+
+    def columns(one):
+        return pl.BlockSpec((one.shape[0], TILE), lambda i: (0, i))
+
+    def whole(one):
+        return pl.BlockSpec(one.shape, lambda i: (0, 0))
+
+    lefts, rights = (near_norm, near_top, far_norm, far_top), tuple(near) + tuple(far)
+    tokens = near_norm.shape[0] + far_norm.shape[0]
+    return pl.pallas_call(
+        partial(weight_grad_kernel, seq_count),
+        grid=(width // TILE,),
+        in_specs=[hold] + [columns(one) for one in lefts] + [whole(one) for one in rights],
+        out_specs=(pl.BlockSpec((TILE, 3 * size), lambda i: (i, 0)), hold),
+        out_shape=(
+            jax.ShapeDtypeStruct((width, 3 * size), LOW),
+            jax.ShapeDtypeStruct(joint.shape, joint.dtype),
+        ),
+        scratch_shapes=[dma((max(seq_count // 2 - 1, 1),)), dma((max(seq_count // 2 - 1, 1),))],
+        compiler_params=pltpu.CompilerParams(collective_id=call_id, has_side_effects=True, vmem_limit_bytes=48 << 20),
+        cost_estimate=pl.CostEstimate(flops=6 * tokens * width * size, bytes_accessed=24 << 20, transcendentals=0),
+    )(joint, *lefts, *rights)
 
 
 def middle_kernel(owners, seq_count, count, part_ref, prior_ref, small_ref, wide_ref, sum_ref, small_out, square_whole,
@@ -1511,10 +1573,6 @@
     def grad_in(values):
         return low_dot(values[1], gate_full, (1, 1)) + low_dot(values[2], up_full, (1, 1))
 
-    def weight_grad(values, normed_part, top_part, which):
-        left, right = ((normed_part, values[1]), (normed_part, values[2]), (top_part, values[0]))[which]
-        return low_dot(left, right, (0, 0))
-
     near_top, far_top = jnp.concatenate(top_parts[:2]), jnp.concatenate(top_parts[2:])
     near = spread_out(near_norm, near_top)
     far_straight, near = lax.optimization_barrier((far_straight, near))
@@ -1534,14 +1592,12 @@
 
     crossed = [core_swapped(grad_in(one).astype(LOW)) for one in picked(far, 1)]
     joint = [(grad_in(one) + other.astype(FULL)).astype(LOW) for one, other in zip(picked(far, 0), crossed)]
-    far, near, joint = lax.optimization_barrier((far, near, joint))
-    grad_parts = [chip_shifted(one, -(k + 1)) for k, one in enumerate(joint)]
-    near_weights = [weight_grad(near, near_norm, near_top, j) for j in range(3)]
-    far_weights = [weight_grad(far, far_norm, far_top, j) for j in range(3)]
-    ff_grads = jnp.concatenate([(a + b).astype(LOW) for a, b in zip(near_weights, far_weights)], axis=1)
+    ff_grads, back_parts = weight_grads(
+        jnp.stack(joint), near_norm, near_top, far_norm, far_top, near, far, seq_count, 6
+    )
     ff_part = lax.psum_scatter(ff_grads, "fsdp", scatter_dimension=0, tiled=True)
-    done_grads, grad_parts = lax.optimization_barrier((ff_grads, grad_parts))
-    grad_normed_two = near_grad[:row_count] + sum(one.astype(FULL) for one in [near_back] + list(grad_parts))
+    back_parts = [near_back] + [back_parts[k] for k in range(chips - 1)]
+    grad_normed_two = near_grad[:row_count] + sum(one.astype(FULL) for one in back_parts)
     back_two, grad_gain_two = norm_back(unit_two, scale_two, gains_wide[1], grad_normed_two)
     grad_residual = back_two + cotangent.astype(FULL)
     grad_attention = grad_residual.astype(LOW)

time: 568 us -> 573 us (level)
  Pallas kernels: 279 us -> 309 us
  matrix products: 85.1 us -> 67.4 us
  waiting for transfers between devices: 84.6 us -> 77.8 us
    pallas_call x0 -> x1, Pallas kernels: none -> 29 us  [weight_grads(): pl.pallas_call(partial(weight_grad_kernel, seq_count), grid=(width // TIL...]
    ppermute x5 -> x4, waiting for transfers between devices: 45.1 us -> 22 us  [chip_shifted(): lax.ppermute(value, 'seq', [(i, (i + 2 * by) % count) for i in range(coun...]
    dot_general x31 -> x25, matrix products: 85.1 us -> 67.4 us  [low_dot(): lax.dot_general(left, right, (((dims[0],), (dims[1],)), ((), ())), prefer...]
    reduce_scatter x1, waiting for transfers between devices: 0.01 us -> 10.9 us  [on_device(): lax.psum_scatter(ff_grads, 'fsdp', scatter_dimension=0, tiled=True)]
    reduce_scatter x1, waiting for transfers between devices: 25.1 us -> 33 us  [on_device(): lax.psum_scatter(square_grads, 'fsdp', scatter_dimension=0, tiled=True)]
    unnamed x164 -> x142, local copies, waits for them, and re-layouts: 35.7 us -> 36 us
  transfers between devices with their start and end apart: 22 -> 21, of which waited for: 9 -> 9; matrix products, arithmetic and copies ran while one was open for 19% -> 18% of each run, Pallas kernels for 24% -> 24%
where the time goes in v3:
time: 573 us; the launch traced here: 565 us
  Pallas kernels  309 us (54%)
  waiting for transfers between devices  77.8 us (14%)
  matrix products  67.4 us (12%)
  local copies, waits for them, and re-layouts  55.8 us (10%)
  other arithmetic  24.2 us (4%)
  starting transfers between devices  15.7 us (3%)
  between operations  15.2 us (3%)
    pallas_call x1, Pallas kernels, handed_back(): pl.pallas_call(partial(hand_back_kernel, owners, seq_count, count), in_sp...  111 us
    dot_general x25, matrix products, low_dot(): lax.dot_general(left, right, (((dims[0],), (dims[1],)), ((), ())), prefer...  67.4 us
    pallas_call x1, Pallas kernels, gathered_mixer(): pl.pallas_call(partial(gather_kernel, along, across, seq_count), in_specs...  53.9 us
    unnamed x142, local copies, waits for them, and re-layouts  36 us
    reduce_scatter x1, waiting for transfers between devices, on_device(): lax.psum_scatter(square_grads, 'fsdp', scatter_dimension=0, tiled=True)  33 us
    pallas_call x1, Pallas kernels, backward_blocks(): pl.pallas_call(backward_kernel, grid=(groups, steps), in_specs=[flat, pl....  29.5 us
    pallas_call x1, Pallas kernels, weight_grads(): pl.pallas_call(partial(weight_grad_kernel, seq_count), grid=(width // TIL...  29 us
    pallas_call x1, Pallas kernels, forward_blocks(): pl.pallas_call(forward_kernel, grid=(groups, steps), in_specs=[pl.BlockSp...  24.9 us
  transfers between devices with their start and end apart: 21, of which 9 were waited for; matrix products, arithmetic and copies ran while one was open for 18% of the time, Pallas kernels for 24%

profile of v3, /device:TPU:31, one launch (start us, length us, event | category | flops | bytes accessed | tf_op | source)
XLA Modules:
  0.0 564.6 jit_solution(3028745338941337761)
XLA Ops:
  19.3 53.9 %shard_map.323 = (bf16[1024,4096]{1,0:T(8,128)(2,1)}, bf16[32,1024]{1,0:T(8,128)(2,1)}) custom-call(bf16[128,4096]{1,0:T(8,128)(2,1)} %copy-done.14, bf16[32,128]{1,0:T(8,128)(2,1)} %copy-done.26), custom_call_target="tpu_custom_call" | custom-call | tf_op jit(solution)/shard_map/pallas_call | solution.py:605
  78.3 6.4 %fusion.4.proj_ref.prev_ref = bf16[512,3072]{1,0:T(8,128)(2,1)S(1)} fusion(bf16[512,1024]{1,0:T(8,128)(2,1)S(1)} %fusion.13, bf16[1024,4096]{1,0:T(8,128)(2,1)} %get-tuple-element.104), kind=kOutput, calls=%fused_computation.5 | convolution fusion | flops 3222798336 | bytes 10485760 | tf_op jit(solution)/shard_map/dot_general | solution.py:659
  89.8 24.9 %shard_map.324 = (bf16[3,512,1024]{2,1,0:T(8,128)(2,1)}, bf16[4,8,128,128]{3,2,1,0:T(8,128)(2,1)S(1)}, bf16[512,1024]{1,0:T(8,128)(2,1)S(1)}, f32[512,1024]{1,0:...) custom-call(bf16[512,3072]{1,0:T(8,128)(2,1)} %copy-done.36, ...), custom_call_target="tpu_custom_call" | custom-call | flops 8589934592 | bytes 25165824 | tf_op jit(solution)/shard_map/pallas_call | solution.py:204
  114.6 11.9 %shard_map.325.state_ref.enter_ref = f32[8,128,128]{2,1,0:T(8,128)S(1)} custom-call(f32[8,128,128]{2,1,0:T(8,128)S(1)} %get-tuple-element.112.local_ref, f32[8,128,128]{2,1,0:T(8,128)S(1)} %get-tuple-element.113.transfer_ref), custom_call_target="tpu_custom_call" | custom-call | tf_op jit(solution)/shard_map/pallas_call | solution.py:753
  132.0 4.1 multiply_reduce_fusion.2
  143.5 7.8 %all-gather.2.cloned.1.call-done = bf16[1024,2304]{1,0:T(8,128)(2,1)} async-done(((bf16[128,2304]{1,0:T(8,128)(2,1)}), bf16[1024,2304]{1,0:T(8,128)(2,1)}) %all-gather.2.cloned.1.call-update) | async-done | bytes 4718608 | tf_op jit(solution)/shard_map/all_gather | solution.py:1516
  161.7 3.9 collective-permute-done.3
  170.2 3.9 convolution_add_fusion
  177.2 4.8 multiply_convert_fusion
  189.1 29.0 %shard_map.327 = (bf16[1024,2304]{1,0:T(8,128)(2,1)}, bf16[1,512,1024]{2,1,0:T(8,128)(2,1)S(1)}) custom-call(bf16[1,512,1024]{2,1,0:T(8,128)(2,1)S(1)} %fusion.36.joint_ref, bf16[1024,1024]{1,0:T(8,128)(2,1)} %pad_maximum_fusion.1.near_norm, bf16[1024,1024]{1,0:T(8,128)(2,1)} %copy-done.54, bf16[1024,1024]{1,0:T(8,128)(2,1)} %copy-done.56, ...), custom_call_target="tpu_custom_call" | custom-call | flops 9663676416 | bytes 25165824 | tf_op jit(solution)/shard_map/pallas_call | solution.py:953
  238.8 5.8 %shard_map.329.leave_ref = f32[8,128,128]{2,1,0:T(8,128)S(1)} custom-call(f32[8,128,128]{2,1,0:T(8,128)S(1)} %get-tuple-element.129.local_ref, f32[8,128,128]{2,1,0:T(8,128)S(1)} %get-tuple-element.113.transfer_ref), custom_call_target="tpu_custom_call" | custom-call | tf_op jit(solution)/shard_map/pallas_call | solution.py:753
  244.6 29.5 %shard_map.330 = (bf16[512,3072]{1,0:T(8,128)(2,1)}, f32[1,512,8]{2,1,0:T(8,128)S(1)}, f32[3,4,1024]{2,1,0:T(4,128)S(1)}, f32[8,3072]{1,0:T(8,128)S(1)}, f32[8,3072]{1,0:T(8,128)S(1)}) custom-call(bf16[512,3072]{1,0:T(8,128)(2,1)} %copy-done.36, bf16[512,3072]{1,0:T(8,128)(2,1)} %copy-done.36, bf16[16,3072]{1,0:T(8,128)(2,1)S(1)} %collective-permute-done.2.rim_ref, ...), custom_call_target="tpu_custom_call" | custom-call | flops 4294967296 | bytes 25165824 | tf_op jit(solution)/shard_map/pallas_call | solution.py:465
  278.3 5.5 convolution_convert_fusion
  283.8 4.3 collective-permute-start.10
  303.3 10.9 %reduce-scatter.3.cloned.1.call-done = bf16[128,2304]{1,0:T(8,128)(2,1)} async-done(((bf16[1024,2304]{1,0:T(8,128)(2,1)}), bf16[128,2304]{1,0:T(8,128)(2,1)}) %reduce-scatter.3.cloned.1.call-update) | async-done | bytes 589840 | tf_op jit(solution)/shard_map/reduce_scatter | solution.py:1598
  317.3 3.8 fusion.42
  322.8 3.9 fusion.44
  331.1 5.1 fusion.18
  347.2 3.8 shard_map.331
  351.0 18.1 %collective-permute-done.17 = bf16[512,1024]{1,0:T(8,128)(2,1)S(1)} collective-permute-done((bf16[512,1024]{1,0:T(8,128)(2,1)S(1)}, bf16[512,1024]{1,0:T(8,128)(2,1)S(1)}, u32[]{:S(2)}, u32[]{:S(2)}) %collective-permute-start.17) | collective-permute-done | bytes 1048608 | tf_op jit(solution)/shard_map/ppermute | solution.py:635
  372.5 33.0 %reduce-scatter.5.cloned.1.call-done.part_ref = bf16[64,4096]{1,0:T(8,128)(2,1)} async-done(((bf16[512,4096]{1,0:T(8,128)(2,1)}), bf16[64,4096]{1,0:T(8,128)(2,1)}) %reduce-scatter.5.cloned.1.call-update) | async-done | bytes 524304 | tf_op jit(solution)/shard_map/reduce_scatter | solution.py:1645
  406.5 23.2 %shard_map.332 = (f32[2,64,4096]{2,1,0:T(8,128)S(1)}, f32[24,128]{1,0:T(8,128)S(1)}, bf16[8,2,64,1024]{3,2,1,0:T(8,128)(2,1)}, bf16[8,2,64,2816]{3,2,1,0:T(8,128)(2,1)}) custom-call(bf16[64,4096]{1,0:T(8,128)(2,1)S(1)} %copy-done.23, f32[64,4096]{1,0:T(8,128)S(1)} %pad_maximum_fusion.2.prior_ref, f32[8,24,128]{2,1,0:T(8,128)S(1)} %bitcast.100, ...), custom_call_target="tpu_custom_call" | custom-call | tf_op jit(solution)/shard_map/pallas_call | solution.py:1046
  434.5 111.4 %shard_map.333 = (bf16[3,2,64,2816]{3,2,1,0:T(8,128)(2,1)}, bf16[4,2,64,1024]{3,2,1,0:T(8,128)(2,1)}) custom-call(bf16[8,64,2816]{2,1,0:T(8,128)(2,1)} %get-tuple-element.298.wide_ref, bf16[8,64,1024]{2,1,0:T(8,128)(2,1)S(1)} %get-tuple-element.299.square_ref), custom_call_target="tpu_custom_call" | custom-call | tf_op jit(solution)/shard_map/pallas_call | solution.py:1088
  545.8 9.0 %shard_map.334 = (f32[3,128,1024]{2,1,0:T(8,128)}, f32[3,128,1024]{2,1,0:T(8,128)}, f32[128,8]{1,0:T(8,128)}, f32[128,8]{1,0:T(8,128)}, f32[3,4,128]{2,1,0:T(4,1...) custom-call(bf16[3,128,2816]{2,1,0:T(8,128)(2,1)} %bitcast.108, ...), custom_call_target="tpu_custom_call" | custom-call | tf_op jit(solution)/shard_map/pallas_call | solution.py:1235
  (274 shorter events, 133.3 us)
Async XLA Ops:
  7.2 144.0 %all-gather.2.cloned.1.call-start = ((), (), s32[]{:S(2)}) async-start(), calls=%async_computation.2 | async-start | bytes 5308416 | tf_op jit(solution)/shard_map/all_gather | solution.py:1516
  7.2 66.0 %collective-permute-start = (bf16[512,1024]{1,0:T(8,128)(2,1)}, bf16[512,1024]{1,0:T(8,128)(2,1)}, u32[]{:S(2)}, u32[]{:S(2)}) collective-permute-start(bf16[512,1024]{1,0:T(8,128)(2,1)} %param.24), channel_id=1, source_target_pairs={{0,8},{8,0},{16,24},{24,16},{1,9},{9,1},{17,25},{25,17},{2,10},{10... | collective-permute-start | bytes 3145736 | tf_op jit(solution)/shard_map/ppermute | solution.py:630
  8.0 65.3 %collective-permute-start.1 = (bf16[512,1024]{1,0:T(8,128)(2,1)}, bf16[512,1024]{1,0:T(8,128)(2,1)}, u32[]{:S(2)}, u32[]{:S(2)}) collective-permute-start(bf16[512,1024]{1,0:T(8,128)(2,1)} %param.24), channel_id=1, source_target_pairs={{0,16},{8,24},{16,0},{24,8},{1,17},{9,25},{17,1},{25,9},{2,18},{10... | collective-permute-start | bytes 3145736 | tf_op jit(solution)/shard_map/ppermute | solution.py:635
  19.3 56.3 %copy-start.39 = (bf16[512,1024]{1,0:T(8,128)(2,1)S(1)}, bf16[512,1024]{1,0:T(8,128)(2,1)}, u32[]{:S(2)}) copy-start(bf16[512,1024]{1,0:T(8,128)(2,1)} %param.23) | copy-start | bytes 3145732
  73.3 240.9 %reduce-scatter.3.cloned.1.call-start = ((), (), s32[]{:S(2)}) async-start(), calls=%async_computation.3 | async-start | bytes 5308416 | tf_op jit(solution)/shard_map/reduce_scatter | solution.py:1598
  86.6 3.2 collective-permute-start.2
  88.3 52.6 %collective-permute-start.7 = (bf16[512,1024]{1,0:T(8,128)(2,1)}, bf16[512,1024]{1,0:T(8,128)(2,1)S(1)}, u32[]{:S(2)}, u32[]{:S(2)}) collective-permute-start(bf16[512,1024]{1,0:T(8,128)(2,1)} %collective-permute-done.1), channel_id=1, source_target_pairs={{0,8},{8,0},{16,24},{24,16},{1,9},{9,1},{17,25},{25,17},{2,10},{10... | collective-permute-start | bytes 3145736 | tf_op jit(solution)/shard_map/ppermute | solution.py:630
  136.4 7.1 %collective-permute-start.4 = (bf16[512,1024]{1,0:T(8,128)(2,1)S(1)}, bf16[512,1024]{1,0:T(8,128)(2,1)}, u32[]{:S(2)}, u32[]{:S(2)}) collective-permute-start(bf16[512,1024]{1,0:T(8,128)(2,1)S(1)} %multiply_convert_fusion.6), channel_id=1, source_target_pairs={{0,8},{8,0},{16,24},{24,16},{1,9},{9,1},{17,25},{25,17},{2,10},{10... | collective-permute-start | bytes 3145736 | tf_op jit(solution)/shard_map/ppermute | solution.py:630
  140.8 24.8 %collective-permute-start.3 = (bf16[512,1024]{1,0:T(8,128)(2,1)S(1)}, bf16[512,1024]{1,0:T(8,128)(2,1)}, u32[]{:S(2)}, u32[]{:S(2)}) collective-permute-start(bf16[512,1024]{1,0:T(8,128)(2,1)S(1)} %multiply_convert_fusion.6), channel_id=1, source_target_pairs={{0,16},{8,24},{16,0},{24,8},{1,17},{9,25},{17,1},{25,9},{2,18},{10... | collective-permute-start | bytes 3145736 | tf_op jit(solution)/shard_map/ppermute | solution.py:635
  161.7 27.4 %copy-start.29 = (bf16[1024,768]{1,0:T(8,128)(2,1)}, bf16[1024,768]{1,0:T(8,128)(2,1)S(1)}, u32[]{:S(2)}) copy-start(bf16[1024,768]{1,0:T(8,128)(2,1)S(1)} %get-tuple-element.142.near_hidden) | copy-start | bytes 4718596
  165.6 8.5 %collective-permute-start.5 = (bf16[512,1024]{1,0:T(8,128)(2,1)}, bf16[512,1024]{1,0:T(8,128)(2,1)S(1)}, u32[]{:S(2)}, u32[]{:S(2)}) collective-permute-start(bf16[512,1024]{1,0:T(8,128)(2,1)} %collective-permute-done.3), channel_id=1, source_target_pairs={{0,8},{8,0},{16,24},{24,16},{1,9},{9,1},{17,25},{25,17},{2,10},{10... | collective-permute-start | bytes 3145736 | tf_op jit(solution)/shard_map/ppermute | solution.py:630
  184.1 3.9 collective-permute-start.8
  218.1 187.4 %reduce-scatter.5.cloned.1.call-start = ((), (), s32[]{:S(2)}) async-start(), calls=%async_computation.4 | async-start | bytes 4718592 | tf_op jit(solution)/shard_map/reduce_scatter | solution.py:1645
  220.9 4.0 collective-permute-start.6
  244.6 32.2 %copy-start.42 = (bf16[512,1024]{0,1:T(8,128)(2,1)S(1)}, bf16[512,1024]{0,1:T(8,128)(2,1)}, u32[]{:S(2)}) copy-start(bf16[512,1024]{0,1:T(8,128)(2,1)} %copy.95) | copy-start | bytes 3145732
  274.2 3.5 collective-permute-start.9
  283.8 12.2 %collective-permute-start.10 = (bf16[512,3072]{1,0:T(8,128)(2,1)}, bf16[512,3072]{1,0:T(8,128)(2,1)}, u32[]{:S(2)}, u32[]{:S(2)}) collective-permute-start(bf16[512,3072]{1,0:T(8,128)(2,1)} %convolution_convert_fusion), channel_id=1, source_target_pairs={{0,8},{8,0},{16,24},{24,16},{1,9},{9,1},{17,25},{25,17},{2,10},{10... | collective-permute-start | bytes 9437192 | tf_op jit(solution)/shard_map/ppermute | solution.py:630
  292.5 2.7 collective-permute-start.11
  316.6 25.2 %collective-permute-start.12 = (bf16[128,2304]{1,0:T(8,128)(2,1)}, bf16[128,2304]{1,0:T(8,128)(2,1)}, u32[]{:S(2)}, u32[]{:S(2)}) collective-permute-start(bf16[128,2304]{1,0:T(8,128)(2,1)} %reduce-scatter.3.cloned.1.call-done), channel_id=1, source_target_pairs={{0,8},{8,0},{16,24},{24,16},{1,9},{9,1},{17,25},{25,17},{2,10},{10... | collective-permute-start | bytes 1769480 | tf_op jit(solution)/shard_map/ppermute | solution.py:630
  317.1 24.6 %collective-permute-start.13 = (bf16[128,2304]{1,0:T(8,128)(2,1)}, bf16[128,2304]{1,0:T(8,128)(2,1)}, u32[]{:S(2)}, u32[]{:S(2)}) collective-permute-start(bf16[128,2304]{1,0:T(8,128)(2,1)} %reduce-scatter.3.cloned.1.call-done), channel_id=1, source_target_pairs={{0,16},{8,24},{16,0},{24,8},{1,17},{9,25},{17,1},{25,9},{2,18},{10... | collective-permute-start | bytes 1769480 | tf_op jit(solution)/shard_map/ppermute | solution.py:635
  322.5 20.4 %collective-permute-start.16 = (bf16[512,1024]{1,0:T(8,128)(2,1)}, bf16[512,1024]{1,0:T(8,128)(2,1)}, u32[]{:S(2)}, u32[]{:S(2)}) collective-permute-start(bf16[512,1024]{1,0:T(8,128)(2,1)} %slice.207), channel_id=1, source_target_pairs={{0,8},{8,0},{16,24},{24,16},{1,9},{9,1},{17,25},{25,17},{2,10},{10... | collective-permute-start | bytes 3145736 | tf_op jit(solution)/shard_map/ppermute | solution.py:630
  327.9 23.1 %collective-permute-start.15 = (bf16[512,1024]{1,0:T(8,128)(2,1)}, bf16[512,1024]{1,0:T(8,128)(2,1)}, u32[]{:S(2)}, u32[]{:S(2)}) collective-permute-start(bf16[512,1024]{1,0:T(8,128)(2,1)} %slice.208), channel_id=1, source_target_pairs={{0,8},{8,0},{16,24},{24,16},{1,9},{9,1},{17,25},{25,17},{2,10},{10... | collective-permute-start | bytes 3145736 | tf_op jit(solution)/shard_map/ppermute | solution.py:630
  341.7 5.4 collective-permute-start.14
  344.7 24.4 %collective-permute-start.17 = (bf16[512,1024]{1,0:T(8,128)(2,1)S(1)}, bf16[512,1024]{1,0:T(8,128)(2,1)S(1)}, u32[]{:S(2)}, u32[]{:S(2)}) collective-permute-start(bf16[512,1024]{1,0:T(8,128)(2,1)S(1)} %fusion.20), channel_id=1, source_target_pairs={{0,16},{8,24},{16,0},{24,8},{1,17},{9,25},{17,1},{25,9},{2,18},{10... | collective-permute-start | bytes 3145736 | tf_op jit(solution)/shard_map/ppermute | solution.py:635
  (64 other events, 339.5 us)
Sparse Core Ops, SparseCore 0:
  73.4 77.7 all-gather.1
  218.2 95.9 reduce-scatter.2
  317.8 87.6 reduce-scatter.4

commit v4 on v3

--- a/solution.py
+++ b/solution.py
@@ -922,14 +922,12 @@
             onward(k).start()
 
     size = near_gate.shape[1]
-    rows = (
-        (near_norm, near_gate, far_norm, far_gate),
-        (near_norm, near_up, far_norm, far_up),
-        (near_top, near_hidden, far_top, far_hidden),
-    )
-    for j, (near_left, near_right, far_left, far_right) in enumerate(rows):
-        value = product(near_left[...], near_right[...], (0, 0)) + product(far_left[...], far_right[...], (0, 0))
+    near_turned, far_turned = near_norm[...].T, far_norm[...].T
+    for j, (near_right, far_right) in enumerate(((near_gate, far_gate), (near_up, far_up))):
+        value = product(near_turned, near_right[...]) + product(far_turned, far_right[...])
         grads_ref[:, j * size : (j + 1) * size] = value.astype(LOW)
+    value = product(near_top[...].T, near_hidden[...]) + product(far_top[...].T, far_hidden[...])
+    grads_ref[:, 2 * size :] = value.astype(LOW)
 
     @pl.when(turn == pl.num_programs(0) - 1)
     def _():

time: 573 us -> 573 us (level)
  no operation moved by 1% of the time
where the time goes in v4:
time: 573 us; the launch traced here: 565 us
  Pallas kernels  309 us (54%)
  waiting for transfers between devices  77.8 us (14%)
  matrix products  67.4 us (12%)
  local copies, waits for them, and re-layouts  55.8 us (10%)
  other arithmetic  24.2 us (4%)
  starting transfers between devices  15.7 us (3%)
  between operations  15.2 us (3%)
    pallas_call x1, Pallas kernels, handed_back(): pl.pallas_call(partial(hand_back_kernel, owners, seq_count, count), in_sp...  111 us
    dot_general x25, matrix products, low_dot(): lax.dot_general(left, right, (((dims[0],), (dims[1],)), ((), ())), prefer...  67.4 us
    pallas_call x1, Pallas kernels, gathered_mixer(): pl.pallas_call(partial(gather_kernel, along, across, seq_count), in_specs...  53.9 us
    unnamed x142, local copies, waits for them, and re-layouts  36 us
    reduce_scatter x1, waiting for transfers between devices, on_device(): lax.psum_scatter(square_grads, 'fsdp', scatter_dimension=0, tiled=True)  33 us
    pallas_call x1, Pallas kernels, backward_blocks(): pl.pallas_call(backward_kernel, grid=(groups, steps), in_specs=[flat, pl....  29.5 us
    pallas_call x1, Pallas kernels, weight_grads(): pl.pallas_call(partial(weight_grad_kernel, seq_count), grid=(width // TIL...  29 us
    pallas_call x1, Pallas kernels, forward_blocks(): pl.pallas_call(forward_kernel, grid=(groups, steps), in_specs=[pl.BlockSp...  24.9 us
  transfers between devices with their start and end apart: 21, of which 9 were waited for; matrix products, arithmetic and copies ran while one was open for 18% of the time, Pallas kernels for 24%

profile of v4, /device:TPU:31, one launch (start us, length us, event | category | flops | bytes accessed | tf_op | source)
XLA Modules:
  0.0 564.6 jit_solution(12757971119827193868)
XLA Ops:
  19.3 53.9 %shard_map.323 = (bf16[1024,4096]{1,0:T(8,128)(2,1)}, bf16[32,1024]{1,0:T(8,128)(2,1)}) custom-call(bf16[128,4096]{1,0:T(8,128)(2,1)} %copy-done.14, bf16[32,128]{1,0:T(8,128)(2,1)} %copy-done.26), custom_call_target="tpu_custom_call" | custom-call | tf_op jit(solution)/shard_map/pallas_call | solution.py:605
  78.3 6.4 %fusion.4.proj_ref.prev_ref = bf16[512,3072]{1,0:T(8,128)(2,1)S(1)} fusion(bf16[512,1024]{1,0:T(8,128)(2,1)S(1)} %fusion.13, bf16[1024,4096]{1,0:T(8,128)(2,1)} %get-tuple-element.104), kind=kOutput, calls=%fused_computation.5 | convolution fusion | flops 3222798336 | bytes 10485760 | tf_op jit(solution)/shard_map/dot_general | solution.py:659
  89.8 24.9 %shard_map.324 = (bf16[3,512,1024]{2,1,0:T(8,128)(2,1)}, bf16[4,8,128,128]{3,2,1,0:T(8,128)(2,1)S(1)}, bf16[512,1024]{1,0:T(8,128)(2,1)S(1)}, f32[512,1024]{1,0:...) custom-call(bf16[512,3072]{1,0:T(8,128)(2,1)} %copy-done.36, ...), custom_call_target="tpu_custom_call" | custom-call | flops 8589934592 | bytes 25165824 | tf_op jit(solution)/shard_map/pallas_call | solution.py:204
  114.6 11.9 %shard_map.325.state_ref.enter_ref = f32[8,128,128]{2,1,0:T(8,128)S(1)} custom-call(f32[8,128,128]{2,1,0:T(8,128)S(1)} %get-tuple-element.112.local_ref, f32[8,128,128]{2,1,0:T(8,128)S(1)} %get-tuple-element.113.transfer_ref), custom_call_target="tpu_custom_call" | custom-call | tf_op jit(solution)/shard_map/pallas_call | solution.py:753
  132.0 4.1 multiply_reduce_fusion.2
  143.5 7.8 %all-gather.2.cloned.1.call-done = bf16[1024,2304]{1,0:T(8,128)(2,1)} async-done(((bf16[128,2304]{1,0:T(8,128)(2,1)}), bf16[1024,2304]{1,0:T(8,128)(2,1)}) %all-gather.2.cloned.1.call-update) | async-done | bytes 4718608 | tf_op jit(solution)/shard_map/all_gather | solution.py:1514
  161.7 3.9 collective-permute-done.3
  170.2 3.9 convolution_add_fusion
  177.2 4.8 multiply_convert_fusion
  189.1 29.0 %shard_map.327 = (bf16[1024,2304]{1,0:T(8,128)(2,1)}, bf16[1,512,1024]{2,1,0:T(8,128)(2,1)S(1)}) custom-call(bf16[1,512,1024]{2,1,0:T(8,128)(2,1)S(1)} %fusion.36.joint_ref, bf16[1024,1024]{1,0:T(8,128)(2,1)} %pad_maximum_fusion.1.near_norm, bf16[1024,1024]{1,0:T(8,128)(2,1)} %copy-done.54, bf16[1024,1024]{1,0:T(8,128)(2,1)} %copy-done.56, ...), custom_call_target="tpu_custom_call" | custom-call | flops 9663676416 | bytes 25165824 | tf_op jit(solution)/shard_map/pallas_call | solution.py:951
  238.8 5.8 %shard_map.329.leave_ref = f32[8,128,128]{2,1,0:T(8,128)S(1)} custom-call(f32[8,128,128]{2,1,0:T(8,128)S(1)} %get-tuple-element.129.local_ref, f32[8,128,128]{2,1,0:T(8,128)S(1)} %get-tuple-element.113.transfer_ref), custom_call_target="tpu_custom_call" | custom-call | tf_op jit(solution)/shard_map/pallas_call | solution.py:753
  244.6 29.5 %shard_map.330 = (bf16[512,3072]{1,0:T(8,128)(2,1)}, f32[1,512,8]{2,1,0:T(8,128)S(1)}, f32[3,4,1024]{2,1,0:T(4,128)S(1)}, f32[8,3072]{1,0:T(8,128)S(1)}, f32[8,3072]{1,0:T(8,128)S(1)}) custom-call(bf16[512,3072]{1,0:T(8,128)(2,1)} %copy-done.36, bf16[512,3072]{1,0:T(8,128)(2,1)} %copy-done.36, bf16[16,3072]{1,0:T(8,128)(2,1)S(1)} %collective-permute-done.2.rim_ref, ...), custom_call_target="tpu_custom_call" | custom-call | flops 4294967296 | bytes 25165824 | tf_op jit(solution)/shard_map/pallas_call | solution.py:465
  278.3 5.5 convolution_convert_fusion
  283.8 4.3 collective-permute-start.10
  303.3 10.9 %reduce-scatter.3.cloned.1.call-done = bf16[128,2304]{1,0:T(8,128)(2,1)} async-done(((bf16[1024,2304]{1,0:T(8,128)(2,1)}), bf16[128,2304]{1,0:T(8,128)(2,1)}) %reduce-scatter.3.cloned.1.call-update) | async-done | bytes 589840 | tf_op jit(solution)/shard_map/reduce_scatter | solution.py:1596
  317.3 3.8 fusion.42
  322.8 3.9 fusion.44
  331.1 5.1 fusion.18
  347.2 3.8 shard_map.331
  351.0 18.1 %collective-permute-done.17 = bf16[512,1024]{1,0:T(8,128)(2,1)S(1)} collective-permute-done((bf16[512,1024]{1,0:T(8,128)(2,1)S(1)}, bf16[512,1024]{1,0:T(8,128)(2,1)S(1)}, u32[]{:S(2)}, u32[]{:S(2)}) %collective-permute-start.17) | collective-permute-done | bytes 1048608 | tf_op jit(solution)/shard_map/ppermute | solution.py:635
  372.5 33.0 %reduce-scatter.5.cloned.1.call-done.part_ref = bf16[64,4096]{1,0:T(8,128)(2,1)} async-done(((bf16[512,4096]{1,0:T(8,128)(2,1)}), bf16[64,4096]{1,0:T(8,128)(2,1)}) %reduce-scatter.5.cloned.1.call-update) | async-done | bytes 524304 | tf_op jit(solution)/shard_map/reduce_scatter | solution.py:1643
  406.5 23.2 %shard_map.332 = (f32[2,64,4096]{2,1,0:T(8,128)S(1)}, f32[24,128]{1,0:T(8,128)S(1)}, bf16[8,2,64,1024]{3,2,1,0:T(8,128)(2,1)}, bf16[8,2,64,2816]{3,2,1,0:T(8,128)(2,1)}) custom-call(bf16[64,4096]{1,0:T(8,128)(2,1)S(1)} %copy-done.23, f32[64,4096]{1,0:T(8,128)S(1)} %pad_maximum_fusion.2.prior_ref, f32[8,24,128]{2,1,0:T(8,128)S(1)} %bitcast.100, ...), custom_call_target="tpu_custom_call" | custom-call | tf_op jit(solution)/shard_map/pallas_call | solution.py:1044
  434.5 111.4 %shard_map.333 = (bf16[3,2,64,2816]{3,2,1,0:T(8,128)(2,1)}, bf16[4,2,64,1024]{3,2,1,0:T(8,128)(2,1)}) custom-call(bf16[8,64,2816]{2,1,0:T(8,128)(2,1)} %get-tuple-element.298.wide_ref, bf16[8,64,1024]{2,1,0:T(8,128)(2,1)S(1)} %get-tuple-element.299.square_ref), custom_call_target="tpu_custom_call" | custom-call | tf_op jit(solution)/shard_map/pallas_call | solution.py:1086
  545.8 9.0 %shard_map.334 = (f32[3,128,1024]{2,1,0:T(8,128)}, f32[3,128,1024]{2,1,0:T(8,128)}, f32[128,8]{1,0:T(8,128)}, f32[128,8]{1,0:T(8,128)}, f32[3,4,128]{2,1,0:T(4,1...) custom-call(bf16[3,128,2816]{2,1,0:T(8,128)(2,1)} %bitcast.108, ...), custom_call_target="tpu_custom_call" | custom-call | tf_op jit(solution)/shard_map/pallas_call | solution.py:1233
  (274 shorter events, 133.3 us)
Async XLA Ops:
  7.2 144.0 %all-gather.2.cloned.1.call-start = ((), (), s32[]{:S(2)}) async-start(), calls=%async_computation.2 | async-start | bytes 5308416 | tf_op jit(solution)/shard_map/all_gather | solution.py:1514
  7.2 66.0 %collective-permute-start = (bf16[512,1024]{1,0:T(8,128)(2,1)}, bf16[512,1024]{1,0:T(8,128)(2,1)}, u32[]{:S(2)}, u32[]{:S(2)}) collective-permute-start(bf16[512,1024]{1,0:T(8,128)(2,1)} %param.24), channel_id=1, source_target_pairs={{0,8},{8,0},{16,24},{24,16},{1,9},{9,1},{17,25},{25,17},{2,10},{10... | collective-permute-start | bytes 3145736 | tf_op jit(solution)/shard_map/ppermute | solution.py:630
  8.0 65.3 %collective-permute-start.1 = (bf16[512,1024]{1,0:T(8,128)(2,1)}, bf16[512,1024]{1,0:T(8,128)(2,1)}, u32[]{:S(2)}, u32[]{:S(2)}) collective-permute-start(bf16[512,1024]{1,0:T(8,128)(2,1)} %param.24), channel_id=1, source_target_pairs={{0,16},{8,24},{16,0},{24,8},{1,17},{9,25},{17,1},{25,9},{2,18},{10... | collective-permute-start | bytes 3145736 | tf_op jit(solution)/shard_map/ppermute | solution.py:635
  19.3 56.3 %copy-start.39 = (bf16[512,1024]{1,0:T(8,128)(2,1)S(1)}, bf16[512,1024]{1,0:T(8,128)(2,1)}, u32[]{:S(2)}) copy-start(bf16[512,1024]{1,0:T(8,128)(2,1)} %param.23) | copy-start | bytes 3145732
  73.3 240.9 %reduce-scatter.3.cloned.1.call-start = ((), (), s32[]{:S(2)}) async-start(), calls=%async_computation.3 | async-start | bytes 5308416 | tf_op jit(solution)/shard_map/reduce_scatter | solution.py:1596
  86.6 3.2 collective-permute-start.2
  88.3 52.6 %collective-permute-start.7 = (bf16[512,1024]{1,0:T(8,128)(2,1)}, bf16[512,1024]{1,0:T(8,128)(2,1)S(1)}, u32[]{:S(2)}, u32[]{:S(2)}) collective-permute-start(bf16[512,1024]{1,0:T(8,128)(2,1)} %collective-permute-done.1), channel_id=1, source_target_pairs={{0,8},{8,0},{16,24},{24,16},{1,9},{9,1},{17,25},{25,17},{2,10},{10... | collective-permute-start | bytes 3145736 | tf_op jit(solution)/shard_map/ppermute | solution.py:630
  136.4 7.1 %collective-permute-start.4 = (bf16[512,1024]{1,0:T(8,128)(2,1)S(1)}, bf16[512,1024]{1,0:T(8,128)(2,1)}, u32[]{:S(2)}, u32[]{:S(2)}) collective-permute-start(bf16[512,1024]{1,0:T(8,128)(2,1)S(1)} %multiply_convert_fusion.6), channel_id=1, source_target_pairs={{0,8},{8,0},{16,24},{24,16},{1,9},{9,1},{17,25},{25,17},{2,10},{10... | collective-permute-start | bytes 3145736 | tf_op jit(solution)/shard_map/ppermute | solution.py:630
  140.8 24.8 %collective-permute-start.3 = (bf16[512,1024]{1,0:T(8,128)(2,1)S(1)}, bf16[512,1024]{1,0:T(8,128)(2,1)}, u32[]{:S(2)}, u32[]{:S(2)}) collective-permute-start(bf16[512,1024]{1,0:T(8,128)(2,1)S(1)} %multiply_convert_fusion.6), channel_id=1, source_target_pairs={{0,16},{8,24},{16,0},{24,8},{1,17},{9,25},{17,1},{25,9},{2,18},{10... | collective-permute-start | bytes 3145736 | tf_op jit(solution)/shard_map/ppermute | solution.py:635
  161.7 27.4 %copy-start.29 = (bf16[1024,768]{1,0:T(8,128)(2,1)}, bf16[1024,768]{1,0:T(8,128)(2,1)S(1)}, u32[]{:S(2)}) copy-start(bf16[1024,768]{1,0:T(8,128)(2,1)S(1)} %get-tuple-element.142.near_hidden) | copy-start | bytes 4718596
  165.6 8.5 %collective-permute-start.5 = (bf16[512,1024]{1,0:T(8,128)(2,1)}, bf16[512,1024]{1,0:T(8,128)(2,1)S(1)}, u32[]{:S(2)}, u32[]{:S(2)}) collective-permute-start(bf16[512,1024]{1,0:T(8,128)(2,1)} %collective-permute-done.3), channel_id=1, source_target_pairs={{0,8},{8,0},{16,24},{24,16},{1,9},{9,1},{17,25},{25,17},{2,10},{10... | collective-permute-start | bytes 3145736 | tf_op jit(solution)/shard_map/ppermute | solution.py:630
  184.1 3.9 collective-permute-start.8
  218.1 187.4 %reduce-scatter.5.cloned.1.call-start = ((), (), s32[]{:S(2)}) async-start(), calls=%async_computation.4 | async-start | bytes 4718592 | tf_op jit(solution)/shard_map/reduce_scatter | solution.py:1643
  220.9 4.0 collective-permute-start.6
  244.6 32.2 %copy-start.42 = (bf16[512,1024]{0,1:T(8,128)(2,1)S(1)}, bf16[512,1024]{0,1:T(8,128)(2,1)}, u32[]{:S(2)}) copy-start(bf16[512,1024]{0,1:T(8,128)(2,1)} %copy.95) | copy-start | bytes 3145732
  274.2 3.5 collective-permute-start.9
  283.8 12.2 %collective-permute-start.10 = (bf16[512,3072]{1,0:T(8,128)(2,1)}, bf16[512,3072]{1,0:T(8,128)(2,1)}, u32[]{:S(2)}, u32[]{:S(2)}) collective-permute-start(bf16[512,3072]{1,0:T(8,128)(2,1)} %convolution_convert_fusion), channel_id=1, source_target_pairs={{0,8},{8,0},{16,24},{24,16},{1,9},{9,1},{17,25},{25,17},{2,10},{10... | collective-permute-start | bytes 9437192 | tf_op jit(solution)/shard_map/ppermute | solution.py:630
  292.5 2.7 collective-permute-start.11
  316.6 25.2 %collective-permute-start.12 = (bf16[128,2304]{1,0:T(8,128)(2,1)}, bf16[128,2304]{1,0:T(8,128)(2,1)}, u32[]{:S(2)}, u32[]{:S(2)}) collective-permute-start(bf16[128,2304]{1,0:T(8,128)(2,1)} %reduce-scatter.3.cloned.1.call-done), channel_id=1, source_target_pairs={{0,8},{8,0},{16,24},{24,16},{1,9},{9,1},{17,25},{25,17},{2,10},{10... | collective-permute-start | bytes 1769480 | tf_op jit(solution)/shard_map/ppermute | solution.py:630
  317.1 24.6 %collective-permute-start.13 = (bf16[128,2304]{1,0:T(8,128)(2,1)}, bf16[128,2304]{1,0:T(8,128)(2,1)}, u32[]{:S(2)}, u32[]{:S(2)}) collective-permute-start(bf16[128,2304]{1,0:T(8,128)(2,1)} %reduce-scatter.3.cloned.1.call-done), channel_id=1, source_target_pairs={{0,16},{8,24},{16,0},{24,8},{1,17},{9,25},{17,1},{25,9},{2,18},{10... | collective-permute-start | bytes 1769480 | tf_op jit(solution)/shard_map/ppermute | solution.py:635
  322.5 20.4 %collective-permute-start.16 = (bf16[512,1024]{1,0:T(8,128)(2,1)}, bf16[512,1024]{1,0:T(8,128)(2,1)}, u32[]{:S(2)}, u32[]{:S(2)}) collective-permute-start(bf16[512,1024]{1,0:T(8,128)(2,1)} %slice.207), channel_id=1, source_target_pairs={{0,8},{8,0},{16,24},{24,16},{1,9},{9,1},{17,25},{25,17},{2,10},{10... | collective-permute-start | bytes 3145736 | tf_op jit(solution)/shard_map/ppermute | solution.py:630
  327.9 23.1 %collective-permute-start.15 = (bf16[512,1024]{1,0:T(8,128)(2,1)}, bf16[512,1024]{1,0:T(8,128)(2,1)}, u32[]{:S(2)}, u32[]{:S(2)}) collective-permute-start(bf16[512,1024]{1,0:T(8,128)(2,1)} %slice.208), channel_id=1, source_target_pairs={{0,8},{8,0},{16,24},{24,16},{1,9},{9,1},{17,25},{25,17},{2,10},{10... | collective-permute-start | bytes 3145736 | tf_op jit(solution)/shard_map/ppermute | solution.py:630
  341.7 5.4 collective-permute-start.14
  344.7 24.4 %collective-permute-start.17 = (bf16[512,1024]{1,0:T(8,128)(2,1)S(1)}, bf16[512,1024]{1,0:T(8,128)(2,1)S(1)}, u32[]{:S(2)}, u32[]{:S(2)}) collective-permute-start(bf16[512,1024]{1,0:T(8,128)(2,1)S(1)} %fusion.20), channel_id=1, source_target_pairs={{0,16},{8,24},{16,0},{24,8},{1,17},{9,25},{17,1},{25,9},{2,18},{10... | collective-permute-start | bytes 3145736 | tf_op jit(solution)/shard_map/ppermute | solution.py:635
  (64 other events, 339.5 us)
Sparse Core Ops, SparseCore 0:
  73.4 77.7 all-gather.1
  218.2 95.9 reduce-scatter.2
  317.8 87.6 reduce-scatter.4
